TPU v7x, 32 devices: a whole 2x2x4 slice. The times are simulated.
32 devices in a mesh: seq: 8 (over z, y), ch: 4 (over x, core).
Axes of the slice: x: 2, y: 2, z: 4, core: 2. Of those that a mesh axis runs over, the one named last changes fastest.
Arguments:
- tokens: bfloat16 [16, 512, 1024], P('seq', 'ch'), may hold values from -6 to 6
- grad_out: bfloat16 [16, 512, 1024], P('seq', 'ch'), may hold values from -6 to 6
- lengths: int32 [16], P('seq'), may hold values from 64 to 512, as said below
- init_num: float32 [16, 1024], P('seq'), may hold values from -300 to 300
- init_den: float32 [16, 1024], P('seq'), may hold values from 20 to 400
- w_key: bfloat16 [1024, 1024], replicated, may hold values from -0.1875 to 0.1875
- w_value: bfloat16 [1024, 1024], replicated, may hold values from -0.1875 to 0.1875
- w_recept: bfloat16 [1024, 1024], replicated, may hold values from -0.1875 to 0.1875
- w_output: bfloat16 [1024, 1024], replicated, may hold values from -0.75 to 0.75
- w_expand: bfloat16 [1024, 4096], replicated, may hold values from -0.1875 to 0.1875
- w_contract: bfloat16 [4096, 1024], replicated, may hold values from -0.09375 to 0.09375
- w_gate: bfloat16 [1024, 1024], replicated, may hold values from -0.1875 to 0.1875
- gain_mix: float32 [1024], replicated, may hold values from 0.5 to 1.5
- bias_mix: float32 [1024], replicated, may hold values from -1.2 to 1.2
- gain_ffn: float32 [1024], replicated, may hold values from 0.5 to 1.5
- bias_ffn: float32 [1024], replicated, may hold values from -1.2 to 1.2
- mix_key: float32 [1024], replicated, may hold values from 0 to 1
- mix_value: float32 [1024], replicated, may hold values from 0 to 1
- mix_recept: float32 [1024], replicated, may hold values from 0 to 1
- blend_key: float32 [1024], replicated, may hold values from 0 to 1
- blend_gate: float32 [1024], replicated, may hold values from 0 to 1
- time_decay: float32 [1024], replicated, may hold values from -9 to -2.5
- time_first: float32 [1024], replicated, may hold values from -1 to 2
Outputs:
- mixed_out: bfloat16 [16, 512, 1024], P('seq', 'ch')
- grad_tokens: bfloat16 [16, 512, 1024], P('seq', 'ch')
- final_num: float32 [16, 1024], P('seq', 'ch')
- final_den: float32 [16, 1024], P('seq', 'ch')
- grad_w_key: float32 [1024, 1024], P('seq', 'ch')
- grad_w_value: float32 [1024, 1024], P('seq', 'ch')
- grad_w_recept: float32 [1024, 1024], P('seq', 'ch')
- grad_w_output: float32 [1024, 1024], P('seq', 'ch')
- grad_w_expand: float32 [1024, 4096], P('seq', 'ch')
- grad_w_contract: float32 [4096, 1024], P('seq', 'ch')
- grad_w_gate: float32 [1024, 1024], P('seq', 'ch')
- grad_gain_mix: float32 [1024], P(('seq', 'ch'))
- grad_bias_mix: float32 [1024], P(('seq', 'ch'))
- grad_gain_ffn: float32 [1024], P(('seq', 'ch'))
- grad_bias_ffn: float32 [1024], P(('seq', 'ch'))
- grad_mix_key: float32 [1024], P(('seq', 'ch'))
- grad_mix_value: float32 [1024], P(('seq', 'ch'))
- grad_mix_recept: float32 [1024], P(('seq', 'ch'))
- grad_blend_key: float32 [1024], P(('seq', 'ch'))
- grad_blend_gate: float32 [1024], P(('seq', 'ch'))
- grad_time_decay: float32 [1024], P(('seq', 'ch'))
- grad_time_first: float32 [1024], P(('seq', 'ch'))
Inputs may be any that keep to these rules, and one draw needn't show every extreme that they name: Slot s is filled in its first lengths[s] positions. Among each 2 consecutive slots, one, drawn from the seed, is full.
All inputs are finite; a program needn't handle non-finite values.
Results may differ from a plain program's by a relative error of at most 0.02.
Values may be sent and summed in bfloat16 or wider, within the bound.
A program may use at most 192 MiB of HBM per device.

v0:
```python
import math

import jax
import jax.numpy as jnp
from jax import lax
from jax.sharding import PartitionSpec as P

EPS = 1e-05
HIGH = lax.Precision.HIGHEST
WIDE_TYPE = jnp.float32
NARROW_TYPE = jnp.bfloat16


def from_behind(value, axis, steps):
    count = lax.axis_size(axis)
    initial, last = (max(0, -steps), min(count, count - steps))
    return lax.ppermute(value, axis, [(source, source + steps) for source in range(initial, last)])


def layer_norm(rows_in, gain, bias):
    center = rows_in - jnp.mean(rows_in, axis=-1, keepdims=True)
    factor = lax.rsqrt(jnp.mean(center * center, axis=-1, keepdims=True) + EPS)
    normed = center * factor
    return (normed * gain + bias, normed, factor)


def norm_back(grad_in, normed, factor, gain):
    scaled = grad_in * gain
    centered = scaled - jnp.mean(scaled, axis=-1, keepdims=True)
    return factor * (centered - normed * jnp.mean(scaled * normed, axis=-1, keepdims=True))


def blend_rows(current, earlier, weights):
    return current * weights + earlier * (1.0 - weights)


def project(rows_in, scaling_coefficient):
    flat_rows = rows_in.reshape(-1, rows_in.shape[-1])
    product = jnp.dot(flat_rows, scaling_coefficient, preferred_element_type=WIDE_TYPE)
    return product.reshape(rows_in.shape[:-1] + (scaling_coefficient.shape[1],))


def project_back(grad_in, scaling_coefficient):
    flat_rows = grad_in.reshape(-1, grad_in.shape[-1])
    product = lax.dot_general(
        flat_rows, scaling_coefficient, (((1,), (1,)), ((), ())), preferred_element_type=WIDE_TYPE
    )
    return product.reshape(grad_in.shape[:-1] + (scaling_coefficient.shape[0],))


def outer_sum(rows_in, grad_in):
    return lax.dot_general(
        rows_in.reshape(-1, rows_in.shape[-1]),
        grad_in.reshape(-1, grad_in.shape[-1]),
        (((0,), (0,)), ((), ())),
        preferred_element_type=WIDE_TYPE,
    )


def row_sum(values):
    return jnp.sum(values, axis=(0, 1))


def shift_in(rows_in, edge_rows):
    return jnp.concatenate([edge_rows, rows_in[:, :-1]], axis=1)


def shift_out(rows_in, edge_rows):
    return jnp.concatenate([rows_in[:, 1:], edge_rows], axis=1)


def weighted_value_prepare(
    incoming_key,
    incoming_value,
    incoming_count,
    preceding_count,
    occupied_lines,
    fading_pace,
    first_token_reward,
):
    slot_count, seq_span, chan_width = incoming_key.shape
    block_len = math.gcd(64, seq_span)
    block_count = seq_span // block_len
    shape_four = (slot_count, block_count, block_len, chan_width)
    exposure = (incoming_count[..., None] * fading_pace).reshape(shape_four)
    exposure_prev = (preceding_count[..., None] * fading_pace).reshape(shape_four)
    block_start = exposure_prev[:, :, 0]
    block_stop = exposure[:, :, block_len - 1]
    exponentiated_lookup = jnp.exp(incoming_key).reshape(shape_four)
    reward_share_term = jnp.exp(first_token_reward) * exponentiated_lookup
    scaling_coefficient = occupied_lines.reshape(shape_four[:3])[..., None] * exponentiated_lookup
    payload_quadruple = incoming_value.reshape(shape_four)
    paired = jnp.stack([scaling_coefficient * payload_quadruple, scaling_coefficient])
    growth = jnp.exp(exposure - block_start[:, :, None])
    shrink = jnp.exp(block_start[:, :, None] - exposure_prev)
    row_index = lax.broadcasted_iota(jnp.int32, (block_len, block_len), 0)
    col_index = lax.broadcasted_iota(jnp.int32, (block_len, block_len), 1)
    strict_lower = (col_index < row_index).astype(WIDE_TYPE)
    scaled = growth[None] * paired
    within = jnp.einsum("ab,pnjbc->pnjac", strict_lower, scaled, precision=HIGH)
    totals = jnp.exp(block_start - block_stop)[None] * jnp.sum(scaled, axis=3)
    bounds = jnp.concatenate([block_start, block_stop[:, block_count - 1 :]], axis=1)
    link_row = lax.broadcasted_iota(jnp.int32, (block_count + 1, block_count), 0)
    link_col = lax.broadcasted_iota(jnp.int32, (block_count + 1, block_count), 1)
    spread = bounds[:, :, None, :] - block_stop[:, None, :, :]
    link_mat = jnp.where(
        (link_col < link_row)[None, :, :, None], jnp.exp(-jnp.maximum(spread, 0.0)), 0.0
    )
    reached = jnp.einsum("njkc,pnkc->pnjc", link_mat, totals, precision=HIGH)
    return (
        exposure,
        exposure_prev,
        block_stop,
        bounds,
        reward_share_term,
        scaling_coefficient,
        payload_quadruple,
        shrink,
        within,
        link_mat,
        reached,
        strict_lower,
    )


def wkv_finish(ready_arguments, start_pair):
    bounds = ready_arguments[3]
    reward_share_term = ready_arguments[4]
    payload_quadruple = ready_arguments[6]
    shrink = ready_arguments[7]
    within = ready_arguments[8]
    reached = ready_arguments[10]
    block_count = shrink.shape[1]
    states = jnp.exp(-bounds)[None] * start_pair[:, :, None, :] + reached
    carried_memory = shrink[None] * (states[:, :, :block_count, None, :] + within)
    upper_accumulator = carried_memory[0] + reward_share_term * payload_quadruple
    normalizer_total = carried_memory[1] + reward_share_term
    layer_answer = upper_accumulator / normalizer_total
    flat_shape = (shrink.shape[0], shrink.shape[1] * shrink.shape[2], shrink.shape[3])
    return (
        layer_answer.reshape(flat_shape),
        states[:, :, block_count],
        (carried_memory, normalizer_total, layer_answer),
    )


def wkv_adjoint(grad_flat, ready_arguments, kept_state):
    bounds = ready_arguments[3]
    shrink = ready_arguments[7]
    carried_memory, normalizer_total, layer_answer = kept_state
    upper_total_cotangent = grad_flat.reshape(normalizer_total.shape) / normalizer_total
    adjoint = jnp.stack([upper_total_cotangent, -upper_total_cotangent * layer_answer])
    block_adj = jnp.sum(shrink[None] * adjoint, axis=3)
    block_count = shrink.shape[1]
    own_part = jnp.sum(jnp.exp(-bounds[:, :block_count])[None] * block_adj, axis=2)
    return (adjoint, block_adj, own_part)


def wkv_backward(
    ready_arguments, kept_state, adjoint, block_adj, tail_adj, fading_pace, occupied_lines
):
    (
        exposure,
        exposure_prev,
        block_stop,
        bounds,
        reward_share_term,
        scaling_coefficient,
        payload_quadruple,
        shrink,
        within,
        link_mat,
        reached,
        strict_lower,
    ) = ready_arguments
    carried_memory, normalizer_total, layer_answer = kept_state
    block_count = shrink.shape[1]
    damped = jnp.exp(exposure - block_stop[:, :, None])
    lifted = jnp.exp(block_stop[:, :, None] - exposure_prev)
    carry_in = jnp.einsum("nkjc,pnkc->pnjc", link_mat[:, :block_count], block_adj, precision=HIGH)
    carry_in = carry_in + link_mat[:, block_count][None] * tail_adj[:, :, None, :]
    inside = jnp.einsum("ab,pnjac->pnjbc", strict_lower, lifted[None] * adjoint, precision=HIGH)
    later_cotangent_carry = damped[None] * (inside + carry_in[:, :, :, None, :])
    upper_total_cotangent = adjoint[0]
    lower_sum_cotangent = adjoint[1]
    payload_cotangent = (
        upper_total_cotangent * reward_share_term + later_cotangent_carry[0] * scaling_coefficient
    )
    immediate_route = (
        upper_total_cotangent * payload_quadruple + lower_sum_cotangent
    ) * reward_share_term
    grad_key = (
        immediate_route
        + (later_cotangent_carry[0] * payload_quadruple + later_cotangent_carry[1])
        * scaling_coefficient
    )
    filled_four = occupied_lines.reshape(normalizer_total.shape[:3])[..., None]
    grad_rate = (
        -fading_pace
        * jnp.exp(-fading_pace)
        * jnp.sum(
            filled_four
            * (
                later_cotangent_carry[0] * carried_memory[0]
                + later_cotangent_carry[1] * carried_memory[1]
            ),
            axis=(0, 1, 2),
        )
    )
    grad_first = jnp.sum(immediate_route, axis=(0, 1, 2))
    flat_shape = (
        normalizer_total.shape[0],
        normalizer_total.shape[1] * normalizer_total.shape[2],
        normalizer_total.shape[3],
    )
    return (
        grad_key.reshape(flat_shape),
        payload_cotangent.reshape(flat_shape),
        grad_first,
        grad_rate,
    )


def body(
    tokens,
    grad_out,
    lengths,
    init_num,
    init_den,
    w_key,
    w_value,
    w_recept,
    w_output,
    w_expand,
    w_contract,
    w_gate,
    gain_mix,
    bias_mix,
    gain_ffn,
    bias_ffn,
    mix_key,
    mix_value,
    mix_recept,
    blend_key,
    blend_gate,
    time_decay,
    time_first,
):
    slot_count, local_len, model_width = tokens.shape
    group_size = lax.axis_size("ch")
    ch_rank = lax.axis_index("ch")
    chan_width = model_width // group_size
    seq_span = local_len * group_size
    length_col = lengths[:, None]
    offset = ch_rank * local_len
    position = offset + lax.broadcasted_iota(jnp.int32, (slot_count, local_len), 1)
    occupied_lines = (position < length_col).astype(WIDE_TYPE)
    fading_pace = jnp.exp(time_decay)
    start_pair = jnp.stack([init_num, init_den])
    rows_in = tokens.astype(WIDE_TYPE)
    normed_mix, unit_mix, factor_mix = layer_norm(rows_in, gain_mix, bias_mix)
    edge_mix = from_behind(normed_mix[:, local_len - 1 :], "ch", 1)
    before_mix = shift_in(normed_mix, edge_mix)
    input_key = blend_rows(normed_mix, before_mix, mix_key).astype(NARROW_TYPE)
    input_value = blend_rows(normed_mix, before_mix, mix_value).astype(NARROW_TYPE)
    input_recept = blend_rows(normed_mix, before_mix, mix_recept).astype(NARROW_TYPE)
    lookup_array = project(input_key, w_key).astype(NARROW_TYPE)
    payload_array = project(input_value, w_value).astype(NARROW_TYPE)
    recept = project(input_recept, w_recept)
    key_cols, value_cols = (
        lax.all_to_all(lookup_array, "ch", split_axis=2, concat_axis=1, tiled=True),
        lax.all_to_all(payload_array, "ch", split_axis=2, concat_axis=1, tiled=True),
    )
    step_index = lax.broadcasted_iota(jnp.int32, (slot_count, seq_span), 1)
    incoming_count = jnp.minimum(step_index + 1, length_col).astype(WIDE_TYPE)
    preceding_count = jnp.minimum(step_index, length_col).astype(WIDE_TYPE)
    filled_cols = (step_index < length_col).astype(WIDE_TYPE)
    rate_part = lax.dynamic_slice_in_dim(fading_pace, ch_rank * chan_width, chan_width)
    first_part = lax.dynamic_slice_in_dim(time_first, ch_rank * chan_width, chan_width)
    init_part = lax.dynamic_slice_in_dim(start_pair, ch_rank * chan_width, chan_width, 2)
    ready_arguments = weighted_value_prepare(
        key_cols.astype(WIDE_TYPE),
        value_cols.astype(WIDE_TYPE),
        incoming_count,
        preceding_count,
        filled_cols,
        rate_part,
        first_part,
    )
    wkv_cols, final_pair, kept_state = wkv_finish(ready_arguments, init_part)
    wkv_rows = lax.all_to_all(
        wkv_cols.astype(NARROW_TYPE), "ch", split_axis=1, concat_axis=2, tiled=True
    )
    gate_mix = jax.nn.sigmoid(recept)
    wkv_float = wkv_rows.astype(WIDE_TYPE)
    gated = (gate_mix * wkv_float).astype(NARROW_TYPE)
    middle = rows_in + project(gated, w_output)
    normed_ffn, unit_ffn, factor_ffn = layer_norm(middle, gain_ffn, bias_ffn)
    edge_ffn = from_behind(normed_ffn[:, local_len - 1 :], "ch", 1)
    before_ffn = shift_in(normed_ffn, edge_ffn)
    input_expand = blend_rows(normed_ffn, before_ffn, blend_key).astype(NARROW_TYPE)
    input_gate = blend_rows(normed_ffn, before_ffn, blend_gate).astype(NARROW_TYPE)
    expanded = project(input_expand, w_expand)
    positive = jnp.maximum(expanded, 0.0)
    hidden = (positive * positive).astype(NARROW_TYPE)
    contracted = project(hidden, w_contract)
    gate_ffn = jax.nn.sigmoid(project(input_gate, w_gate))
    mask_three = occupied_lines[..., None]
    mixed_out = (mask_three * (middle + gate_ffn * contracted)).astype(NARROW_TYPE)
    grad_res = mask_three * grad_out.astype(WIDE_TYPE)
    grad_contracted = (grad_res * gate_ffn).astype(NARROW_TYPE)
    grad_logit = (grad_res * contracted * gate_ffn * (1.0 - gate_ffn)).astype(NARROW_TYPE)
    grad_expanded = (project_back(grad_contracted, w_contract) * 2.0 * positive).astype(NARROW_TYPE)
    grad_w_contract = outer_sum(hidden, grad_contracted)
    grad_w_expand = outer_sum(input_expand, grad_expanded)
    grad_w_gate = outer_sum(input_gate, grad_logit)
    grad_in_expand = project_back(grad_expanded, w_expand)
    grad_in_gate = project_back(grad_logit, w_gate)
    gap_ffn = normed_ffn - before_ffn
    grad_blend_key = row_sum(grad_in_expand * gap_ffn)
    grad_blend_gate = row_sum(grad_in_gate * gap_ffn)
    grad_before_ffn = grad_in_expand * (1.0 - blend_key) + grad_in_gate * (1.0 - blend_gate)
    from_next_ffn = from_behind(grad_before_ffn[:, :1], "ch", -1)
    grad_normed_ffn = (
        grad_in_expand * blend_key
        + grad_in_gate * blend_gate
        + shift_out(grad_before_ffn, from_next_ffn)
    )
    grad_gain_ffn = row_sum(grad_normed_ffn * unit_ffn)
    grad_bias_ffn = row_sum(grad_normed_ffn)
    grad_middle = grad_res + norm_back(grad_normed_ffn, unit_ffn, factor_ffn, gain_ffn)
    grad_branch = grad_middle.astype(NARROW_TYPE)
    grad_w_output = outer_sum(gated, grad_branch)
    grad_gated = project_back(grad_branch, w_output)
    grad_wkv = (grad_gated * gate_mix).astype(NARROW_TYPE)
    grad_recept = (grad_gated * wkv_float * gate_mix * (1.0 - gate_mix)).astype(NARROW_TYPE)
    grad_cols = lax.all_to_all(grad_wkv, "ch", split_axis=2, concat_axis=1, tiled=True)
    adjoint, block_adj, own_part = wkv_adjoint(
        grad_cols.astype(WIDE_TYPE), ready_arguments, kept_state
    )
    grad_key_cols, grad_value_cols, first_grad_part, rate_grad_part = wkv_backward(
        ready_arguments,
        kept_state,
        adjoint,
        block_adj,
        jnp.zeros_like(own_part),
        rate_part,
        filled_cols,
    )
    grad_key_rows, grad_value_rows = (
        lax.all_to_all(
            grad_key_cols.astype(NARROW_TYPE), "ch", split_axis=1, concat_axis=2, tiled=True
        ),
        lax.all_to_all(
            grad_value_cols.astype(NARROW_TYPE), "ch", split_axis=1, concat_axis=2, tiled=True
        ),
    )
    grad_time_decay = lax.dynamic_update_slice_in_dim(
        jnp.zeros((model_width,), WIDE_TYPE), rate_grad_part, ch_rank * chan_width, 0
    )
    grad_time_first = lax.dynamic_update_slice_in_dim(
        jnp.zeros((model_width,), WIDE_TYPE), first_grad_part, ch_rank * chan_width, 0
    )
    grad_w_key = outer_sum(input_key, grad_key_rows)
    grad_w_value = outer_sum(input_value, grad_value_rows)
    grad_w_recept = outer_sum(input_recept, grad_recept)
    grad_in_key = project_back(grad_key_rows, w_key)
    grad_in_value = project_back(grad_value_rows, w_value)
    grad_in_recept = project_back(grad_recept, w_recept)
    gap_mix = normed_mix - before_mix
    grad_mix_key = row_sum(grad_in_key * gap_mix)
    grad_mix_value = row_sum(grad_in_value * gap_mix)
    grad_mix_recept = row_sum(grad_in_recept * gap_mix)
    grad_before_mix = (
        grad_in_key * (1.0 - mix_key)
        + grad_in_value * (1.0 - mix_value)
        + grad_in_recept * (1.0 - mix_recept)
    )
    from_next_mix = from_behind(grad_before_mix[:, :1], "ch", -1)
    grad_normed_mix = (
        grad_in_key * mix_key
        + grad_in_value * mix_value
        + grad_in_recept * mix_recept
        + shift_out(grad_before_mix, from_next_mix)
    )
    grad_gain_mix = row_sum(grad_normed_mix * unit_mix)
    grad_bias_mix = row_sum(grad_normed_mix)
    grad_tokens = (grad_middle + norm_back(grad_normed_mix, unit_mix, factor_mix, gain_mix)).astype(
        NARROW_TYPE
    )
    row_sums = (
        lax.psum_scatter(
            grad_w_key.astype(jnp.bfloat16), "seq", scatter_dimension=0, tiled=True
        ).astype(jnp.float32),
        lax.psum_scatter(
            grad_w_value.astype(jnp.bfloat16), "seq", scatter_dimension=0, tiled=True
        ).astype(jnp.float32),
        lax.psum_scatter(
            grad_w_recept.astype(jnp.bfloat16), "seq", scatter_dimension=0, tiled=True
        ).astype(jnp.float32),
        lax.psum_scatter(
            grad_w_output.astype(jnp.bfloat16), "seq", scatter_dimension=0, tiled=True
        ).astype(jnp.float32),
        lax.psum_scatter(
            grad_w_expand.astype(jnp.bfloat16), "seq", scatter_dimension=0, tiled=True
        ).astype(jnp.float32),
        lax.psum_scatter(
            grad_w_contract.astype(jnp.bfloat16), "seq", scatter_dimension=0, tiled=True
        ).astype(jnp.float32),
        lax.psum_scatter(
            grad_w_gate.astype(jnp.bfloat16), "seq", scatter_dimension=0, tiled=True
        ).astype(jnp.float32),
        lax.psum_scatter(
            grad_gain_mix.astype(jnp.bfloat16), "seq", scatter_dimension=0, tiled=True
        ).astype(jnp.float32),
        lax.psum_scatter(
            grad_bias_mix.astype(jnp.bfloat16), "seq", scatter_dimension=0, tiled=True
        ).astype(jnp.float32),
        lax.psum_scatter(
            grad_gain_ffn.astype(jnp.bfloat16), "seq", scatter_dimension=0, tiled=True
        ).astype(jnp.float32),
        lax.psum_scatter(
            grad_bias_ffn.astype(jnp.bfloat16), "seq", scatter_dimension=0, tiled=True
        ).astype(jnp.float32),
        lax.psum_scatter(
            grad_mix_key.astype(jnp.bfloat16), "seq", scatter_dimension=0, tiled=True
        ).astype(jnp.float32),
        lax.psum_scatter(
            grad_mix_value.astype(jnp.bfloat16), "seq", scatter_dimension=0, tiled=True
        ).astype(jnp.float32),
        lax.psum_scatter(
            grad_mix_recept.astype(jnp.bfloat16), "seq", scatter_dimension=0, tiled=True
        ).astype(jnp.float32),
        lax.psum_scatter(
            grad_blend_key.astype(jnp.bfloat16), "seq", scatter_dimension=0, tiled=True
        ).astype(jnp.float32),
        lax.psum_scatter(
            grad_blend_gate.astype(jnp.bfloat16), "seq", scatter_dimension=0, tiled=True
        ).astype(jnp.float32),
        lax.psum_scatter(
            grad_time_decay.astype(jnp.bfloat16), "seq", scatter_dimension=0, tiled=True
        ).astype(jnp.float32),
        lax.psum_scatter(
            grad_time_first.astype(jnp.bfloat16), "seq", scatter_dimension=0, tiled=True
        ).astype(jnp.float32),
    )
    all_sums = (
        lax.psum_scatter(
            row_sums[0].astype(jnp.bfloat16), "ch", scatter_dimension=1, tiled=True
        ).astype(jnp.float32),
        lax.psum_scatter(
            row_sums[1].astype(jnp.bfloat16), "ch", scatter_dimension=1, tiled=True
        ).astype(jnp.float32),
        lax.psum_scatter(
            row_sums[2].astype(jnp.bfloat16), "ch", scatter_dimension=1, tiled=True
        ).astype(jnp.float32),
        lax.psum_scatter(
            row_sums[3].astype(jnp.bfloat16), "ch", scatter_dimension=1, tiled=True
        ).astype(jnp.float32),
        lax.psum_scatter(
            row_sums[4].astype(jnp.bfloat16), "ch", scatter_dimension=1, tiled=True
        ).astype(jnp.float32),
        lax.psum_scatter(
            row_sums[5].astype(jnp.bfloat16), "ch", scatter_dimension=1, tiled=True
        ).astype(jnp.float32),
        lax.psum_scatter(
            row_sums[6].astype(jnp.bfloat16), "ch", scatter_dimension=1, tiled=True
        ).astype(jnp.float32),
        lax.psum_scatter(
            row_sums[7].astype(jnp.bfloat16), "ch", scatter_dimension=0, tiled=True
        ).astype(jnp.float32),
        lax.psum_scatter(
            row_sums[8].astype(jnp.bfloat16), "ch", scatter_dimension=0, tiled=True
        ).astype(jnp.float32),
        lax.psum_scatter(
            row_sums[9].astype(jnp.bfloat16), "ch", scatter_dimension=0, tiled=True
        ).astype(jnp.float32),
        lax.psum_scatter(
            row_sums[10].astype(jnp.bfloat16), "ch", scatter_dimension=0, tiled=True
        ).astype(jnp.float32),
        lax.psum_scatter(
            row_sums[11].astype(jnp.bfloat16), "ch", scatter_dimension=0, tiled=True
        ).astype(jnp.float32),
        lax.psum_scatter(
            row_sums[12].astype(jnp.bfloat16), "ch", scatter_dimension=0, tiled=True
        ).astype(jnp.float32),
        lax.psum_scatter(
            row_sums[13].astype(jnp.bfloat16), "ch", scatter_dimension=0, tiled=True
        ).astype(jnp.float32),
        lax.psum_scatter(
            row_sums[14].astype(jnp.bfloat16), "ch", scatter_dimension=0, tiled=True
        ).astype(jnp.float32),
        lax.psum_scatter(
            row_sums[15].astype(jnp.bfloat16), "ch", scatter_dimension=0, tiled=True
        ).astype(jnp.float32),
        lax.psum_scatter(
            row_sums[16].astype(jnp.bfloat16), "ch", scatter_dimension=0, tiled=True
        ).astype(jnp.float32),
        lax.psum_scatter(
            row_sums[17].astype(jnp.bfloat16), "ch", scatter_dimension=0, tiled=True
        ).astype(jnp.float32),
    )
    return (
        mixed_out,
        grad_tokens,
        final_pair[0],
        final_pair[1],
        all_sums[0],
        all_sums[1],
        all_sums[2],
        all_sums[3],
        all_sums[4],
        all_sums[5],
        all_sums[6],
        all_sums[7],
        all_sums[8],
        all_sums[9],
        all_sums[10],
        all_sums[11],
        all_sums[12],
        all_sums[13],
        all_sums[14],
        all_sums[15],
        all_sums[16],
        all_sums[17],
    )


def solution(mesh):
    placed = (
        P("seq", "ch", None),
        P("seq", "ch", None),
        P("seq"),
        P("seq", None),
        P("seq", None),
        P(),
        P(),
        P(),
        P(),
        P(),
        P(),
        P(),
        P(),
        P(),
        P(),
        P(),
        P(),
        P(),
        P(),
        P(),
        P(),
        P(),
        P(),
    )
    return jax.shard_map(
        body,
        mesh=mesh,
        in_specs=placed,
        out_specs=(
            P("seq", "ch", None),
            P("seq", "ch", None),
            P("seq", "ch"),
            P("seq", "ch"),
            P("seq", "ch"),
            P("seq", "ch"),
            P("seq", "ch"),
            P("seq", "ch"),
            P("seq", "ch"),
            P("seq", "ch"),
            P("seq", "ch"),
            P(("seq", "ch")),
            P(("seq", "ch")),
            P(("seq", "ch")),
            P(("seq", "ch")),
            P(("seq", "ch")),
            P(("seq", "ch")),
            P(("seq", "ch")),
            P(("seq", "ch")),
            P(("seq", "ch")),
            P(("seq", "ch")),
            P(("seq", "ch")),
        ),
        check_vma=False,
    )
```

profile of v0, /device:TPU:0, one launch (start us, length us, event | category | flops | bytes accessed | tf_op | source)
XLA Modules:
  0.0 939.8 jit_solution(16529665846056420181)
XLA Ops:
  11.3 2.4 collective-permute-start
  14.5 2.7 subtract_exponential_fusion.3
  21.7 3.9 all-to-all-start.1
  26.2 3.1 fusion.73
  31.3 3.1 all-to-all-done.1
  34.5 4.1 all-to-all-start
  47.5 2.2 convert_exponential_fusion
  49.7 2.5 copy.210
  56.0 9.2 fusion.91
  66.4 3.6 bitcast_multiply_fusion.1
  74.1 3.7 all-to-all-start.2
  77.8 8.7 all-to-all-done.2
  95.7 5.9 fusion.8
  101.7 2.3 fusion.2
  109.5 7.1 fusion.17
  116.7 6.7 fusion.4
  131.7 2.9 multiply_convert_fusion.1
  136.8 3.4 exponential_select_fusion
  141.3 4.5 all-to-all-start.3
  147.9 7.0 all-to-all-done.3
  154.9 2.3 fusion.136
  157.2 2.6 copy.227
  164.6 6.2 fusion.88
  172.0 3.7 bitcast_multiply_fusion
  180.7 11.2 %all_to_all.66 = bf16[2,512,256]{2,0,1:T(2,128)(2,1)S(1)} all-to-all(bf16[2,512,256]{2,0,1:T(2,128)(2,1)S(1)} %copy.231), channel_id=1, replica_groups=mesh['seq'=8,'ch'=4] {'ch'}, dimensions={1} | all-to-all | bytes 1048576 | tf_op jit(solution)/shard_map/all_to_all | solution.py:351
  193.3 2.2 convolution_convert_fusion.1
  196.1 11.2 %all_to_all.67 = bf16[2,512,256]{2,0,1:T(2,128)(2,1)S(1)} all-to-all(bf16[2,512,256]{2,0,1:T(2,128)(2,1)S(1)} %copy.233), channel_id=1, replica_groups=mesh['seq'=8,'ch'=4] {'ch'}, dimensions={1} | all-to-all | bytes 1048576 | tf_op jit(solution)/shard_map/all_to_all | solution.py:354
  211.0 7.9 bitcast_convert_fusion
  220.0 7.3 bitcast_convert_fusion.1
  228.1 22.2 %reduce-scatter.27.cloned.1.call-done = bf16[128,1024]{1,0:T(8,128)(2,1)} async-done(((bf16[1024,1024]{1,0:T(8,128)(2,1)}), bf16[128,1024]{1,0:T(8,128)(2,1)}) %reduce-scatter.27.cloned.1.call-update) | async-done | bytes 262160 | tf_op jit(solution)/shard_map/reduce_scatter | solution.py:401
  250.3 70.3 %reduce-scatter.23.cloned.1.call-done = bf16[128,1024]{1,0:T(8,128)(2,1)} async-done(((bf16[1024,1024]{1,0:T(8,128)(2,1)}), bf16[128,1024]{1,0:T(8,128)(2,1)}) %reduce-scatter.23.cloned.1.call-update) | async-done | bytes 262160 | tf_op jit(solution)/shard_map/reduce_scatter | solution.py:398
  320.7 70.0 %reduce-scatter.15.cloned.1.call-done = bf16[128,1024]{1,0:T(8,128)(2,1)} async-done(((bf16[1024,1024]{1,0:T(8,128)(2,1)}), bf16[128,1024]{1,0:T(8,128)(2,1)}) %reduce-scatter.15.cloned.1.call-update) | async-done | bytes 262160 | tf_op jit(solution)/shard_map/reduce_scatter | solution.py:392
  390.8 70.1 %reduce-scatter.19.cloned.1.call-done = bf16[128,1024]{1,0:T(8,128)(2,1)} async-done(((bf16[1024,1024]{1,0:T(8,128)(2,1)}), bf16[128,1024]{1,0:T(8,128)(2,1)}) %reduce-scatter.19.cloned.1.call-update) | async-done | bytes 262160 | tf_op jit(solution)/shard_map/reduce_scatter | solution.py:395
  463.5 2.6 copy.240
  467.4 145.0 %reduce-scatter.35.cloned.1.call-done = bf16[512,1024]{1,0:T(8,128)(2,1)} async-done(((bf16[4096,1024]{1,0:T(8,128)(2,1)}), bf16[512,1024]{1,0:T(8,128)(2,1)}) %reduce-scatter.35.cloned.1.call-update) | async-done | bytes 1048592 | tf_op jit(solution)/shard_map/reduce_scatter | solution.py:407
  612.5 5.8 slice_reduce_fusion
  622.9 2.5 fusion.30
  632.4 2.4 slice.106
  634.8 129.8 %reduce-scatter.31.cloned.1.call-done = bf16[128,4096]{1,0:T(8,128)(2,1)} async-done(((bf16[1024,4096]{1,0:T(8,128)(2,1)}), bf16[128,4096]{1,0:T(8,128)(2,1)}) %reduce-scatter.31.cloned.1.call-update) | async-done | bytes 1048592 | tf_op jit(solution)/shard_map/reduce_scatter | solution.py:404
  764.6 4.0 fusion.98
  768.7 35.2 %all-reduce.22 = (bf16[1024]{0:T(1024)(128)(2,1)S(1)}, bf16[1024]{0:T(1024)(128)(2,1)S(1)}, bf16[1024]{0:T(1024)(128)(2,1)S(1)}, bf16[1024]{0:T(1024)(128)(2,1)S...) all-reduce(bf16[1024]{0:T(1024)(128)(2,1)S(1)} %get-tuple-element.2, ...), channel_id=16, replica_groups=mesh['seq'=8,'ch'=4] {'seq'}, use_global_device_ids=true, to_apply=%region_25.26.clone | all-reduce | flops 11264 | bytes 45056
  804.7 5.7 all-reduce.23
  816.8 2.9 fusion.97
  822.8 8.4 reduce-scatter.25.cloned.1.call-done
  832.7 21.1 %reduce-scatter.17.cloned.1.call-done = bf16[128,256]{1,0:T(8,128)(2,1)} async-done(((bf16[128,1024]{1,0:T(8,128)(2,1)}), bf16[128,256]{1,0:T(8,128)(2,1)}) %reduce-scatter.17.cloned.1.call-update) | async-done | bytes 65552 | tf_op jit(solution)/shard_map/reduce_scatter | solution.py:448
  855.3 20.9 %reduce-scatter.21.cloned.1.call-done = bf16[128,256]{1,0:T(8,128)(2,1)} async-done(((bf16[128,1024]{1,0:T(8,128)(2,1)}), bf16[128,256]{1,0:T(8,128)(2,1)}) %reduce-scatter.21.cloned.1.call-update) | async-done | bytes 65552 | tf_op jit(solution)/shard_map/reduce_scatter | solution.py:451
  877.7 26.1 %reduce-scatter.37.cloned.1.call-done = bf16[512,256]{1,0:T(8,128)(2,1)} async-done(((bf16[512,1024]{1,0:T(8,128)(2,1)}), bf16[512,256]{1,0:T(8,128)(2,1)}) %reduce-scatter.37.cloned.1.call-update) | async-done | bytes 262160 | tf_op jit(solution)/shard_map/reduce_scatter | solution.py:463
  905.6 25.5 %reduce-scatter.33.cloned.1.call-done = bf16[128,1024]{1,0:T(8,128)(2,1)} async-done(((bf16[128,4096]{1,0:T(8,128)(2,1)}), bf16[128,1024]{1,0:T(8,128)(2,1)}) %reduce-scatter.33.cloned.1.call-update) | async-done | bytes 262160 | tf_op jit(solution)/shard_map/reduce_scatter | solution.py:460
  (357 shorter events, 108.6 us)
Async XLA Ops:
  7.2 96.8 %copy-start = (bf16[1024,1024]{1,0:T(8,128)(2,1)S(1)}, bf16[1024,1024]{1,0:T(8,128)(2,1)}, u32[]{:S(2)}) copy-start(bf16[1024,1024]{1,0:T(8,128)(2,1)} %param.34) | copy-start | bytes 6291460
  7.2 6.5 copy-start.88
  7.2 6.5 copy-start.84
  9.9 7.3 copy-start.78
  11.3 5.9 copy-start.23
  11.3 5.9 collective-permute-start
  19.9 5.7 copy-start.87
  19.9 6.3 copy-start.57
  21.7 12.7 %all-to-all-start.1 = ((bf16[2,128,1024]{1,0,2:T(2,128)(2,1)}), bf16[2,128,1024]{1,0,2:T(2,128)(2,1)S(1)}, u32[]{:S(2)}, u32[]{:S(2)}) async-start(bf16[2,128,1024]{1,0,2:T(2,128)(2,1)} %copy.211), calls=%async_computation.1 | async-start | bytes 1048576 | tf_op jit(solution)/shard_map/all_to_all | solution.py:272
  29.3 12.5 %copy-start.82 = (f32[2,2,256]{2,1,0:T(2,128)S(1)}, f32[2,2,256]{2,1,0:T(2,128)}, u32[]{:S(2)}) copy-start(f32[2,2,256]{2,1,0:T(2,128)} %fusion.126) | copy-start | bytes 12292
  34.5 13.0 %all-to-all-start = ((bf16[2,128,1024]{1,0,2:T(2,128)(2,1)}), bf16[2,128,1024]{1,0,2:T(2,128)(2,1)}, u32[]{:S(2)}, u32[]{:S(2)}) async-start(bf16[2,128,1024]{1,0,2:T(2,128)(2,1)} %copy.208), calls=%async_computation | async-start | bytes 1048576 | tf_op jit(solution)/shard_map/all_to_all | solution.py:271
  45.5 25.9 %copy-start.5 = (f32[2,4,128,256]{3,2,1,0:T(8,128)}, f32[2,4,128,256]{3,2,1,0:T(8,128)S(1)}, u32[]{:S(2)}) copy-start(f32[2,4,128,256]{3,2,1,0:T(8,128)S(1)} %copy.213) | copy-start | bytes 3145732
  74.1 12.5 %all-to-all-start.2 = ((bf16[2,512,256]{2,0,1:T(2,128)(2,1)}), bf16[2,512,256]{2,0,1:T(2,128)(2,1)S(1)}, u32[]{:S(2)}, u32[]{:S(2)}) async-start(bf16[2,512,256]{2,0,1:T(2,128)(2,1)} %copy.222), calls=%async_computation.2 | async-start | bytes 1048576 | tf_op jit(solution)/shard_map/all_to_all | solution.py:291
  77.7 149.6 %reduce-scatter.39.cloned.1.call-start = ((), (), s32[]{:S(2)}) async-start(), calls=%async_computation.32 | async-start | bytes 2359296 | tf_op jit(solution)/shard_map/reduce_scatter | solution.py:410
  91.9 2.4 collective-permute-start.1
  94.2 7.4 slice-start
  95.7 5.9 slice-start.1
  109.1 141.2 %reduce-scatter.27.cloned.1.call-start = ((), (), s32[]{:S(2)}) async-start(), calls=%async_computation.26 | async-start | bytes 2359296 | tf_op jit(solution)/shard_map/reduce_scatter | solution.py:401
  116.6 6.8 copy-start.33
  116.6 6.8 copy-start.14
  116.6 6.8 copy-start.54
  124.4 3.4 collective-permute-start.2
  131.6 189.1 %reduce-scatter.23.cloned.1.call-start = ((), (), s32[]{:S(2)}) async-start(), calls=%async_computation.24 | async-start | bytes 2359296 | tf_op jit(solution)/shard_map/reduce_scatter | solution.py:398
  141.3 13.6 %all-to-all-start.3 = ((bf16[2,128,1024]{1,0,2:T(2,128)(2,1)}), bf16[2,128,1024]{1,0,2:T(2,128)(2,1)}, u32[]{:S(2)}, u32[]{:S(2)}) async-start(bf16[2,128,1024]{1,0,2:T(2,128)(2,1)} %copy.225), calls=%async_computation.3 | async-start | bytes 1048576 | tf_op jit(solution)/shard_map/all_to_all | solution.py:337
  145.8 244.9 %reduce-scatter.15.cloned.1.call-start = ((), (), s32[]{:S(2)}) async-start(), calls=%async_computation.20 | async-start | bytes 2359296 | tf_op jit(solution)/shard_map/reduce_scatter | solution.py:392
  147.8 11.9 %copy-start.3 = (f32[2,2,8,64,256]{4,3,2,1,0:T(8,128)S(1)}, f32[2,2,8,64,256]{4,3,2,1,0:T(8,128)}, u32[]{:S(2)}) copy-start(f32[2,2,8,64,256]{4,3,2,1,0:T(8,128)} %copy-done.2) | copy-start | bytes 6291460
  147.9 11.9 %copy-start.6 = (f32[2,4,128,256]{3,2,1,0:T(8,128)S(1)}, f32[2,4,128,256]{3,2,1,0:T(8,128)}, u32[]{:S(2)}) copy-start(f32[2,4,128,256]{3,2,1,0:T(8,128)} %copy-done.5) | copy-start | bytes 3145732
  180.2 13.1 %copy-start.58 = (bf16[2,128,1024]{2,1,0:T(8,128)(2,1)S(1)}, bf16[2,128,1024]{2,1,0:T(8,128)(2,1)}, u32[]{:S(2)}) copy-start(bf16[2,128,1024]{2,1,0:T(8,128)(2,1)} %get-tuple-element.81) | copy-start | bytes 1572868
  195.5 265.5 %reduce-scatter.19.cloned.1.call-start = ((), (), s32[]{:S(2)}) async-start(), calls=%async_computation.22 | async-start | bytes 2359296 | tf_op jit(solution)/shard_map/reduce_scatter | solution.py:395
  195.5 13.1 %copy-start.56 = (bf16[2,128,1024]{2,1,0:T(8,128)(2,1)S(1)}, bf16[2,128,1024]{2,1,0:T(8,128)(2,1)}, u32[]{:S(2)}) copy-start(bf16[2,128,1024]{2,1,0:T(8,128)(2,1)} %copy-done.55) | copy-start | bytes 1572868
  210.7 401.7 %reduce-scatter.35.cloned.1.call-start = ((), (), s32[]{:S(2)}) async-start(), calls=%async_computation.30 | async-start | bytes 9437184 | tf_op jit(solution)/shard_map/reduce_scatter | solution.py:407
  219.0 545.6 %reduce-scatter.31.cloned.1.call-start = ((), (), s32[]{:S(2)}) async-start(), calls=%async_computation.28 | async-start | bytes 9437184 | tf_op jit(solution)/shard_map/reduce_scatter | solution.py:404
  227.3 233.7 %copy-start.90 = (u32[32]{0:T(128)S(1)}, u32[32]{0:T(128)}, u32[]{:S(2)}) copy-start(u32[32]{0:T(128)} %constant.48) | copy-start | bytes 388
  227.3 234.3 %copy-start.89 = (u32[32]{0:T(128)S(1)}, u32[32]{0:T(128)}, u32[]{:S(2)}) copy-start(u32[32]{0:T(128)} %constant.52) | copy-start | bytes 388
  227.3 238.8 %copy-start.20 = (f32[1,2,8,64,256]{4,3,2,1,0:T(8,128)S(1)}, f32[1,2,8,64,256]{4,3,2,1,0:T(8,128)}, u32[]{:S(2)}) copy-start(f32[1,2,8,64,256]{4,3,2,1,0:T(8,128)} %copy-done.18) | copy-start | bytes 3145732
  227.3 592.5 %reduce-scatter.41.cloned.1.call-start = ((), (), s32[]{:S(2)}) async-start(), calls=%async_computation.33 | async-start | bytes 327680 | tf_op jit(solution)/shard_map/reduce_scatter | solution.py:466
  228.1 593.2 %reduce-scatter.29.cloned.1.call-start = ((), (), s32[]{:S(2)}) async-start(), calls=%async_computation.27 | async-start | bytes 327680 | tf_op jit(solution)/shard_map/reduce_scatter | solution.py:457
  250.3 580.9 %reduce-scatter.25.cloned.1.call-start = ((), (), s32[]{:S(2)}) async-start(), calls=%async_computation.25 | async-start | bytes 327680 | tf_op jit(solution)/shard_map/reduce_scatter | solution.py:454
  320.7 533.1 %reduce-scatter.17.cloned.1.call-start = ((), (), s32[]{:S(2)}) async-start(), calls=%async_computation.21 | async-start | bytes 327680 | tf_op jit(solution)/shard_map/reduce_scatter | solution.py:448
  390.8 485.4 %reduce-scatter.21.cloned.1.call-start = ((), (), s32[]{:S(2)}) async-start(), calls=%async_computation.23 | async-start | bytes 327680 | tf_op jit(solution)/shard_map/reduce_scatter | solution.py:451
  461.0 442.9 %reduce-scatter.37.cloned.1.call-start = ((), (), s32[]{:S(2)}) async-start(), calls=%async_computation.31 | async-start | bytes 1310720 | tf_op jit(solution)/shard_map/reduce_scatter | solution.py:463
  612.5 318.7 %reduce-scatter.33.cloned.1.call-start = ((), (), s32[]{:S(2)}) async-start(), calls=%async_computation.29 | async-start | bytes 1310720 | tf_op jit(solution)/shard_map/reduce_scatter | solution.py:460
  629.0 135.6 %copy-start.11 = (bf16[2,128,1024]{2,1,0:T(8,128)(2,1)S(1)}, bf16[2,128,1024]{2,1,0:T(8,128)(2,1)}, u32[]{:S(2)}) copy-start(bf16[2,128,1024]{2,1,0:T(8,128)(2,1)} %param.23) | copy-start | bytes 1572868
  629.0 135.6 %copy-start.24 = (f32[2,128,1024]{2,1,0:T(8,128)S(1)}, f32[2,128,1024]{2,1,0:T(8,128)}, u32[]{:S(2)}) copy-start(f32[2,128,1024]{2,1,0:T(8,128)} %copy-done.23) | copy-start | bytes 3145732
  629.0 135.6 %copy-start.77 = (f32[2,1,1024]{2,1,0:T(1,128)S(1)}, f32[2,1,1024]{2,1,0:T(1,128)}, u32[]{:S(2)}) copy-start(f32[2,1,1024]{2,1,0:T(1,128)} %copy-done.76) | copy-start | bytes 24580
  629.0 135.6 %copy-start.79 = (f32[2,128]{1,0:T(2,128)S(1)}, f32[2,128]{1,0:T(2,128)}, u32[]{:S(2)}) copy-start(f32[2,128]{1,0:T(2,128)} %copy-done.78) | copy-start | bytes 3076
  630.0 134.6 %collective-permute-start.3 = (f32[2,1,1024]{2,1,0:T(1,128)S(1)}, f32[2,1,1024]{2,1,0:T(1,128)S(1)}, u32[]{:S(2)}, u32[]{:S(2)}) collective-permute-start(f32[2,1,1024]{2,1,0:T(1,128)S(1)} %slice.107), channel_id=1, source_target_pairs={{1,0},{2,1},{3,2},{5,4},{6,5},{7,6},{9,8},{10,9},{11,10},{13,12},{... | collective-permute-start | bytes 24584 | tf_op jit(solution)/shard_map/ppermute | solution.py:17
  816.8 116.1 %copy-start.1 = (bf16[1024,1024]{1,0:T(8,128)(2,1)S(1)}, bf16[1024,1024]{1,0:T(8,128)(2,1)}, u32[]{:S(2)}) copy-start(bf16[1024,1024]{1,0:T(8,128)(2,1)} %param.34) | copy-start | bytes 6291460
  (67 other events, 139.7 us)
Sparse Core Ops, SparseCore 0:
  109.2 70.7 reduce-scatter.38
  183.5 66.6 reduce-scatter.26
  253.8 66.8 reduce-scatter.22
  324.1 66.6 reduce-scatter.14
  394.1 66.7 reduce-scatter.18
  464.4 147.9 reduce-scatter.34
  616.5 148.0 reduce-scatter.30
  767.0 19.0 reduce-scatter.40
  788.7 19.9 reduce-scatter.28
  811.0 20.1 reduce-scatter.24
  833.8 19.9 reduce-scatter.16
  856.1 20.0 reduce-scatter.20
  878.9 24.8 reduce-scatter.36
  906.2 24.8 reduce-scatter.32
where the time goes:
time: 950 us; the launch traced here: 940 us
  waiting for transfers between devices  634 us (67%)
  matrix products  87.9 us (9%)
  blocking collectives  63.4 us (7%)
  other arithmetic  57.3 us (6%)
  local copies, waits for them, and re-layouts  56.3 us (6%)
  starting transfers between devices  23.9 us (3%)
  between operations  17 us (2%)
    reduce_scatter x1, waiting for transfers between devices, body(): lax.psum_scatter(grad_w_contract.astype(jnp.bfloat16), 'seq', scatter_dim...  145 us
    reduce_scatter x1, waiting for transfers between devices, body(): lax.psum_scatter(grad_w_expand.astype(jnp.bfloat16), 'seq', scatter_dimen...  130 us
    reduce_scatter x1, waiting for transfers between devices, body(): lax.psum_scatter(grad_w_recept.astype(jnp.bfloat16), 'seq', scatter_dimen...  70.3 us
    reduce_scatter x1, waiting for transfers between devices, body(): lax.psum_scatter(grad_w_value.astype(jnp.bfloat16), 'seq', scatter_dimens...  70.1 us
    reduce_scatter x1, waiting for transfers between devices, body(): lax.psum_scatter(grad_w_key.astype(jnp.bfloat16), 'seq', scatter_dimensio...  70 us
    unnamed x2, blocking collectives  40.9 us
    reduce_scatter x1, waiting for transfers between devices, body(): lax.psum_scatter(row_sums[5].astype(jnp.bfloat16), 'ch', scatter_dimensio...  26.1 us
    dot_general x7, matrix products, outer_sum(): lax.dot_general(rows_in.reshape(-1, rows_in.shape[-1]), grad_in.reshape(-...  25.8 us
  transfers between devices with their start and end apart: 22, of which 17 were waited for; matrix products, arithmetic and copies ran while one was open for 14% of the time, Pallas kernels for 0%

commit v1 on v0

--- a/solution.py
+++ b/solution.py
@@ -1,8 +1,11 @@
+import functools
 import math
 
 import jax
 import jax.numpy as jnp
 from jax import lax
+from jax.experimental import pallas as pl
+from jax.experimental.pallas import tpu as pltpu
 from jax.sharding import PartitionSpec as P
 
 EPS = 1e-05
@@ -219,6 +222,210 @@
         grad_first,
         grad_rate,
     )
+
+
+MESH = pl.DeviceIdType.MESH
+AXES = "kzyx"
+
+
+def axis_sizes():
+    seq_size, ch_size = lax.axis_size("seq"), lax.axis_size("ch")
+    return {"k": 2, "x": ch_size // 2, "y": 2, "z": seq_size // 2}
+
+
+def coordinates():
+    seq_at, ch_at = lax.axis_index("seq"), lax.axis_index("ch")
+    return {"z": seq_at // 2, "y": seq_at % 2, "x": ch_at // 2, "k": ch_at % 2}
+
+
+def device_at(place):
+    return (place["z"] * 2 + place["y"], place["x"] * 2 + place["k"])
+
+
+def moved(place, sizes, axis, step):
+    return {**place, axis: lax.rem(place[axis] + step, sizes[axis])}
+
+
+def greet(sizes, place):
+    barrier = pltpu.get_barrier_semaphore()
+    total = 0
+    for axis in AXES:
+        for step in range(1, sizes[axis]):
+            there = moved(place, sizes, axis, step)
+            pl.semaphore_signal(barrier, inc=1, device_id=device_at(there), device_id_type=MESH)
+            total += 1
+    pl.semaphore_wait(barrier, total)
+
+
+class Piece:
+    def __init__(self, current, order, sizes, place, landings, sends, receives):
+        self.current, self.order, self.sizes, self.place = current, order, sizes, place
+        self.landings, self.sends, self.receives = landings, sends, receives
+        self.axes = [axis for axis in AXES if axis in order]
+        self.stage = 0
+
+    def start(self):
+        axis = self.order[self.stage]
+        at = self.axes.index(axis)
+        self.copies = []
+        for step in range(1, self.sizes[axis]):
+            there = moved(self.place, self.sizes, axis, step)
+            where = (slice(None),) * at + (there[axis],)
+            copy = pltpu.make_async_remote_copy(
+                src_ref=self.current.at[where],
+                dst_ref=self.landings[self.stage].at[step - 1],
+                send_sem=self.sends[self.stage][step - 1],
+                recv_sem=self.receives[self.stage][step - 1],
+                device_id=device_at(there),
+                device_id_type=MESH,
+            )
+            copy.start()
+            self.copies.append(copy)
+
+    def finish(self, out_ref=None, own_ref=None):
+        axis = self.order[self.stage]
+        at = self.axes.index(axis)
+        landing = self.landings[self.stage]
+        others = self.sizes[axis] - 1
+        if own_ref is None:
+            own_ref = self.current.at[(slice(None),) * at + (self.place[axis],)]
+        for copy in self.copies:
+            copy.wait()
+        remaining = [a for a in self.axes if a != axis]
+        lead = tuple(self.sizes[a] for a in remaining)
+        rows, columns = landing.shape[-2:]
+        tile = math.gcd(rows, max(16, 32768 // columns))
+        blocks = math.prod(lead)
+
+        def add(index, carry):
+            part = index % (rows // tile)
+            rest = index // (rows // tile)
+            where = ()
+            for size in reversed(lead):
+                where = (rest % size,) + where
+                rest = rest // size
+            where = where + (pl.ds(pl.multiple_of(part * tile, tile), tile), slice(None))
+            total = own_ref[where].astype(jnp.float32)
+            for other in range(others):
+                total = total + landing[(other,) + where].astype(jnp.float32)
+            if out_ref is None:
+                landing[(0,) + where] = total.astype(jnp.bfloat16)
+            else:
+                out_ref[where] = total
+            return carry
+
+        lax.fori_loop(0, blocks * (rows // tile), add, 0)
+        self.axes = remaining
+        self.current = landing.at[0]
+        self.stage += 1
+
+
+def landing_shapes(order, sizes, rows, columns):
+    axes = [axis for axis in AXES if axis in order]
+    shapes = []
+    for axis in order:
+        axes = [a for a in axes if a != axis]
+        shapes.append((sizes[axis] - 1,) + tuple(sizes[a] for a in axes) + (rows, columns))
+    return shapes
+
+
+def scatter_kernel(plan, sizes, *refs):
+    count = len(plan)
+    inputs, outs = refs[:count], refs[count : 2 * count]
+    scratch = list(refs[2 * count :])
+    place = coordinates()
+    send_sems, recv_sems, own_sems = scratch[-3:]
+    used = 0
+    pieces, owns, loads = [], [], []
+    for index, order in enumerate(plan):
+        own = scratch.pop(0)
+        landings = [scratch.pop(0) for _ in order]
+        sends, receives = [], []
+        for axis in order:
+            sends.append([send_sems.at[used + s] for s in range(sizes[axis] - 1)])
+            receives.append([recv_sems.at[used + s] for s in range(sizes[axis] - 1)])
+            used += sizes[axis] - 1
+        piece = Piece(inputs[index], order, sizes, place, landings, sends, receives)
+        at = piece.axes.index(order[0])
+        load = pltpu.make_async_copy(
+            inputs[index].at[(slice(None),) * at + (place[order[0]],)], own, own_sems.at[index]
+        )
+        load.start()
+        pieces.append(piece)
+        owns.append(own)
+        loads.append(load)
+    greet(sizes, place)
+    stages = len(plan[0])
+    ahead = 2
+    for index in range(min(ahead, count)):
+        pieces[index].start()
+    for turn in range(count + stages - 1):
+        for stage in reversed(range(stages)):
+            index = turn - stage
+            if not 0 <= index < count:
+                continue
+            piece = pieces[index]
+            if stage == 0:
+                loads[index].wait()
+                piece.finish(own_ref=owns[index])
+                if index + ahead < count:
+                    pieces[index + ahead].start()
+            elif stage < stages - 1:
+                piece.finish()
+            else:
+                piece.finish(out_ref=outs[index])
+            if stage < stages - 1:
+                piece.start()
+
+
+def scatter_sum(terms, orders):
+    sizes = axis_sizes()
+    scratch, outs, total = [], [], 0
+    for term, order in zip(terms, orders):
+        rows, columns = term.shape[-2:]
+        at = [axis for axis in AXES if axis in order].index(order[0])
+        scratch.append(pltpu.VMEM(term.shape[:at] + term.shape[at + 1 :], jnp.bfloat16))
+        for shape in landing_shapes(order, sizes, rows, columns):
+            scratch.append(pltpu.VMEM(shape, jnp.bfloat16))
+        outs.append(jax.ShapeDtypeStruct((rows, columns), jnp.float32))
+        total += sum(sizes[axis] - 1 for axis in order)
+    scratch += [
+        pltpu.SemaphoreType.DMA((total,)),
+        pltpu.SemaphoreType.DMA((total,)),
+        pltpu.SemaphoreType.DMA((len(terms),)),
+    ]
+    return pl.pallas_call(
+        functools.partial(scatter_kernel, orders, sizes),
+        out_shape=outs,
+        in_specs=[pl.BlockSpec(memory_space=pl.ANY)] * len(terms),
+        out_specs=[pl.BlockSpec(memory_space=pltpu.VMEM)] * len(terms),
+        scratch_shapes=scratch,
+        compiler_params=pltpu.CompilerParams(
+            collective_id=0, has_side_effects=True, vmem_limit_bytes=60 * 2**20
+        ),
+    )(*terms)
+
+
+def by_owner(grad, sizes):
+    rows = grad.shape[0] // (sizes["z"] * sizes["y"])
+    columns = grad.shape[1] // (sizes["x"] * sizes["k"])
+    split = grad.astype(jnp.bfloat16).reshape(
+        sizes["z"], sizes["y"], rows, sizes["x"], sizes["k"], columns
+    )
+    return split.transpose(4, 0, 1, 3, 2, 5)
+
+
+def vectors_by_owner(vectors, sizes):
+    part = vectors[0].shape[0] // (sizes["z"] * sizes["y"] * sizes["x"] * sizes["k"])
+    stacked = jnp.stack(vectors).reshape(
+        len(vectors), sizes["z"], sizes["y"], sizes["x"], sizes["k"], part
+    )
+    flat = stacked.transpose(4, 1, 2, 3, 0, 5).reshape(
+        sizes["k"], sizes["z"], sizes["y"], sizes["x"], len(vectors) * part
+    )
+    rows = 16 * -(-flat.shape[-1] // 2048)
+    flat = jnp.pad(flat, ((0, 0),) * 4 + ((0, rows * 128 - flat.shape[-1]),))
+    return flat.astype(jnp.bfloat16).reshape(flat.shape[:4] + (rows, 128))
 
 
 def body(
@@ -388,118 +595,49 @@
     grad_tokens = (grad_middle + norm_back(grad_normed_mix, unit_mix, factor_mix, gain_mix)).astype(
         NARROW_TYPE
     )
-    row_sums = (
-        lax.psum_scatter(
-            grad_w_key.astype(jnp.bfloat16), "seq", scatter_dimension=0, tiled=True
-        ).astype(jnp.float32),
-        lax.psum_scatter(
-            grad_w_value.astype(jnp.bfloat16), "seq", scatter_dimension=0, tiled=True
-        ).astype(jnp.float32),
-        lax.psum_scatter(
-            grad_w_recept.astype(jnp.bfloat16), "seq", scatter_dimension=0, tiled=True
-        ).astype(jnp.float32),
-        lax.psum_scatter(
-            grad_w_output.astype(jnp.bfloat16), "seq", scatter_dimension=0, tiled=True
-        ).astype(jnp.float32),
-        lax.psum_scatter(
-            grad_w_expand.astype(jnp.bfloat16), "seq", scatter_dimension=0, tiled=True
-        ).astype(jnp.float32),
-        lax.psum_scatter(
-            grad_w_contract.astype(jnp.bfloat16), "seq", scatter_dimension=0, tiled=True
-        ).astype(jnp.float32),
-        lax.psum_scatter(
-            grad_w_gate.astype(jnp.bfloat16), "seq", scatter_dimension=0, tiled=True
-        ).astype(jnp.float32),
-        lax.psum_scatter(
-            grad_gain_mix.astype(jnp.bfloat16), "seq", scatter_dimension=0, tiled=True
-        ).astype(jnp.float32),
-        lax.psum_scatter(
-            grad_bias_mix.astype(jnp.bfloat16), "seq", scatter_dimension=0, tiled=True
-        ).astype(jnp.float32),
-        lax.psum_scatter(
-            grad_gain_ffn.astype(jnp.bfloat16), "seq", scatter_dimension=0, tiled=True
-        ).astype(jnp.float32),
-        lax.psum_scatter(
-            grad_bias_ffn.astype(jnp.bfloat16), "seq", scatter_dimension=0, tiled=True
-        ).astype(jnp.float32),
-        lax.psum_scatter(
-            grad_mix_key.astype(jnp.bfloat16), "seq", scatter_dimension=0, tiled=True
-        ).astype(jnp.float32),
-        lax.psum_scatter(
-            grad_mix_value.astype(jnp.bfloat16), "seq", scatter_dimension=0, tiled=True
-        ).astype(jnp.float32),
-        lax.psum_scatter(
-            grad_mix_recept.astype(jnp.bfloat16), "seq", scatter_dimension=0, tiled=True
-        ).astype(jnp.float32),
-        lax.psum_scatter(
-            grad_blend_key.astype(jnp.bfloat16), "seq", scatter_dimension=0, tiled=True
-        ).astype(jnp.float32),
-        lax.psum_scatter(
-            grad_blend_gate.astype(jnp.bfloat16), "seq", scatter_dimension=0, tiled=True
-        ).astype(jnp.float32),
-        lax.psum_scatter(
-            grad_time_decay.astype(jnp.bfloat16), "seq", scatter_dimension=0, tiled=True
-        ).astype(jnp.float32),
-        lax.psum_scatter(
-            grad_time_first.astype(jnp.bfloat16), "seq", scatter_dimension=0, tiled=True
-        ).astype(jnp.float32),
-    )
+    sizes = axis_sizes()
+    vectors = (
+        grad_gain_mix,
+        grad_bias_mix,
+        grad_gain_ffn,
+        grad_bias_ffn,
+        grad_mix_key,
+        grad_mix_value,
+        grad_mix_recept,
+        grad_blend_key,
+        grad_blend_gate,
+        grad_time_decay,
+        grad_time_first,
+    )
+    contract_terms = by_owner(grad_w_contract, sizes)
+    expand_terms = by_owner(grad_w_expand, sizes)
+    half_rows = contract_terms.shape[-2] // 2
+    half_columns = expand_terms.shape[-1] // 2
+    terms = [
+        contract_terms[..., :half_rows, :],
+        expand_terms[..., :half_columns],
+        contract_terms[..., half_rows:, :],
+        expand_terms[..., half_columns:],
+        by_owner(grad_w_gate, sizes),
+        by_owner(grad_w_output, sizes),
+        by_owner(grad_w_key, sizes),
+        by_owner(grad_w_value, sizes),
+        by_owner(grad_w_recept, sizes),
+        vectors_by_owner(vectors, sizes),
+    ]
+    orders = ["kxyz", "kyxz", "kxyz", "kyxz", "kxyz", "kyxz", "kxyz", "kyxz", "kxyz", "kyxz"]
+    sums = scatter_sum(terms, orders)
+    part = model_width // (lax.axis_size("seq") * group_size)
+    vector_sums = sums[9].reshape(-1)[: len(vectors) * part].reshape(len(vectors), part)
     all_sums = (
-        lax.psum_scatter(
-            row_sums[0].astype(jnp.bfloat16), "ch", scatter_dimension=1, tiled=True
-        ).astype(jnp.float32),
-        lax.psum_scatter(
-            row_sums[1].astype(jnp.bfloat16), "ch", scatter_dimension=1, tiled=True
-        ).astype(jnp.float32),
-        lax.psum_scatter(
-            row_sums[2].astype(jnp.bfloat16), "ch", scatter_dimension=1, tiled=True
-        ).astype(jnp.float32),
-        lax.psum_scatter(
-            row_sums[3].astype(jnp.bfloat16), "ch", scatter_dimension=1, tiled=True
-        ).astype(jnp.float32),
-        lax.psum_scatter(
-            row_sums[4].astype(jnp.bfloat16), "ch", scatter_dimension=1, tiled=True
-        ).astype(jnp.float32),
-        lax.psum_scatter(
-            row_sums[5].astype(jnp.bfloat16), "ch", scatter_dimension=1, tiled=True
-        ).astype(jnp.float32),
-        lax.psum_scatter(
-            row_sums[6].astype(jnp.bfloat16), "ch", scatter_dimension=1, tiled=True
-        ).astype(jnp.float32),
-        lax.psum_scatter(
-            row_sums[7].astype(jnp.bfloat16), "ch", scatter_dimension=0, tiled=True
-        ).astype(jnp.float32),
-        lax.psum_scatter(
-            row_sums[8].astype(jnp.bfloat16), "ch", scatter_dimension=0, tiled=True
-        ).astype(jnp.float32),
-        lax.psum_scatter(
-            row_sums[9].astype(jnp.bfloat16), "ch", scatter_dimension=0, tiled=True
-        ).astype(jnp.float32),
-        lax.psum_scatter(
-            row_sums[10].astype(jnp.bfloat16), "ch", scatter_dimension=0, tiled=True
-        ).astype(jnp.float32),
-        lax.psum_scatter(
-            row_sums[11].astype(jnp.bfloat16), "ch", scatter_dimension=0, tiled=True
-        ).astype(jnp.float32),
-        lax.psum_scatter(
-            row_sums[12].astype(jnp.bfloat16), "ch", scatter_dimension=0, tiled=True
-        ).astype(jnp.float32),
-        lax.psum_scatter(
-            row_sums[13].astype(jnp.bfloat16), "ch", scatter_dimension=0, tiled=True
-        ).astype(jnp.float32),
-        lax.psum_scatter(
-            row_sums[14].astype(jnp.bfloat16), "ch", scatter_dimension=0, tiled=True
-        ).astype(jnp.float32),
-        lax.psum_scatter(
-            row_sums[15].astype(jnp.bfloat16), "ch", scatter_dimension=0, tiled=True
-        ).astype(jnp.float32),
-        lax.psum_scatter(
-            row_sums[16].astype(jnp.bfloat16), "ch", scatter_dimension=0, tiled=True
-        ).astype(jnp.float32),
-        lax.psum_scatter(
-            row_sums[17].astype(jnp.bfloat16), "ch", scatter_dimension=0, tiled=True
-        ).astype(jnp.float32),
-    )
+        sums[6],
+        sums[7],
+        sums[8],
+        sums[5],
+        jnp.concatenate([sums[1], sums[3]], axis=1),
+        jnp.concatenate([sums[0], sums[2]], axis=0),
+        sums[4],
+    ) + tuple(vector_sums[i] for i in range(len(vectors)))
     return (
         mixed_out,
         grad_tokens,

time: 950 us -> 578 us (0.61)
  waiting for transfers between devices: 634 us -> 22.5 us
  Pallas kernels: 0 us -> 243 us
  local copies, waits for them, and re-layouts: 56.3 us -> 153 us
  blocking collectives: 63.4 us -> 0 us
  between operations: 17 us -> 2.42 us
  other arithmetic: 57.3 us -> 42.9 us
  matrix products: 87.9 us -> 76.7 us
    reduce_scatter x14 -> x0, waiting for transfers between devices: 610 us -> none  [the longest x1 145 us: body(): lax.psum_scatter(grad_w_contract.astype(jnp.bfloat16), 'seq', scatter_dim...]
    pallas_call x0 -> x1, Pallas kernels: none -> 243 us  [scatter_sum(): pl.pallas_call(functools.partial(scatter_kernel, orders, sizes), out_shap...]
    reshape x0 -> x16, local copies, waits for them, and re-layouts: none -> 81.1 us  [the longest x14 80.3 us: by_owner(): grad.astype(jnp.bfloat16)]
    unnamed x2 -> x0, blocking collectives: 40.9 us -> none
    all_to_all x2 -> x0, blocking collectives: 22.5 us -> none  [the longest x1 11.2 us: body(): lax.all_to_all(grad_key_cols.astype(NARROW_TYPE), 'ch', split_axis=1, con...]
    convert_element_type x20 -> x0, other arithmetic: 17.5 us -> none  [the longest x18 17.5 us: body(): all_sums = (lax.psum_scatter(row_sums[0].astype(jnp.bfloat16), 'ch', scat...]
    slice x0 -> x3, local copies, waits for them, and re-layouts: none -> 13.7 us  [the longest x1 6.04 us: body(): expand_terms[..., half_columns:]]
    unnamed x203 -> x189, local copies, waits for them, and re-layouts: 19.8 us -> 17.8 us
  transfers between devices with their start and end apart: 22 -> 10, of which waited for: 17 -> 5; matrix products, arithmetic and copies ran while one was open for 14% -> 25% of each run, Pallas kernels for 0% -> 0%
where the time goes in v1:
time: 578 us; the launch traced here: 571 us
  Pallas kernels  243 us (42%)
  local copies, waits for them, and re-layouts  153 us (26%)
  matrix products  76.7 us (13%)
  other arithmetic  42.9 us (7%)
  starting transfers between devices  31.2 us (5%)
  waiting for transfers between devices  22.5 us (4%)
    pallas_call x1, Pallas kernels, scatter_sum(): pl.pallas_call(functools.partial(scatter_kernel, orders, sizes), out_shap...  243 us
    reshape x14, local copies, waits for them, and re-layouts, by_owner(): grad.astype(jnp.bfloat16)  80.3 us
    dot_general x7, matrix products, outer_sum(): lax.dot_general(rows_in.reshape(-1, rows_in.shape[-1]), grad_in.reshape(-...  19.7 us
    unnamed x189, local copies, waits for them, and re-layouts  17.8 us
    dot_general x7, matrix products, project_back(): lax.dot_general(flat_rows, scaling_coefficient, (((1,), (1,)), ((), ())),...  17.8 us
    dot_general x7, matrix products, project(): jnp.dot(flat_rows, scaling_coefficient, preferred_element_type=WIDE_TYPE)  16.7 us
  transfers between devices with their start and end apart: 10, of which 5 were waited for; matrix products, arithmetic and copies ran while one was open for 25% of the time, Pallas kernels for 0%

profile of v1, /device:TPU:0, one launch (start us, length us, event | category | flops | bytes accessed | tf_op | source)
XLA Modules:
  0.0 571.3 jit_solution(15880507643894719667)
XLA Ops:
  9.1 2.5 subtract_exponential_fusion.3
  11.9 3.4 exponential_select_fusion
  15.4 3.0 add_convert_fusion.4
  21.1 3.9 all-to-all-start.1
  25.7 3.1 fusion.73
  30.8 3.0 all-to-all-done.1
  33.8 4.4 all-to-all-start
  43.5 3.6 all-to-all-done
  49.3 2.5 copy.242
  55.6 9.2 %fusion.91 = f32[2,2,9,256]{2,0,3,1:T(2,128)} fusion(f32[2,2,8,256]{2,0,3,1:T(2,128)} %copy.248, f32[2,8,256]{1,2,0:T(8,128)S(1)} %bitcast.343, f32[2,9,256]{1,2,0:T(8,128)} %copy-done.63, pred[9,8]{1,0:T(8,128)(4,1)S(1)} %iota_compare_fusion.1, f32[2,2,256]{0,2,1:T(8,128)} %copy.239, f32[2,9,256]{1,2,0:T(8,128)} %copy.238), kind=kOutput, calls=%fused_computation.80 | convolution fusion | flops 1050624 | bytes 127048 | tf_op jit(solution)/shard_map/njkc,pnkc->pnjc/dot_general | solution.py:112
  66.0 3.6 bitcast_multiply_fusion.1
  73.6 3.5 all-to-all-start.2
  78.9 7.0 %all-to-all-done.2 = bf16[2,512,256]{2,0,1:T(2,128)(2,1)S(1)} async-done(((bf16[2,512,256]{2,0,1:T(2,128)(2,1)}), bf16[2,512,256]{2,0,1:T(2,128)(2,1)S(1)}, u32[]{:S(2)}, u32[]{:S(2)}) %all-to-all-start.2) | async-done | bytes 524320 | tf_op jit(solution)/shard_map/all_to_all | solution.py:498
  94.1 4.6 slice_reduce_fusion
  98.6 2.5 copy.279
  101.2 2.5 copy.280
  105.7 6.0 %fusion.8 = f32[2,128,4096]{2,1,0:T(8,128)S(1)} fusion(bf16[2,128,1024]{2,1,0:T(8,128)(2,1)S(1)} %get-tuple-element.72, bf16[1024,4096]{1,0:T(8,128)(2,1)} %param.32), kind=kOutput, calls=%fused_computation.12 | convolution fusion | flops 2148532224 | bytes 13107200 | tf_op jit(solution)/shard_map/dot_general | solution.py:42
  111.7 2.4 fusion.2
  118.5 6.2 %bitcast_convert_fusion.1 = bf16[4096,1024]{1,0:T(8,128)(2,1)} fusion(bf16[2,128,1024]{2,1,0:T(8,128)(2,1)S(1)} %get-tuple-element.86, f32[2,128,4096]{2,1,0:T(8,128)S(1)} %fusion.8), kind=kOutput, calls=%fused_computation.1 | convolution fusion | flops 2153775104 | bytes 13107200 | tf_op jit(solution)/shard_map/dot_general | solution.py:55
  124.7 5.7 %fusion.4 = f32[2,128,1024]{2,1,0:T(8,128)S(1)} fusion(bf16[2,128,4096]{2,1,0:T(8,128)(2,1)S(1)} %fusion.17, bf16[1024,4096]{1,0:T(8,128)(2,1)} %param.32), kind=kOutput, calls=%fused_computation.6 | convolution fusion | flops 2147483648 | bytes 11534336 | tf_op jit(solution)/shard_map/dot_general | solution.py:48
  130.5 5.7 bitcast_convert_fusion
  140.6 14.5 %reshape.555 = bf16[4,2,512,2,2,256]{5,4,3,2,1,0:T(2,128)(2,1)} reshape(bf16[4096,1024]{1,0:T(8,128)(2,1)} %bitcast_convert_fusion.1) | data formatting | bytes 16777216 | tf_op jit(solution)/shard_map/reshape | solution.py:412
  155.1 8.2 %copy.320 = bf16[4,2,512,2,2,256]{5,2,3,1,0,4:T(8,128)(2,1)} copy(bf16[4,2,512,2,2,256]{5,4,3,2,1,0:T(2,128)(2,1)} %reshape.555) | data formatting | bytes 16777216 | tf_op jit(solution)/shard_map/reshape | solution.py:412
  163.3 6.0 %fusion.134 = (bf16[2,4,2,2,256,256]{5,4,3,2,1,0:T(8,128)(2,1)}, bf16[2,4,2,2,256,256]{5,4,3,2,1,0:T(8,128)(2,1)}) fusion(bf16[2,4,2,2,512,256]{5,4,3,2,1,0:T(8,128)(2,1)} %bitcast.299), kind=kLoop, calls=%fused_computation.230 | loop fusion | bytes 16777216 | tf_op jit(solution)/shard_map/slice | solution.py:619
  169.3 14.4 %reshape.556 = bf16[4,2,128,2,2,1024]{5,4,3,2,1,0:T(2,128)(2,1)} reshape(bf16[1024,4096]{1,0:T(8,128)(2,1)} %bitcast_convert_fusion) | data formatting | bytes 16777216 | tf_op jit(solution)/shard_map/reshape | solution.py:412
  183.7 9.8 %copy.319 = bf16[4,2,128,2,2,1024]{5,2,3,1,0,4:T(8,128)(2,1)} copy(bf16[4,2,128,2,2,1024]{5,4,3,2,1,0:T(2,128)(2,1)} %reshape.556) | data formatting | bytes 16777216 | tf_op jit(solution)/shard_map/reshape | solution.py:412
  193.5 6.0 %fusion.133 = (bf16[2,4,2,2,128,512]{5,4,3,2,1,0:T(8,128)(2,1)}, bf16[2,4,2,2,128,512]{5,4,3,2,1,0:T(8,128)(2,1)}) fusion(bf16[2,4,2,2,128,1024]{5,4,3,2,1,0:T(8,128)(2,1)} %bitcast.300), kind=kLoop, calls=%fused_computation.229 | loop fusion | bytes 16777216 | tf_op jit(solution)/shard_map/slice | solution.py:620
  202.1 2.7 reshape.557
  204.8 3.5 copy.325
  213.5 4.6 all-to-all-start.3
  220.4 3.3 reshape.558
  226.2 2.8 reshape.565
  229.1 3.3 copy.321
  232.4 2.5 fusion.137
  234.9 2.5 copy.259
  242.2 6.0 %fusion.88 = f32[2,2,8,256]{2,0,3,1:T(2,128)} fusion(f32[2,2,8,256]{2,0,3,1:T(2,128)} %copy.261, f32[2,9,8,256]{2,1,3,0:T(8,128)} %exponential_select_fusion, f32[2,8,256]{1,2,0:T(8,128)S(1)} %bitcast.344), kind=kOutput, calls=%fused_computation.78 | convolution fusion | flops 794624 | bytes 2670592 | tf_op jit(solution)/shard_map/nkjc,pnkc->pnjc/dot_general | solution.py:183
  249.4 3.7 bitcast_multiply_fusion
  258.4 4.4 all-to-all-start.5
  267.4 4.4 all-to-all-done.5
  271.8 3.5 all-to-all-start.4
  279.5 4.5 all-to-all-done.4
  285.6 2.6 fusion.34
  297.0 4.5 reshape.564
  301.6 3.4 copy.322
  304.9 4.5 reshape.561
  309.5 3.5 copy.323
  313.0 3.5 fusion.98
  318.1 242.7 %shard_map.390 = (f32[256,256]{1,0:T(8,128)}, f32[128,512]{1,0:T(8,128)}, f32[256,256]{1,0:T(8,128)}, f32[128,512]{1,0:T(8,128)}, f32[128,256]{1,0:T(8,128)}, /*...) custom-call(bf16[2,4,2,2,256,256]{5,4,3,2,1,0:T(8,128)(2,1)} %get-tup, ...), custom_call_target="tpu_custom_call" | custom-call | tf_op jit(solution)/shard_map/pallas_call | solution.py:397
  (320 shorter events, 105.2 us)
Async XLA Ops:
  0.7 113.5 %copy-start = (bf16[1024,1024]{1,0:T(8,128)(2,1)S(1)}, bf16[1024,1024]{1,0:T(8,128)(2,1)}, u32[]{:S(2)}) copy-start(bf16[1024,1024]{1,0:T(8,128)(2,1)} %param.34) | copy-start | bytes 6291460
  0.7 7.5 %copy-start.82 = (f32[1024]{0:T(1024)S(1)}, f32[1024]{0:T(1024)}, u32[]{:S(2)}) copy-start(f32[1024]{0:T(1024)} %param.44) | copy-start | bytes 12292
  0.7 7.5 %copy-start.81 = (s32[2]{0:T(128)S(1)}, s32[2]{0:T(128)}, u32[]{:S(2)}) copy-start(s32[2]{0:T(128)} %param.25) | copy-start | bytes 28
  3.4 5.7 copy-start.75
  5.7 9.7 %collective-permute-start = (f32[2,1,1024]{2,1,0:T(1,128)S(1)}, f32[2,1,1024]{2,1,0:T(1,128)S(1)}, u32[]{:S(2)}, u32[]{:S(2)}) collective-permute-start(f32[2,1,1024]{2,1,0:T(1,128)S(1)} %slice.173), channel_id=1, source_target_pairs={{0,1},{1,2},{2,3},{4,5},{5,6},{6,7},{8,9},{9,10},{10,11},{12,13},{... | collective-permute-start | bytes 24584 | tf_op jit(solution)/shard_map/ppermute | solution.py:20
  11.8 3.5 copy-start.63
  11.9 3.6 copy-start.8
  11.9 3.5 copy-start.72
  11.9 3.5 copy-start.74
  15.4 3.8 copy-start.49
  18.4 7.2 %copy-start.55 = (bf16[2,128,1024]{2,1,0:T(8,128)(2,1)}, bf16[2,128,1024]{2,1,0:T(8,128)(2,1)S(1)}, u32[]{:S(2)}) copy-start(bf16[2,128,1024]{2,1,0:T(8,128)(2,1)S(1)} %get-tuple-element.83) | copy-start | bytes 1572868
  21.1 12.7 %all-to-all-start.1 = ((bf16[2,128,1024]{1,0,2:T(2,128)(2,1)}), bf16[2,128,1024]{1,0,2:T(2,128)(2,1)S(1)}, u32[]{:S(2)}, u32[]{:S(2)}) async-start(bf16[2,128,1024]{1,0,2:T(2,128)(2,1)} %copy.243), calls=%async_computation.1 | async-start | bytes 1048576 | tf_op jit(solution)/shard_map/all_to_all | solution.py:479
  33.8 13.3 %all-to-all-start = ((bf16[2,128,1024]{1,0,2:T(2,128)(2,1)}), bf16[2,128,1024]{1,0,2:T(2,128)(2,1)}, u32[]{:S(2)}, u32[]{:S(2)}) async-start(bf16[2,128,1024]{1,0,2:T(2,128)(2,1)} %copy.240), calls=%async_computation | async-start | bytes 1048576 | tf_op jit(solution)/shard_map/all_to_all | solution.py:478
  43.5 27.4 %copy-start.4 = (f32[2,4,128,256]{3,2,1,0:T(8,128)}, f32[2,4,128,256]{3,2,1,0:T(8,128)S(1)}, u32[]{:S(2)}) copy-start(f32[2,4,128,256]{3,2,1,0:T(8,128)S(1)} %copy.245) | copy-start | bytes 3145732
  73.6 12.3 %all-to-all-start.2 = ((bf16[2,512,256]{2,0,1:T(2,128)(2,1)}), bf16[2,512,256]{2,0,1:T(2,128)(2,1)S(1)}, u32[]{:S(2)}, u32[]{:S(2)}) async-start(bf16[2,512,256]{2,0,1:T(2,128)(2,1)} %copy.254), calls=%async_computation.2 | async-start | bytes 1048576 | tf_op jit(solution)/shard_map/all_to_all | solution.py:498
  86.2 3.6 copy-start.44
  92.2 11.5 %collective-permute-start.1 = (f32[2,1,1024]{2,1,0:T(1,128)S(1)}, f32[2,1,1024]{2,1,0:T(1,128)S(1)}, u32[]{:S(2)}, u32[]{:S(2)}) collective-permute-start(f32[2,1,1024]{2,1,0:T(1,128)S(1)} %slice.181), channel_id=1, source_target_pairs={{0,1},{1,2},{2,3},{4,5},{5,6},{6,7},{8,9},{9,10},{10,11},{12,13},{... | collective-permute-start | bytes 24584 | tf_op jit(solution)/shard_map/ppermute | solution.py:20
  103.7 8.0 %slice-start = ((s8[8388608]{0:T(1024)(128)(4,1)}), s8[4194304]{0:T(1024)(128)(4,1)S(1)}, s32[]{:S(2)}) async-start(s8[8388608]{0:T(1024)(128)(4,1)} %bitcast.313), calls=%async_computation.6 | async-start | bytes 8388608
  105.7 8.4 %copy-start.61 = (bf16[2,128,1024]{2,1,0:T(8,128)(2,1)}, bf16[2,128,1024]{2,1,0:T(8,128)(2,1)S(1)}, u32[]{:S(2)}) copy-start(bf16[2,128,1024]{2,1,0:T(8,128)(2,1)S(1)} %get-tuple-element.73) | copy-start | bytes 1572868
  105.7 6.0 %slice-start.1 = ((s8[8388608]{0:T(1024)(128)(4,1)}), s8[4194304]{0:T(1024)(128)(4,1)S(1)}, s32[]{:S(2)}) async-start(s8[8388608]{0:T(1024)(128)(4,1)} %bitcast.313), calls=%async_computation.7 | async-start | bytes 8388608
  116.1 20.0 %copy-start.53 = (bf16[2,128,1024]{2,1,0:T(8,128)(2,1)}, bf16[2,128,1024]{2,1,0:T(8,128)(2,1)S(1)}, u32[]{:S(2)}) copy-start(bf16[2,128,1024]{2,1,0:T(8,128)(2,1)S(1)} %get-tuple-element.74) | copy-start | bytes 1572868
  130.4 5.7 %copy-start.39 = (f32[2,128,1024]{2,1,0:T(8,128)}, f32[2,128,1024]{2,1,0:T(8,128)S(1)}, u32[]{:S(2)}) copy-start(f32[2,128,1024]{2,1,0:T(8,128)S(1)} %fusion.4) | copy-start | bytes 3145732
  130.4 5.7 copy-start.12
  139.1 69.2 %collective-permute-start.2 = (f32[2,1,1024]{2,1,0:T(1,128)S(1)}, f32[2,1,1024]{2,1,0:T(1,128)S(1)}, u32[]{:S(2)}, u32[]{:S(2)}) collective-permute-start(f32[2,1,1024]{2,1,0:T(1,128)S(1)} %slice.184), channel_id=1, source_target_pairs={{1,0},{2,1},{3,2},{5,4},{6,5},{7,6},{9,8},{10,9},{11,10},{13,12},{... | collective-permute-start | bytes 24584 | tf_op jit(solution)/shard_map/ppermute | solution.py:20
  193.5 6.0 %copy-start.54 = (bf16[2,128,1024]{2,1,0:T(8,128)(2,1)S(1)}, bf16[2,128,1024]{2,1,0:T(8,128)(2,1)}, u32[]{:S(2)}) copy-start(bf16[2,128,1024]{2,1,0:T(8,128)(2,1)} %copy-done.53) | copy-start | bytes 1572868
  193.5 6.0 %copy-start.62 = (bf16[2,128,1024]{2,1,0:T(8,128)(2,1)S(1)}, bf16[2,128,1024]{2,1,0:T(8,128)(2,1)}, u32[]{:S(2)}) copy-start(bf16[2,128,1024]{2,1,0:T(8,128)(2,1)} %copy-done.61) | copy-start | bytes 1572868
  204.8 3.5 copy-start.40
  204.8 3.5 copy-start.41
  204.8 3.5 copy-start.46
  209.8 8.3 %copy-start.13 = (f32[2,128,1024]{2,1,0:T(8,128)}, f32[2,128,1024]{2,1,0:T(8,128)S(1)}, u32[]{:S(2)}) copy-start(f32[2,128,1024]{2,1,0:T(8,128)S(1)} %multiply_add_fusion.1) | copy-start | bytes 3145732
  212.4 13.1 %copy-start.33 = (bf16[2,128,1024]{2,1,0:T(8,128)(2,1)}, bf16[2,128,1024]{2,1,0:T(8,128)(2,1)S(1)}, u32[]{:S(2)}) copy-start(bf16[2,128,1024]{2,1,0:T(8,128)(2,1)S(1)} %get-tuple-element.77) | copy-start | bytes 1572868
  212.4 5.7 %copy-start.48 = (bf16[2,128,1024]{2,1,0:T(8,128)(2,1)S(1)}, bf16[2,128,1024]{2,1,0:T(8,128)(2,1)}, u32[]{:S(2)}) copy-start(bf16[2,128,1024]{2,1,0:T(8,128)(2,1)} %copy-done.47) | copy-start | bytes 1572868
  213.5 18.9 %all-to-all-start.3 = ((bf16[2,128,1024]{1,0,2:T(2,128)(2,1)}), bf16[2,128,1024]{1,0,2:T(2,128)(2,1)}, u32[]{:S(2)}, u32[]{:S(2)}) async-start(bf16[2,128,1024]{1,0,2:T(2,128)(2,1)} %copy.257), calls=%async_computation.3 | async-start | bytes 1048576 | tf_op jit(solution)/shard_map/all_to_all | solution.py:544
  232.4 5.0 copy-start.3
  232.4 5.0 copy-start.5
  257.0 8.4 %copy-start.25 = (f32[2,128,1024]{1,2,0:T(8,128)S(1)}, f32[2,128,1024]{1,2,0:T(8,128)}, u32[]{:S(2)}) copy-start(f32[2,128,1024]{1,2,0:T(8,128)} %convert_exponential_fusion) | copy-start | bytes 3145732
  257.0 8.4 %copy-start.42 = (f32[2,4,128,256]{2,3,1,0:T(8,128)S(1)}, f32[2,4,128,256]{2,3,1,0:T(8,128)}, u32[]{:S(2)}) copy-start(f32[2,4,128,256]{2,3,1,0:T(8,128)} %copy.279) | copy-start | bytes 3145732
  257.0 8.4 %copy-start.43 = (f32[2,4,128,256]{2,3,1,0:T(8,128)S(1)}, f32[2,4,128,256]{2,3,1,0:T(8,128)}, u32[]{:S(2)}) copy-start(f32[2,4,128,256]{2,3,1,0:T(8,128)} %copy.280) | copy-start | bytes 3145732
  258.4 13.3 %all-to-all-start.5 = ((bf16[2,512,256]{2,0,1:T(2,128)(2,1)}), bf16[2,512,256]{2,0,1:T(2,128)(2,1)}, u32[]{:S(2)}, u32[]{:S(2)}) async-start(bf16[2,512,256]{2,0,1:T(2,128)(2,1)} %copy.265), calls=%async_computation.5 | async-start | bytes 1048576 | tf_op jit(solution)/shard_map/all_to_all | solution.py:561
  271.8 12.3 %all-to-all-start.4 = ((bf16[2,512,256]{2,0,1:T(2,128)(2,1)}), bf16[2,512,256]{2,0,1:T(2,128)(2,1)S(1)}, u32[]{:S(2)}, u32[]{:S(2)}) async-start(bf16[2,512,256]{2,0,1:T(2,128)(2,1)} %copy.263), calls=%async_computation.4 | async-start | bytes 1048576 | tf_op jit(solution)/shard_map/all_to_all | solution.py:558
  290.1 22.8 %collective-permute-start.3 = (f32[2,1,1024]{2,1,0:T(1,128)S(1)}, f32[2,1,1024]{2,1,0:T(1,128)S(1)}, u32[]{:S(2)}, u32[]{:S(2)}) collective-permute-start(f32[2,1,1024]{2,1,0:T(1,128)S(1)} %slice.190), channel_id=1, source_target_pairs={{1,0},{2,1},{3,2},{5,4},{6,5},{7,6},{9,8},{10,9},{11,10},{13,12},{... | collective-permute-start | bytes 24584 | tf_op jit(solution)/shard_map/ppermute | solution.py:20
  309.5 3.5 copy-start.24
  309.5 3.5 copy-start.38
  560.8 5.5 copy-start.14
  560.8 5.5 copy-start.37
  564.4 3.8 copy-start.70
  566.3 4.5 copy-start.1
  566.3 3.9 copy-start.67
  (47 other events, 90.0 us)

commit v2 on v0

v2 whole, which is shorter than its diff:
```python
import functools
import math

import jax
import jax.numpy as jnp
from jax import lax
from jax.experimental import pallas as pl
from jax.experimental.pallas import tpu as pltpu
from jax.sharding import PartitionSpec as P

EPS = 1e-05
MESH = pl.DeviceIdType.MESH
AXES = "zyx"
F32 = jnp.float32
BF16 = jnp.bfloat16
TILE = 16
WIDE = 256
SLOTS_OF_WEIGHTS = 3

NN = (((1,), (0,)), ((), ()))
NT = (((1,), (1,)), ((), ()))
TN = (((0,), (0,)), ((), ()))


def dot(left, right, how):
    return lax.dot_general(left, right, how, preferred_element_type=F32)


def axis_sizes():
    seq_size, ch_size = lax.axis_size("seq"), lax.axis_size("ch")
    return {"k": 2, "x": ch_size // 2, "y": 2, "z": seq_size // 2}


def coordinates():
    seq_at, ch_at = lax.axis_index("seq"), lax.axis_index("ch")
    return {"z": seq_at // 2, "y": seq_at % 2, "x": ch_at // 2, "k": ch_at % 2}


def device_at(place):
    return (place["z"] * 2 + place["y"], place["x"] * 2 + place["k"])


def moved(place, sizes, axis, step):
    return {**place, axis: lax.rem(place[axis] + step, sizes[axis])}


class Copies:
    def __init__(self, sends, receives):
        self.sends, self.receives, self.used = sends, receives, 0
        self.open = []

    def start(self, source, target, device):
        copy = pltpu.make_async_remote_copy(
            src_ref=source,
            dst_ref=target,
            send_sem=self.sends.at[self.used],
            recv_sem=self.receives.at[self.used],
            device_id=device,
            device_id_type=MESH,
        )
        self.used += 1
        copy.start()
        return copy


class Piece:
    def __init__(self, make, order, sizes, place, copies, held, landings, out_ref):
        self.make, self.order, self.sizes, self.place = make, order, sizes, place
        self.remote, self.held, self.landings, self.out_ref = copies, held, landings, out_ref
        self.axes = list(AXES)
        self.stage = 0
        self.copies = []

    def start(self):
        axis = self.order[self.stage]
        at = self.axes.index(axis)
        for step in range(1, self.sizes[axis]):
            there = moved(self.place, self.sizes, axis, step)
            if self.stage == 0:

                def keep(where, value, slot=step - 1):
                    self.held[(slot,) + where] = value.astype(BF16)

                self.make(there[axis], keep)
                source = self.held.at[step - 1]
            else:
                source = self.landings[self.stage - 1].at[
                    (0,) + (slice(None),) * at + (there[axis],)
                ]
            self.copies.append(
                self.remote.start(
                    source, self.landings[self.stage].at[step - 1], device_at(there)
                )
            )

    def finish(self):
        axis = self.order[self.stage]
        at = self.axes.index(axis)
        landing = self.landings[self.stage]
        others = self.sizes[axis] - 1
        for copy in self.copies:
            copy.wait()
        self.copies = []
        remaining = [a for a in self.axes if a != axis]
        if self.stage == 0:

            def add(where, value):
                for other in range(others):
                    value = value + landing[(other,) + where].astype(F32)
                landing[(0,) + where] = value.astype(BF16)

            self.make(self.place[axis], add)
        else:
            own = self.landings[self.stage - 1].at[
                (0,) + (slice(None),) * at + (self.place[axis],)
            ]
            lead = tuple(self.sizes[a] for a in remaining)
            rows, columns = landing.shape[-2:]
            tile = math.gcd(rows, max(16, 32768 // columns))
            parts = rows // tile

            def add_tile(index, carry):
                part, rest = index % parts, index // parts
                where = ()
                for size in reversed(lead):
                    where = (rest % size,) + where
                    rest = rest // size
                spot = pl.ds(pl.multiple_of(part * tile, tile), tile)
                where = where + (spot, slice(None))
                total = own[where].astype(F32)
                for other in range(others):
                    total = total + landing[(other,) + where].astype(F32)
                if remaining:
                    landing[(0,) + where] = total.astype(BF16)
                else:
                    self.out_ref[where] = total
                return carry

            lax.fori_loop(0, math.prod(lead) * parts, add_tile, 0)
        self.axes = remaining
        self.stage += 1

    def advance(self):
        self.finish()
        if self.axes:
            self.start()


class Plan:
    def __init__(self, tokens, w_expand):
        self.slots, self.length, self.width = tokens.shape
        self.hidden = w_expand.shape[1]
        self.sizes = sizes = axis_sizes()
        self.seq, self.ch = sizes["z"] * 2, sizes["x"] * 2
        self.rows = self.slots * self.length
        rows, width, hidden = self.rows, self.width, self.hidden
        self.narrow = width // self.ch
        self.broad = hidden // self.ch
        self.short = width // self.seq
        self.tall = hidden // self.seq
        half = sizes["x"] * self.narrow
        self.pieces = []
        cuts = 2 if (self.tall // 2) % 128 == 0 else 1
        self.contract_cuts = cuts
        for _ in range(cuts):
            self.pieces.append(("contract", "yxz", self.tall // cuts, self.narrow))
        cuts = 2 if (self.broad // 2) % 128 == 0 else 1
        self.expand_cuts = cuts
        for _ in range(cuts):
            self.pieces.append(("expand", "xyz", self.short, self.broad // cuts))
        first_z = "zxy" if (2 * self.short) % 128 == 0 else "xyz"
        for name, order in (
            ("gate", first_z),
            ("output", "xyz"),
            ("key", first_z),
            ("value", "xyz"),
            ("recept", "xyz"),
        ):
            self.pieces.append((name, order, self.short, self.narrow))
        vmem = pltpu.VMEM
        shapes = {
            "panels": vmem((SLOTS_OF_WEIGHTS, width, width), BF16),
            "both_hidden": vmem((2 * rows, hidden), BF16),
            "grad_expanded": vmem((rows, hidden), BF16),
            "their_expanded": vmem((rows, hidden // 2), BF16),
            "key": vmem((rows, width), BF16),
            "value": vmem((rows, width), BF16),
            "edges_out": vmem((4, 8, width), F32),
            "edges_in": vmem((4, 8, width), F32),
            "sums_out": vmem((2, 8, width), F32),
            "sums_in": vmem((2, self.ch - 1, 8, width), F32),
            "states": vmem((8, width), F32),
            "finals": vmem((8, width), F32),
            "later": vmem((8, width), F32),
            "factor_ffn": vmem((rows, 128), F32),
            "vector_in": vmem((self.count_vector_slots(), 16, width), F32),
        }
        for name in ("expand", "gate", "output", "key", "value", "recept"):
            shapes["both_" + name] = vmem((2 * rows, width), BF16)
        for name in ("contract", "gate", "output", "key", "value", "recept"):
            shapes["back_" + name] = vmem((2 * rows, half), BF16)
        for index in range(4):
            shapes["rows_" + str(index)] = vmem((rows, width), BF16)
        for name in ("middle", "total", "sigmoid", "num", "den", "unit", "gap"):
            shapes["wide_" + name] = vmem((rows, width), F32)
        copies = 64 + 4 * self.ch
        for index, (name, order, height, breadth) in enumerate(self.pieces):
            axes = [axis for axis in AXES if axis != order[0]]
            lead = tuple(sizes[a] for a in axes)
            shapes["held_" + str(index)] = vmem(
                (sizes[order[0]] - 1,) + lead + (height, breadth), BF16
            )
            axes = list(AXES)
            for stage, axis in enumerate(order):
                axes.remove(axis)
                shape = (sizes[axis] - 1,) + tuple(sizes[a] for a in axes) + (height, breadth)
                shapes["landing_" + str(index) + "_" + str(stage)] = vmem(shape, BF16)
                copies += sizes[axis] - 1
        copies += self.count_vector_slots()
        shapes["sends"] = pltpu.SemaphoreType.DMA((copies,))
        shapes["receives"] = pltpu.SemaphoreType.DMA((copies,))
        shapes["panel_sems"] = pltpu.SemaphoreType.DMA((SLOTS_OF_WEIGHTS,))
        self.shapes = shapes

    def count_vector_slots(self):
        return sum(size - 1 for size in self.sizes.values())


INPUTS = (
    "tokens",
    "grad_out",
    "lengths",
    "init_num",
    "init_den",
    "w_key",
    "w_value",
    "w_recept",
    "w_output",
    "w_expand",
    "w_contract",
    "w_gate",
    "gain_mix",
    "bias_mix",
    "gain_ffn",
    "bias_ffn",
    "mix_key",
    "mix_value",
    "mix_recept",
    "blend_key",
    "blend_gate",
    "time_decay",
    "time_first",
)
OUTPUTS = (
    "mixed_out",
    "grad_tokens",
    "final",
    "grad_key",
    "grad_value",
    "grad_recept",
    "grad_output",
    "grad_expand",
    "grad_contract",
    "grad_gate",
    "vectors",
)
VECTORS = (
    "gain_mix",
    "bias_mix",
    "gain_ffn",
    "bias_ffn",
    "mix_key",
    "mix_value",
    "mix_recept",
    "blend_key",
    "blend_gate",
    "time_decay",
    "time_first",
)


class Panels:
    def __init__(self, sources, ref, sems):
        self.sources, self.ref, self.sems = sources, ref, sems
        self.used = 0
        for index in range(min(SLOTS_OF_WEIGHTS, len(sources))):
            self.copy(index).start()

    def copy(self, index):
        slot = index % SLOTS_OF_WEIGHTS
        return pltpu.make_async_copy(self.sources[index], self.ref.at[slot], self.sems.at[slot])

    def take(self):
        self.copy(self.used).wait()
        return self.ref.at[self.used % SLOTS_OF_WEIGHTS]

    def release(self):
        index = self.used + SLOTS_OF_WEIGHTS
        if index < len(self.sources):
            self.copy(index).start()
        self.used += 1


def layer_kernel(plan, *all_refs):
    inputs = dict(zip(INPUTS, all_refs))
    outputs = dict(zip(OUTPUTS, all_refs[len(INPUTS) :]))
    held = dict(zip(plan.shapes, all_refs[len(INPUTS) + len(OUTPUTS) :]))
    sizes = plan.sizes
    place = coordinates()
    ch_at = lax.axis_index("ch")
    seq_at = lax.axis_index("seq")
    slots, length, width, rows = plan.slots, plan.length, plan.width, plan.rows
    hidden, ch_size = plan.hidden, plan.ch
    panel_count = hidden // width
    tokens, grad_out, lengths = inputs["tokens"], inputs["grad_out"], inputs["lengths"]
    first_rows = slice(0, rows)
    last_rows = slice(rows, 2 * rows)

    w_expand, w_contract = inputs["w_expand"], inputs["w_contract"]

    def expand_panel(index):
        return w_expand.at[:, pl.ds(index * width, width)]

    def contract_panel(index):
        return w_contract.at[pl.ds(index * width, width), :]

    order = [inputs["w_key"], inputs["w_value"], inputs["w_recept"], inputs["w_output"]]
    for index in range(panel_count):
        order += [expand_panel(index), contract_panel(index)]
    order += [inputs["w_gate"]]
    order += [contract_panel(index) for index in range(panel_count)]
    order += [expand_panel(index) for index in range(panel_count)]
    order += [inputs["w_gate"], inputs["w_output"]]
    order += [inputs["w_key"], inputs["w_value"], inputs["w_recept"]]
    panels = Panels(order, held["panels"], held["panel_sems"])

    barrier = pltpu.get_barrier_semaphore()
    greeted = 0
    for step in range(1, ch_size):
        pl.semaphore_signal(
            barrier,
            inc=1,
            device_id=(seq_at, lax.rem(ch_at + step, ch_size)),
            device_id_type=MESH,
        )
        greeted += 1
    for axis in "yz":
        for step in range(1, sizes[axis]):
            there = device_at(moved(place, sizes, axis, step))
            pl.semaphore_signal(barrier, inc=1, device_id=there, device_id_type=MESH)
            greeted += 1
    copies = Copies(held["sends"], held["receives"])
    partner = device_at({**place, "k": 1 - place["k"]})
    after = (seq_at, lax.rem(ch_at + 1, ch_size))
    before = (seq_at, lax.rem(ch_at + ch_size - 1, ch_size))

    filled_here = [
        jnp.clip(lengths[slot] - ch_at * length, 0, length) for slot in range(slots)
    ]
    vectors = outputs["vectors"]
    vectors[...] = jnp.zeros_like(vectors)

    def add_vector(name, value):
        at = VECTORS.index(name)
        vectors[at : at + 1, :] += jnp.sum(value, axis=0, keepdims=True)

    def normalize(value):
        center = value - jnp.mean(value, axis=-1, keepdims=True)
        factor = lax.rsqrt(jnp.mean(center * center, axis=-1, keepdims=True) + EPS)
        return center * factor, factor

    def blend(current, earlier, weights):
        return current * weights + earlier * (1.0 - weights)

    def tiles_of(slot, index):
        return pl.ds(pl.multiple_of(slot * length + index * TILE, TILE), TILE)

    row_in_tile = lax.broadcasted_iota(jnp.int32, (TILE, width), 0)

    def shift_down(value, carry):
        return jnp.where(row_in_tile == 0, carry, pltpu.roll(value, 1, 0))

    def shift_up(value, carry):
        return jnp.where(row_in_tile == TILE - 1, carry, pltpu.roll(value, TILE - 1, 0))

    steps_in_slot = length // TILE

    def matmul(left, panel, how, use, left_columns=None):
        def step(index, carry):
            columns = pl.ds(pl.multiple_of(index * WIDE, WIDE), WIDE)
            right = panel[:, columns] if how is NN else panel[columns, :]
            source = left[...] if left_columns is None else left[:, left_columns]
            use(columns, dot(source, right, how))
            return carry

        lax.fori_loop(0, width // WIDE, step, 0)

    def counts(slot, shape, offset):
        at = lax.broadcasted_iota(jnp.int32, shape, 0) + offset
        earlier = jnp.minimum(at, filled_here[slot]).astype(F32)
        upto = jnp.minimum(at + 1, filled_here[slot]).astype(F32)
        return earlier, upto, at < filled_here[slot]

    def tall_mask(columns):
        at = lax.broadcasted_iota(jnp.int32, (rows, columns), 0)
        inside = at < filled_here[0]
        for slot in range(1, slots):
            shifted = at - slot * length
            inside = inside | ((shifted >= 0) & (shifted < filled_here[slot]))
        return inside

    edges_out, edges_in = held["edges_out"], held["edges_in"]
    edges_out[...] = jnp.zeros_like(edges_out)
    for slot in range(slots):
        last = tokens[slot * length + length - TILE : slot * length + length, :].astype(F32)
        edges_out[0, slot : slot + 1, :] = last[TILE - 1 :, :]
    pl.semaphore_wait(barrier, greeted)
    edge_copy = copies.start(edges_out.at[0], edges_in.at[0], after)

    gain_mix, bias_mix = inputs["gain_mix"], inputs["bias_mix"]
    keep_edge = jnp.where(ch_at > 0, 1.0, 0.0)
    keep_next = jnp.where(ch_at < ch_size - 1, 1.0, 0.0)

    edge_copy.wait()
    edge_unit, _ = normalize(edges_in[0])
    edges_in[0] = (edge_unit * gain_mix[...] + bias_mix[...]) * keep_edge
    mixes = [inputs["mix_key"], inputs["mix_value"], inputs["mix_recept"]]
    both_mix = [held["both_key"], held["both_value"], held["both_recept"]]
    for slot in range(slots):

        def mix_step(index, carry, slot=slot):
            spot = tiles_of(slot, index)
            unit, _ = normalize(tokens[spot, :].astype(F32))
            normed = unit * gain_mix[...] + bias_mix[...]
            earlier = shift_down(normed, carry)
            for weights, target in zip(mixes, both_mix):
                target[spot, :] = blend(normed, earlier, weights[...]).astype(BF16)
            return normed[TILE - 1 :, :]

        lax.fori_loop(0, steps_in_slot, mix_step, edges_in[0, slot : slot + 1, :])
    exchanges = {}
    for name in ("key", "value", "recept"):
        ref = held["both_" + name]
        exchanges[name] = [
            copies.start(ref.at[pl.ds(0, rows), :], ref.at[pl.ds(rows, rows), :], partner)
        ]

    key_ref, value_ref = held["key"], held["value"]
    wide = {
        name: held["wide_" + name]
        for name in ("middle", "total", "sigmoid", "num", "den", "unit", "gap")
    }

    def own(name):
        return held["both_" + name].at[pl.ds(0, rows), :]

    def store_key(columns, product):
        key_ref[:, columns] = product.astype(BF16)

    def store_value(columns, product):
        value_ref[:, columns] = product.astype(BF16)

    matmul(own("key"), panels.take(), NN, store_key)
    panels.release()
    matmul(own("value"), panels.take(), NN, store_value)
    panels.release()

    time_decay, time_first = inputs["time_decay"], inputs["time_first"]
    square = (length, 3 * length)
    at_row = lax.broadcasted_iota(jnp.int32, square, 0)
    at_column = lax.rem(lax.broadcasted_iota(jnp.int32, square, 1), length)
    lower = jnp.where(at_column < at_row, 1.0, 0.0).astype(BF16)
    upper = jnp.where(at_column > at_row, 1.0, 0.0).astype(BF16)

    def triangle(matrix, value):
        high = value.astype(BF16)
        rest = value - high.astype(F32)
        middle = rest.astype(BF16)
        low = (rest - middle.astype(F32)).astype(BF16)
        return dot(matrix, jnp.concatenate([high, middle, low], axis=0), NN)

    sums_out, sums_in = held["sums_out"], held["sums_in"]
    sums_out[...] = jnp.zeros_like(sums_out)
    for slot in range(slots):

        def local_step(index, carry, slot=slot):
            columns = pl.ds(pl.multiple_of(index * WIDE, WIDE), WIDE)
            spot = pl.ds(slot * length, length)
            rate = jnp.exp(time_decay[:, columns])
            earlier, upto, filled = counts(slot, (length, WIDE), 0)
            stop = rate * filled_here[slot].astype(F32)
            keys = key_ref[spot, columns].astype(F32)
            weight = jnp.where(filled, jnp.exp(rate * upto - stop) * jnp.exp(keys), 0.0)
            payload = weight * value_ref[spot, columns].astype(F32)
            raised = jnp.exp(stop - rate * earlier)
            wide["num"][spot, columns] = raised * triangle(lower, payload)
            wide["den"][spot, columns] = raised * triangle(lower, weight)
            sums_out[0, slot : slot + 1, columns] = jnp.sum(payload, axis=0, keepdims=True)
            at = slots + slot
            sums_out[0, at : at + 1, columns] = jnp.sum(weight, axis=0, keepdims=True)
            return carry

        lax.fori_loop(0, width // WIDE, local_step, 0)

    def share(which):
        return [
            copies.start(
                sums_out.at[which],
                sums_in.at[which, step - 1],
                (seq_at, lax.rem(ch_at + step, ch_size)),
            )
            for step in range(1, ch_size)
        ]

    sum_copies = share(0)

    def store_sigmoid(columns, product):
        wide["sigmoid"][:, columns] = jax.nn.sigmoid(product)

    matmul(own("recept"), panels.take(), NN, store_sigmoid)
    panels.release()
    for copy in sum_copies:
        copy.wait()

    rate_row = jnp.exp(time_decay[...])
    states, finals = held["states"], held["finals"]
    states[...] = jnp.zeros_like(states)
    finals[...] = jnp.zeros_like(finals)
    for slot in range(slots):
        size = lengths[slot]
        reached = jnp.minimum(size, ch_at * length)
        for pair, initial in enumerate((inputs["init_num"], inputs["init_den"])):
            at = pair * slots + slot
            start_row = initial[slot : slot + 1, :]
            state = jnp.exp(-rate_row * reached.astype(F32)) * start_row
            final = jnp.exp(-rate_row * size.astype(F32)) * start_row
            for step in range(ch_size):
                source = lax.rem(ch_at + ch_size - step, ch_size)
                done = jnp.minimum(size, (source + 1) * length)
                term = (
                    sums_out[0, at : at + 1, :]
                    if step == 0
                    else sums_in[0, step - 1, at : at + 1, :]
                )
                final = final + jnp.exp(-rate_row * (size - done).astype(F32)) * term
                if step:
                    gone = jnp.maximum(reached - done, 0).astype(F32)
                    state = state + jnp.where(source < ch_at, jnp.exp(-rate_row * gone) * term, 0.0)
            states[at : at + 1, :] = state
            finals[at : at + 1, :] = final
    own_columns = pl.ds(pl.multiple_of(ch_at * plan.narrow, plan.narrow), plan.narrow)
    outputs["final"][...] = finals[:, own_columns]

    both_output = held["both_output"]
    for slot in range(slots):

        def wkv_step(index, carry, slot=slot):
            spot = tiles_of(slot, index)
            earlier, _, _ = counts(slot, (TILE, width), index * TILE)
            faded = jnp.exp(-rate_row * earlier)
            num = wide["num"][spot, :] + faded * states[slot : slot + 1, :]
            den = wide["den"][spot, :] + faded * states[slots + slot : slots + slot + 1, :]
            wide["num"][spot, :] = num
            wide["den"][spot, :] = den
            bonus = jnp.exp(time_first[...] + key_ref[spot, :].astype(F32))
            wkv = (num + bonus * value_ref[spot, :].astype(F32)) / (den + bonus)
            sent = wkv.astype(BF16).astype(F32)
            both_output[spot, :] = (wide["sigmoid"][spot, :] * sent).astype(BF16)
            return carry

        lax.fori_loop(0, steps_in_slot, wkv_step, 0)
    exchanges["output"] = [
        copies.start(
            both_output.at[pl.ds(0, rows), :], both_output.at[pl.ds(rows, rows), :], partner
        )
    ]

    def store_middle(columns, product):
        wide["middle"][:, columns] = tokens[:, columns].astype(F32) + product

    matmul(own("output"), panels.take(), NN, store_middle)
    panels.release()

    gain_ffn, bias_ffn = inputs["gain_ffn"], inputs["bias_ffn"]
    factor_ffn = held["factor_ffn"]
    for slot in range(slots):
        last = wide["middle"][slot * length + length - TILE : slot * length + length, :]
        unit, _ = normalize(last)
        edges_out[1, slot : slot + 1, :] = (unit * gain_ffn[...] + bias_ffn[...])[TILE - 1 :, :]
    edge_copy = copies.start(edges_out.at[1], edges_in.at[1], after)

    def unit_step(index, carry):
        spot = pl.ds(pl.multiple_of(index * TILE, TILE), TILE)
        unit, factor = normalize(wide["middle"][spot, :])
        wide["unit"][spot, :] = unit
        factor_ffn[spot, :] = jnp.broadcast_to(factor, (TILE, 128))
        return carry

    lax.fori_loop(0, rows // TILE, unit_step, 0)
    edge_copy.wait()
    blends = [inputs["blend_key"], inputs["blend_gate"]]
    both_blend = [held["both_expand"], held["both_gate"]]
    for slot in range(slots):

        def blend_step(index, carry, slot=slot):
            spot = tiles_of(slot, index)
            normed = wide["unit"][spot, :] * gain_ffn[...] + bias_ffn[...]
            earlier = shift_down(normed, carry)
            wide["gap"][spot, :] = normed - earlier
            for weights, target in zip(blends, both_blend):
                target[spot, :] = blend(normed, earlier, weights[...]).astype(BF16)
            return normed[TILE - 1 :, :]

        lax.fori_loop(
            0, steps_in_slot, blend_step, edges_in[1, slot : slot + 1, :] * keep_edge
        )
    for name in ("expand", "gate"):
        ref = held["both_" + name]
        exchanges[name] = [
            copies.start(ref.at[pl.ds(0, rows), :], ref.at[pl.ds(rows, rows), :], partner)
        ]

    both_hidden = held["both_hidden"]
    exchanges["hidden"] = []
    for index in range(panel_count):

        def store_hidden(columns, product, index=index):
            positive = jnp.maximum(product, 0.0)
            start = pl.multiple_of(columns.start + index * width, WIDE)
            both_hidden[first_rows, pl.ds(start, WIDE)] = (positive * positive).astype(BF16)

        matmul(own("expand"), panels.take(), NN, store_hidden)
        panels.release()
        part = pl.ds(index * width, width)
        exchanges["hidden"].append(
            copies.start(
                both_hidden.at[pl.ds(0, rows), part],
                both_hidden.at[pl.ds(rows, rows), part],
                partner,
            )
        )

        def add_contracted(columns, product, index=index):
            if index:
                product = product + wide["total"][:, columns]
            wide["total"][:, columns] = product

        matmul(both_hidden.at[pl.ds(0, rows), part], panels.take(), NN, add_contracted)
        panels.release()

    grad_contracted, grad_logit = held["rows_0"], held["rows_1"]

    def finish_forward(columns, product):
        gate = jax.nn.sigmoid(product)
        contracted = wide["total"][:, columns]
        inside = tall_mask(WIDE)
        mixed = wide["middle"][:, columns] + gate * contracted
        outputs["mixed_out"][:, columns] = jnp.where(inside, mixed, 0.0).astype(BF16)
        grad = jnp.where(inside, grad_out[:, columns].astype(F32), 0.0)
        grad_contracted[:, columns] = (grad * gate).astype(BF16)
        grad_logit[:, columns] = (grad * contracted * gate * (1.0 - gate)).astype(BF16)

    matmul(own("gate"), panels.take(), NN, finish_forward)
    panels.release()

    def hand_over(name, source):
        target = held["back_" + name]
        part = plan.narrow
        exchanges["back_" + name] = []
        for x_at in range(sizes["x"]):
            theirs = pl.multiple_of((x_at * 2 + 1 - place["k"]) * part, part)
            mine = pl.multiple_of((x_at * 2 + place["k"]) * part, part)
            spot = pl.ds(x_at * part, part)
            exchanges["back_" + name].append(
                copies.start(
                    source.at[:, pl.ds(theirs, part)],
                    target.at[pl.ds(rows, rows), spot],
                    partner,
                )
            )
            target[first_rows, spot] = source[:, pl.ds(mine, part)]

    def settle(*wanted):
        for name in wanted:
            for copy in exchanges.pop(name):
                copy.wait()

    height = min(256, width)
    owners = height // plan.short

    def emit_owners(emit, tile, value):
        for owner in range(owners):
            part = value[owner * plan.short : (owner + 1) * plan.short, :]
            emit((tile * (owners // 2) + owner // 2, owner % 2), part)

    def square_maker(name, first):
        lefts, rights = held["both_" + name], held["back_" + name]

        def by_x(x_at, emit):
            spot = pl.ds(pl.multiple_of(x_at * plan.narrow, plan.narrow), plan.narrow)

            def step(tile, carry):
                left = lefts[:, pl.ds(pl.multiple_of(tile * height, height), height)]
                emit_owners(emit, tile, dot(left, rights[:, spot], TN))
                return carry

            lax.fori_loop(0, width // height, step, 0)

        def by_z(z_at, emit):
            part = 2 * plan.short
            left = lefts[:, pl.ds(pl.multiple_of(z_at * part, part), part)]
            value = dot(left, rights[...], TN)
            for y_at in range(2):
                for x_at in range(sizes["x"]):
                    emit(
                        (y_at, x_at),
                        value[
                            y_at * plan.short : (y_at + 1) * plan.short,
                            x_at * plan.narrow : (x_at + 1) * plan.narrow,
                        ],
                    )

        return by_x if first == "x" else by_z

    def contract_maker(cut):
        part = plan.tall // plan.contract_cuts

        def make(y_at, emit):
            def step(z_at, carry):
                start = (z_at * 2 + y_at) * plan.tall + cut * part
                left = both_hidden[:, pl.ds(pl.multiple_of(start, part), part)]
                value = dot(left, held["back_contract"][...], TN)
                for x_at in range(sizes["x"]):
                    emit(
                        (z_at, x_at),
                        value[:, x_at * plan.narrow : (x_at + 1) * plan.narrow],
                    )
                return carry

            lax.fori_loop(0, sizes["z"], step, 0)

        return make

    grad_expanded, their_expanded = held["grad_expanded"], held["their_expanded"]

    def expand_maker(cut):
        part = plan.broad // plan.expand_cuts

        def make(x_at, emit):
            mine = pl.ds(
                pl.multiple_of((x_at * 2 + place["k"]) * plan.broad + cut * part, part), part
            )
            theirs = pl.ds(pl.multiple_of(x_at * plan.broad + cut * part, part), part)

            def step(tile, carry):
                spot = pl.ds(pl.multiple_of(tile * height, height), height)
                left = held["both_expand"]
                value = dot(left[first_rows, spot], grad_expanded[:, mine], TN)
                value = value + dot(left[last_rows, spot], their_expanded[:, theirs], TN)
                emit_owners(emit, tile, value)
                return carry

            lax.fori_loop(0, width // height, step, 0)

        return make

    pieces = {}
    seen = {}
    for index, (name, order_of, tall, broad) in enumerate(plan.pieces):
        cut = seen.get(name, 0)
        seen[name] = cut + 1
        out_ref = outputs["grad_" + name]
        if name == "contract":
            make = contract_maker(cut)
            out_ref = out_ref.at[pl.ds(cut * tall, tall), :]
        elif name == "expand":
            make = expand_maker(cut)
            out_ref = out_ref.at[:, pl.ds(cut * broad, broad)]
        else:
            make = square_maker(name, order_of[0])
        landings = [
            held["landing_" + str(index) + "_" + str(stage)] for stage in range(len(order_of))
        ]
        pieces[name + str(cut)] = Piece(
            make, order_of, sizes, place, copies, held["held_" + str(index)], landings, out_ref
        )
    contract_names = ["contract" + str(cut) for cut in range(plan.contract_cuts)]
    expand_names = ["expand" + str(cut) for cut in range(plan.expand_cuts)]

    hand_over("contract", grad_contracted)
    hand_over("gate", grad_logit)
    settle("hidden", "back_contract")
    for name in contract_names:
        pieces[name].start()

    for index in range(panel_count):

        def store_expanded(columns, product, index=index):
            start = pl.multiple_of(columns.start + index * width, WIDE)
            spot = pl.ds(start, WIDE)
            positive = jnp.sqrt(both_hidden[first_rows, spot].astype(F32))
            grad_expanded[:, spot] = (product * 2.0 * positive).astype(BF16)

        matmul(grad_contracted, panels.take(), NT, store_expanded)
        panels.release()
    exchanges["expanded"] = []
    for x_at in range(sizes["x"]):
        theirs = pl.multiple_of((x_at * 2 + 1 - place["k"]) * plan.broad, plan.broad)
        exchanges["expanded"].append(
            copies.start(
                grad_expanded.at[:, pl.ds(theirs, plan.broad)],
                their_expanded.at[:, pl.ds(x_at * plan.broad, plan.broad)],
                partner,
            )
        )
    for index in range(panel_count):

        def add_expand(columns, product, index=index):
            if index:
                product = product + wide["total"][:, columns]
            wide["total"][:, columns] = product

        matmul(
            grad_expanded,
            panels.take(),
            NT,
            add_expand,
            left_columns=pl.ds(index * width, width),
        )
        panels.release()

    def store_gate(columns, product):
        wide["middle"][:, columns] = product

    matmul(grad_logit, panels.take(), NT, store_gate)
    panels.release()

    for slot in range(slots):
        spot = slice(slot * length, slot * length + TILE)
        edge = wide["total"][spot, :] * (1.0 - blends[0][...])
        edge = edge + wide["middle"][spot, :] * (1.0 - blends[1][...])
        edges_out[2, slot : slot + 1, :] = edge[:1, :]
    edge_copy = copies.start(edges_out.at[2], edges_in.at[2], before)
    settle("expand", "expanded")
    for name in expand_names:
        pieces[name].start()
    settle("gate", "back_gate")
    pieces["gate0"].start()
    edge_copy.wait()

    grad_branch = held["rows_2"]
    for slot in range(slots):

        def ffn_back_step(index, carry, slot=slot):
            spot = tiles_of(slot, steps_in_slot - 1 - index)
            at = (steps_in_slot - 1 - index) * TILE
            in_expand, in_gate = wide["total"][spot, :], wide["middle"][spot, :]
            gap = wide["gap"][spot, :]
            unit = wide["unit"][spot, :]
            add_vector("blend_key", in_expand * gap)
            add_vector("blend_gate", in_gate * gap)
            weight_key, weight_gate = blends[0][...], blends[1][...]
            earlier = in_expand * (1.0 - weight_key) + in_gate * (1.0 - weight_gate)
            grad_normed = (
                in_expand * weight_key + in_gate * weight_gate + shift_up(earlier, carry)
            )
            add_vector("gain_ffn", grad_normed * unit)
            add_vector("bias_ffn", grad_normed)
            scaled = grad_normed * gain_ffn[...]
            centered = scaled - jnp.mean(scaled, axis=-1, keepdims=True)
            centered = centered - unit * jnp.mean(scaled * unit, axis=-1, keepdims=True)
            _, _, filled = counts(slot, (TILE, width), at)
            grad = jnp.where(filled, grad_out[spot, :].astype(F32), 0.0)
            grad = grad + factor_ffn[spot, :1] * centered
            wide["total"][spot, :] = grad
            grad_branch[spot, :] = grad.astype(BF16)
            return earlier[:1, :]

        lax.fori_loop(
            0, steps_in_slot, ffn_back_step, edges_in[2, slot : slot + 1, :] * keep_next
        )

    hand_over("output", grad_branch)
    grad_recept = held["rows_3"]

    def gated_back(columns, product):
        gate = wide["sigmoid"][:, columns]
        bonus = jnp.exp(time_first[:, columns] + key_ref[:, columns].astype(F32))
        norm = wide["den"][:, columns] + bonus
        wkv = (wide["num"][:, columns] + bonus * value_ref[:, columns].astype(F32)) / norm
        sent = wkv.astype(BF16).astype(F32)
        grad_wkv = (product * gate).astype(BF16).astype(F32)
        grad_recept[:, columns] = (product * sent * gate * (1.0 - gate)).astype(BF16)
        upper_part = grad_wkv / norm
        wide["middle"][:, columns] = upper_part
        wide["gap"][:, columns] = -upper_part * wkv

    matmul(grad_branch, panels.take(), NT, gated_back)
    panels.release()

    for slot in range(slots):

        def adjoint_step(index, carry, slot=slot):
            columns = pl.ds(pl.multiple_of(index * WIDE, WIDE), WIDE)
            spot = pl.ds(slot * length, length)
            rate = jnp.exp(time_decay[:, columns])
            earlier, upto, _ = counts(slot, (length, WIDE), 0)
            faded = jnp.exp(-rate * earlier)
            raised = jnp.exp(rate * upto)
            for pair, (source, target) in enumerate((("middle", "sigmoid"), ("gap", "unit"))):
                terms = faded * wide[source][spot, columns]
                wide[target][spot, columns] = raised * triangle(upper, terms)
                at = pair * slots + slot
                sums_out[1, at : at + 1, columns] = jnp.sum(terms, axis=0, keepdims=True)
            return carry

        lax.fori_loop(0, width // WIDE, adjoint_step, 0)
    sum_copies = share(1)
    settle("output", "back_output")
    pieces["output0"].start()
    for copy in sum_copies:
        copy.wait()
    later = held["later"]
    later[...] = jnp.zeros_like(later)
    for slot in range(slots):
        size = lengths[slot]
        done = jnp.minimum(size, (ch_at + 1) * length)
        for pair in range(2):
            at = pair * slots + slot
            total = jnp.zeros((1, width), F32)
            for step in range(1, ch_size):
                source = lax.rem(ch_at + ch_size - step, ch_size)
                reached = jnp.minimum(size, source * length)
                gone = jnp.maximum(reached - done, 0).astype(F32)
                term = sums_in[1, step - 1, at : at + 1, :]
                total = total + jnp.where(source > ch_at, jnp.exp(-rate_row * gone) * term, 0.0)
            later[at : at + 1, :] = total

    grad_key, grad_value = held["rows_0"], held["rows_1"]
    for slot in range(slots):

        def wkv_back_step(index, carry, slot=slot):
            spot = tiles_of(slot, index)
            _, upto, filled = counts(slot, (TILE, width), index * TILE)
            left = filled_here[slot].astype(F32) - upto
            faded = jnp.exp(-rate_row * left)
            adj_num = wide["sigmoid"][spot, :] + faded * later[slot : slot + 1, :]
            adj_den = wide["unit"][spot, :] + faded * later[slots + slot : slots + slot + 1, :]
            keys, values = key_ref[spot, :].astype(F32), value_ref[spot, :].astype(F32)
            bonus = jnp.exp(time_first[...] + keys)
            weight = jnp.where(filled, jnp.exp(keys), 0.0)
            upper_part, lower_part = wide["middle"][spot, :], wide["gap"][spot, :]
            direct = (upper_part * values + lower_part) * bonus
            grad_value[spot, :] = (upper_part * bonus + weight * adj_num).astype(BF16)
            grad_key[spot, :] = (direct + weight * (adj_num * values + adj_den)).astype(BF16)
            add_vector("time_first", direct)
            decay = adj_num * wide["num"][spot, :] + adj_den * wide["den"][spot, :]
            add_vector("time_decay", jnp.where(filled, decay, 0.0))
            return carry

        lax.fori_loop(0, steps_in_slot, wkv_back_step, 0)
    decay_at = VECTORS.index("time_decay")
    vectors[decay_at : decay_at + 1, :] *= -rate_row * jnp.exp(-rate_row)

    hand_over("key", grad_key)
    hand_over("value", grad_value)
    hand_over("recept", grad_recept)

    def keeper(name):
        def keep(columns, product):
            wide[name][:, columns] = product

        return keep

    for source, name in ((grad_key, "sigmoid"), (grad_value, "unit"), (grad_recept, "gap")):
        matmul(source, panels.take(), NT, keeper(name))
        panels.release()
    in_names = ("sigmoid", "unit", "gap")
    for slot in range(slots):
        spot = slice(slot * length, slot * length + TILE)
        edge = jnp.zeros((TILE, width), F32)
        for name, weights in zip(in_names, mixes):
            edge = edge + wide[name][spot, :] * (1.0 - weights[...])
        edges_out[3, slot : slot + 1, :] = edge[:1, :]
    edge_copy = copies.start(edges_out.at[3], edges_in.at[3], before)
    for name in ("key", "value", "recept"):
        settle(name, "back_" + name)
        pieces[name + "0"].start()

    for slot in range(slots):

        def again_step(index, carry, slot=slot):
            spot = tiles_of(slot, index)
            unit, _ = normalize(tokens[spot, :].astype(F32))
            normed = unit * gain_mix[...] + bias_mix[...]
            wide["num"][spot, :] = unit
            wide["den"][spot, :] = normed - shift_down(normed, carry)
            return normed[TILE - 1 :, :]

        lax.fori_loop(0, steps_in_slot, again_step, edges_in[0, slot : slot + 1, :])
    edge_copy.wait()
    vector_names = ("mix_key", "mix_value", "mix_recept")
    for slot in range(slots):

        def mix_back_step(index, carry, slot=slot):
            spot = tiles_of(slot, steps_in_slot - 1 - index)
            _, factor = normalize(tokens[spot, :].astype(F32))
            unit, gap = wide["num"][spot, :], wide["den"][spot, :]
            earlier = jnp.zeros((TILE, width), F32)
            grad_normed = jnp.zeros((TILE, width), F32)
            for name, weights, vector in zip(in_names, mixes, vector_names):
                grad = wide[name][spot, :]
                add_vector(vector, grad * gap)
                earlier = earlier + grad * (1.0 - weights[...])
                grad_normed = grad_normed + grad * weights[...]
            grad_normed = grad_normed + shift_up(earlier, carry)
            add_vector("gain_mix", grad_normed * unit)
            add_vector("bias_mix", grad_normed)
            scaled = grad_normed * gain_mix[...]
            centered = scaled - jnp.mean(scaled, axis=-1, keepdims=True)
            centered = centered - unit * jnp.mean(scaled * unit, axis=-1, keepdims=True)
            grad = wide["total"][spot, :] + factor * centered
            outputs["grad_tokens"][spot, :] = grad.astype(BF16)
            return earlier[:1, :]

        lax.fori_loop(
            0, steps_in_slot, mix_back_step, edges_in[3, slot : slot + 1, :] * keep_next
        )

    vector_in = held["vector_in"]
    vector_slot = 0

    def start_vectors(axis):
        nonlocal vector_slot
        found = []
        for step in range(1, sizes[axis]):
            there = device_at(moved(place, sizes, axis, step))
            found.append(copies.start(vectors, vector_in.at[vector_slot], there))
            vector_slot += 1
        return found

    def finish_vectors(found):
        for copy in found:
            copy.wait()
        for at in range(vector_slot - len(found), vector_slot):
            vectors[...] += vector_in[at]

    squares = ["gate0", "output0", "key0", "value0", "recept0"]
    rounds = contract_names[:1] + expand_names[:1] + ["gate0"]
    rounds += contract_names[1:] + expand_names[1:]
    rounds += ["output0", "key0", "value0", "recept0"]
    for turn in range(3):
        axis = "kxy"[turn]
        found = start_vectors(axis)
        for name in rounds:
            pieces[name].advance()
        finish_vectors(found)
    finish_vectors(start_vectors("z"))


def body(*arguments):
    values = dict(zip(INPUTS, arguments))
    plan = Plan(values["tokens"], values["w_expand"])
    rows, width = plan.rows, plan.width
    operands, specs = [], []
    for name in INPUTS:
        value = values[name]
        space = pltpu.VMEM
        if name in ("tokens", "grad_out"):
            value = value.reshape(rows, width)
        elif name == "lengths":
            space = pltpu.SMEM
        elif name.startswith("w_"):
            space = pl.ANY
        elif value.ndim == 1:
            value = value.reshape(1, width)
        operands.append(value)
        specs.append(pl.BlockSpec(memory_space=space))
    outs = {
        "mixed_out": ((rows, width), BF16),
        "grad_tokens": ((rows, width), BF16),
        "final": ((8, plan.narrow), F32),
        "grad_key": ((plan.short, plan.narrow), F32),
        "grad_value": ((plan.short, plan.narrow), F32),
        "grad_recept": ((plan.short, plan.narrow), F32),
        "grad_output": ((plan.short, plan.narrow), F32),
        "grad_expand": ((plan.short, plan.broad), F32),
        "grad_contract": ((plan.tall, plan.narrow), F32),
        "grad_gate": ((plan.short, plan.narrow), F32),
        "vectors": ((16, width), F32),
    }
    results = pl.pallas_call(
        functools.partial(layer_kernel, plan),
        out_shape=[jax.ShapeDtypeStruct(*outs[name]) for name in OUTPUTS],
        in_specs=specs,
        out_specs=[pl.BlockSpec(memory_space=pltpu.VMEM)] * len(OUTPUTS),
        scratch_shapes=list(plan.shapes.values()),
        compiler_params=pltpu.CompilerParams(
            collective_id=0, has_side_effects=True, vmem_limit_bytes=62 * 2**20
        ),
    )(*operands)
    got = dict(zip(OUTPUTS, results))
    shape = values["tokens"].shape
    part = width // (plan.seq * plan.ch)
    at = (lax.axis_index("seq") * plan.ch + lax.axis_index("ch")) * part
    vectors = lax.dynamic_slice_in_dim(got["vectors"], at, part, 1)
    slots = plan.slots
    return (
        got["mixed_out"].reshape(shape),
        got["grad_tokens"].reshape(shape),
        got["final"][:slots],
        got["final"][slots : 2 * slots],
        got["grad_key"],
        got["grad_value"],
        got["grad_recept"],
        got["grad_output"],
        got["grad_expand"],
        got["grad_contract"],
        got["grad_gate"],
    ) + tuple(vectors[index] for index in range(len(VECTORS)))


def solution(mesh):
    split, copied = P("seq", "ch", None), P()
    placed = (split, split, P("seq"), P("seq", None), P("seq", None)) + (copied,) * 18
    both = P("seq", "ch")
    return jax.shard_map(
        body,
        mesh=mesh,
        in_specs=placed,
        out_specs=(split, split) + (both,) * 9 + (P(("seq", "ch")),) * 11,
        check_vma=False,
    )
```

time: 950 us -> 234 us (0.25); the launches traced: 940 us -> 234 us
  waiting for transfers between devices: 634 us -> 0 us
  Pallas kernels: 0 us -> 221 us
  matrix products: 87.9 us -> 0 us
  blocking collectives: 63.4 us -> 0 us
  other arithmetic: 57.3 us -> 0 us
  local copies, waits for them, and re-layouts: 56.3 us -> 11.7 us
  starting transfers between devices: 23.9 us -> 0 us
  between operations: 17 us -> 0.73 us
    reduce_scatter x14 -> x0, waiting for transfers between devices: 610 us -> none  [the longest x1 145 us: body(): lax.psum_scatter(grad_w_contract.astype(jnp.bfloat16), 'seq', scatter_dim...]
    pallas_call x0 -> x1, Pallas kernels: none -> 221 us  [body(): pl.pallas_call(functools.partial(layer_kernel, plan), out_shape=[jax.Shap...]
    dot_general x25 -> x0, matrix products: 87.9 us -> none  [the longest x7 25.8 us: outer_sum(): lax.dot_general(rows_in.reshape(-1, rows_in.shape[-1]), grad_in.reshape(-...]
    unnamed x2 -> x0, blocking collectives: 40.9 us -> none
    convert_element_type x29 -> x0, other arithmetic: 25.1 us -> none  [the longest x18 17.5 us: body(): all_sums = (lax.psum_scatter(row_sums[0].astype(jnp.bfloat16), 'ch', scat...]
    all_to_all x2 -> x0, blocking collectives: 22.5 us -> none  [the longest x1 11.2 us: body(): lax.all_to_all(grad_key_cols.astype(NARROW_TYPE), 'ch', split_axis=1, con...]
    all_to_all x4 -> x0, waiting for transfers between devices: 20.9 us -> none  [the longest x1 8.72 us: body(): lax.all_to_all(wkv_cols.astype(NARROW_TYPE), 'ch', split_axis=1, concat_a...]
    all_to_all x4 -> x0, starting transfers between devices: 16.2 us -> none  [the longest x1 4.49 us: body(): lax.all_to_all(grad_wkv, 'ch', split_axis=2, concat_axis=1, tiled=True)]
  transfers between devices with their start and end apart: 22 -> 0, of which waited for: 17 -> 0; matrix products, arithmetic and copies ran while one was open for 14% -> 0% of each run, Pallas kernels for 0% -> 0%
where the time goes in v2:
time: 234 us
  Pallas kernels  221 us (94%)
  local copies, waits for them, and re-layouts  11.7 us (5%)
    pallas_call x1, Pallas kernels, body(): pl.pallas_call(functools.partial(layer_kernel, plan), out_shape=[jax.Shap...  221 us
    unnamed x23, local copies, waits for them, and re-layouts  8.72 us

profile of v2, /device:TPU:0, one launch (start us, length us, event | category | flops | bytes accessed | tf_op | source)
XLA Modules:
  0.0 233.8 jit_solution(10246097686623486313)
XLA Ops:
  0.7 221.4 %shard_map.390 = (bf16[256,1024]{1,0:T(8,128)(2,1)}, bf16[256,1024]{1,0:T(8,128)(2,1)}, f32[8,256]{1,0:T(8,128)}, f32[128,256]{1,0:T(8,128)}, f32[128,256]{1,0:T...) custom-call(bf16[256,1024]{1,0:T(8,128)(2,1)} %bitcast.37, ...), custom_call_target="tpu_custom_call" | custom-call | tf_op jit(solution)/shard_map/pallas_call | solution.py:1092
  222.1 0.0 copy-start.6
  222.1 0.0 copy-start.5
  222.1 0.0 copy-start.4
  222.1 0.0 copy-start.3
  222.1 0.0 copy-start.1
  222.1 1.6 dynamic-slice_bitcast_fusion
  223.8 1.4 fusion
  225.1 0.0 copy-start
  225.1 1.9 copy.54
  227.0 0.0 copy-start.2
  227.0 1.9 copy.55
  228.9 0.0 copy-done.6
  228.9 0.7 copy.56
  229.6 0.0 copy-done.5
  229.6 0.7 copy.57
  230.3 0.0 copy-done.4
  230.3 0.7 copy.58
  230.9 0.0 copy-done.3
  230.9 0.7 copy.59
  231.6 0.0 copy-done.1
  231.6 0.8 copy.60
  232.4 0.0 copy-done
  232.4 0.8 copy.61
  233.2 0.0 copy-done.2
  233.2 0.7 copy.62
Async XLA Ops:
  222.1 6.9 %copy-start.6 = (f32[128,256]{1,0:T(8,128)S(1)}, f32[128,256]{1,0:T(8,128)}, u32[]{:S(2)}) copy-start(f32[128,256]{1,0:T(8,128)} %get-tuple-element.83) | copy-start | bytes 393220
  222.1 7.5 %copy-start.5 = (f32[128,256]{1,0:T(8,128)S(1)}, f32[128,256]{1,0:T(8,128)}, u32[]{:S(2)}) copy-start(f32[128,256]{1,0:T(8,128)} %get-tuple-element.84) | copy-start | bytes 393220
  222.1 8.2 %copy-start.4 = (f32[128,256]{1,0:T(8,128)S(1)}, f32[128,256]{1,0:T(8,128)}, u32[]{:S(2)}) copy-start(f32[128,256]{1,0:T(8,128)} %get-tuple-element.85) | copy-start | bytes 393220
  222.1 8.8 %copy-start.3 = (f32[128,256]{1,0:T(8,128)S(1)}, f32[128,256]{1,0:T(8,128)}, u32[]{:S(2)}) copy-start(f32[128,256]{1,0:T(8,128)} %get-tuple-element.86) | copy-start | bytes 393220
  222.1 9.5 %copy-start.1 = (f32[128,1024]{1,0:T(8,128)S(1)}, f32[128,1024]{1,0:T(8,128)}, u32[]{:S(2)}) copy-start(f32[128,1024]{1,0:T(8,128)} %get-tuple-element.87) | copy-start | bytes 1572868
  225.1 7.3 %copy-start = (f32[512,256]{1,0:T(8,128)S(1)}, f32[512,256]{1,0:T(8,128)}, u32[]{:S(2)}) copy-start(f32[512,256]{1,0:T(8,128)} %get-tuple-element.88) | copy-start | bytes 1572868
  227.0 6.1 %copy-start.2 = (f32[128,256]{1,0:T(8,128)S(1)}, f32[128,256]{1,0:T(8,128)}, u32[]{:S(2)}) copy-start(f32[128,256]{1,0:T(8,128)} %get-tuple-element.89) | copy-start | bytes 393220

commit v3 on v2

--- a/solution.py
+++ b/solution.py
@@ -10,12 +10,36 @@
 
 EPS = 1e-05
 MESH = pl.DeviceIdType.MESH
-AXES = "zyx"
+AXES = "hlyx"
 F32 = jnp.float32
 BF16 = jnp.bfloat16
-TILE = 16
+TILE = 64
 WIDE = 256
 SLOTS_OF_WEIGHTS = 3
+
+ORDERS = {
+    "c0": "xylh",
+    "c1": "yxlh",
+    "c2": "lxyh",
+    "c3": "yxlh",
+    "e0": "xylh",
+    "e1": "yxlh",
+    "e2": "lyxh",
+    "e3": "lxyh",
+    "g": "lyxh",
+    "o": "xylh",
+    "k": "yxlh",
+    "v": "xylh",
+    "r": "yxlh",
+}
+PUMPS = (
+    (),
+    ("c0", "c1", "c2"),
+    ("c3", "e0", "e2"),
+    ("g", "c0", "c1", "c2"),
+    (),
+    ("e1", "e3", "o", "c3", "c0", "c1", "c2"),
+)
 
 NN = (((1,), (0,)), ((), ()))
 NT = (((1,), (1,)), ((), ()))
@@ -28,16 +52,22 @@
 
 def axis_sizes():
     seq_size, ch_size = lax.axis_size("seq"), lax.axis_size("ch")
-    return {"k": 2, "x": ch_size // 2, "y": 2, "z": seq_size // 2}
+    return {"k": 2, "x": ch_size // 2, "y": 2, "l": 2, "h": seq_size // 4}
 
 
 def coordinates():
     seq_at, ch_at = lax.axis_index("seq"), lax.axis_index("ch")
-    return {"z": seq_at // 2, "y": seq_at % 2, "x": ch_at // 2, "k": ch_at % 2}
+    return {
+        "h": seq_at // 4,
+        "l": seq_at // 2 % 2,
+        "y": seq_at % 2,
+        "x": ch_at // 2,
+        "k": ch_at % 2,
+    }
 
 
 def device_at(place):
-    return (place["z"] * 2 + place["y"], place["x"] * 2 + place["k"])
+    return (place["h"] * 4 + place["l"] * 2 + place["y"], place["x"] * 2 + place["k"])
 
 
 def moved(place, sizes, axis, step):
@@ -151,7 +181,7 @@
         self.slots, self.length, self.width = tokens.shape
         self.hidden = w_expand.shape[1]
         self.sizes = sizes = axis_sizes()
-        self.seq, self.ch = sizes["z"] * 2, sizes["x"] * 2
+        self.seq, self.ch = sizes["h"] * 4, sizes["x"] * 2
         self.rows = self.slots * self.length
         rows, width, hidden = self.rows, self.width, self.hidden
         self.narrow = width // self.ch
@@ -160,23 +190,19 @@
         self.tall = hidden // self.seq
         half = sizes["x"] * self.narrow
         self.pieces = []
-        cuts = 2 if (self.tall // 2) % 128 == 0 else 1
-        self.contract_cuts = cuts
-        for _ in range(cuts):
-            self.pieces.append(("contract", "yxz", self.tall // cuts, self.narrow))
-        cuts = 2 if (self.broad // 2) % 128 == 0 else 1
-        self.expand_cuts = cuts
-        for _ in range(cuts):
-            self.pieces.append(("expand", "xyz", self.short, self.broad // cuts))
-        first_z = "zxy" if (2 * self.short) % 128 == 0 else "xyz"
-        for name, order in (
-            ("gate", first_z),
-            ("output", "xyz"),
-            ("key", first_z),
-            ("value", "xyz"),
-            ("recept", "xyz"),
-        ):
-            self.pieces.append((name, order, self.short, self.narrow))
+        cuts = 4 if (self.tall // 4) % 128 == 0 else 1
+        part = self.tall // cuts
+        for cut in range(cuts):
+            self.pieces.append(("contract", "c" + str(cut), part, cut * part, self.narrow, 0))
+        cuts = 4 if (self.broad // 4) % 128 == 0 else 1
+        part = self.broad // cuts
+        for cut in range(cuts):
+            self.pieces.append(("expand", "e" + str(cut), self.short, 0, part, cut * part))
+        for name in ("gate", "output", "key", "value", "recept"):
+            self.pieces.append((name, name[0], self.short, 0, self.narrow, 0))
+        self.orders = {
+            piece[1]: ORDERS[piece[1]] if piece[2] % 128 == 0 else "xylh" for piece in self.pieces
+        }
         vmem = pltpu.VMEM
         shapes = {
             "panels": vmem((SLOTS_OF_WEIGHTS, width, width), BF16),
@@ -204,17 +230,18 @@
         for name in ("middle", "total", "sigmoid", "num", "den", "unit", "gap"):
             shapes["wide_" + name] = vmem((rows, width), F32)
         copies = 64 + 4 * self.ch
-        for index, (name, order, height, breadth) in enumerate(self.pieces):
+        for name, short_name, height, _, breadth, _ in self.pieces:
+            order = self.orders[short_name]
             axes = [axis for axis in AXES if axis != order[0]]
             lead = tuple(sizes[a] for a in axes)
-            shapes["held_" + str(index)] = vmem(
+            shapes["held_" + short_name] = vmem(
                 (sizes[order[0]] - 1,) + lead + (height, breadth), BF16
             )
             axes = list(AXES)
             for stage, axis in enumerate(order):
                 axes.remove(axis)
                 shape = (sizes[axis] - 1,) + tuple(sizes[a] for a in axes) + (height, breadth)
-                shapes["landing_" + str(index) + "_" + str(stage)] = vmem(shape, BF16)
+                shapes["landing_" + short_name + str(stage)] = vmem(shape, BF16)
                 copies += sizes[axis] - 1
         copies += self.count_vector_slots()
         shapes["sends"] = pltpu.SemaphoreType.DMA((copies,))
@@ -344,7 +371,7 @@
             device_id_type=MESH,
         )
         greeted += 1
-    for axis in "yz":
+    for axis in "ylh":
         for step in range(1, sizes[axis]):
             there = device_at(moved(place, sizes, axis, step))
             pl.semaphore_signal(barrier, inc=1, device_id=there, device_id_type=MESH)
@@ -685,113 +712,98 @@
             for copy in exchanges.pop(name):
                 copy.wait()
 
-    height = min(256, width)
-    owners = height // plan.short
-
-    def emit_owners(emit, tile, value):
-        for owner in range(owners):
-            part = value[owner * plan.short : (owner + 1) * plan.short, :]
-            emit((tile * (owners // 2) + owner // 2, owner % 2), part)
-
-    def square_maker(name, first):
-        lefts, rights = held["both_" + name], held["back_" + name]
-
-        def by_x(x_at, emit):
-            spot = pl.ds(pl.multiple_of(x_at * plan.narrow, plan.narrow), plan.narrow)
-
-            def step(tile, carry):
-                left = lefts[:, pl.ds(pl.multiple_of(tile * height, height), height)]
-                emit_owners(emit, tile, dot(left, rights[:, spot], TN))
+    grad_expanded, their_expanded = held["grad_expanded"], held["their_expanded"]
+
+    def maker(piece):
+        name, short_name, height, row_cut, breadth, column_cut = piece
+        first = plan.orders[short_name][0]
+        left = held["both_" + ("hidden" if name == "contract" else name)]
+        row_step = plan.tall if name == "contract" else plan.short
+        if name == "expand":
+            rights = (
+                (
+                    first_rows,
+                    grad_expanded,
+                    lambda at: (at * 2 + place["k"]) * plan.broad + column_cut,
+                ),
+                (last_rows, their_expanded, lambda at: at * plan.broad + column_cut),
+            )
+        else:
+            rights = ((slice(None), held["back_" + name], lambda at: at * plan.narrow),)
+
+        def along(axis, coordinate):
+            return [coordinate] if axis == first else range(sizes[axis])
+
+        def make(coordinate, emit):
+            places = [(l, y) for l in along("l", coordinate) for y in along("y", coordinate)]
+            columns = along("x", coordinate)
+
+            def step(h, carry):
+                starts = [((h * 2 + l) * 2 + y) * row_step + row_cut for l, y in places]
+                spans = [(start, height) for start in starts]
+                if row_step == height and first in "xl":
+                    spans = [(starts[0], len(starts) * height)]
+                value = None
+                for part, right, column_of in rights:
+                    a = [
+                        left[part, pl.ds(pl.multiple_of(start, math.gcd(span, 512)), span)]
+                        for start, span in spans
+                    ]
+                    b = [
+                        right[:, pl.ds(pl.multiple_of(column_of(x), breadth), breadth)]
+                        for x in columns
+                    ]
+                    a = jnp.concatenate(a, axis=1) if len(a) > 1 else a[0]
+                    b = jnp.concatenate(b, axis=1) if len(b) > 1 else b[0]
+                    product = dot(a, b, TN)
+                    value = product if value is None else value + product
+                for index, (l, y) in enumerate(places):
+                    rows_of = value[index * height : (index + 1) * height, :]
+                    for x in columns:
+                        at = 0 if first == "x" else x
+                        block = rows_of[:, at * breadth : (at + 1) * breadth]
+                        where = {"h": h, "l": l, "y": y, "x": x}
+                        emit(tuple(where[a] for a in AXES if a != first), block)
                 return carry
 
-            lax.fori_loop(0, width // height, step, 0)
-
-        def by_z(z_at, emit):
-            part = 2 * plan.short
-            left = lefts[:, pl.ds(pl.multiple_of(z_at * part, part), part)]
-            value = dot(left, rights[...], TN)
-            for y_at in range(2):
-                for x_at in range(sizes["x"]):
-                    emit(
-                        (y_at, x_at),
-                        value[
-                            y_at * plan.short : (y_at + 1) * plan.short,
-                            x_at * plan.narrow : (x_at + 1) * plan.narrow,
-                        ],
-                    )
-
-        return by_x if first == "x" else by_z
-
-    def contract_maker(cut):
-        part = plan.tall // plan.contract_cuts
-
-        def make(y_at, emit):
-            def step(z_at, carry):
-                start = (z_at * 2 + y_at) * plan.tall + cut * part
-                left = both_hidden[:, pl.ds(pl.multiple_of(start, part), part)]
-                value = dot(left, held["back_contract"][...], TN)
-                for x_at in range(sizes["x"]):
-                    emit(
-                        (z_at, x_at),
-                        value[:, x_at * plan.narrow : (x_at + 1) * plan.narrow],
-                    )
-                return carry
-
-            lax.fori_loop(0, sizes["z"], step, 0)
+            lax.fori_loop(0, sizes["h"], step, 0)
 
         return make
 
-    grad_expanded, their_expanded = held["grad_expanded"], held["their_expanded"]
-
-    def expand_maker(cut):
-        part = plan.broad // plan.expand_cuts
-
-        def make(x_at, emit):
-            mine = pl.ds(
-                pl.multiple_of((x_at * 2 + place["k"]) * plan.broad + cut * part, part), part
-            )
-            theirs = pl.ds(pl.multiple_of(x_at * plan.broad + cut * part, part), part)
-
-            def step(tile, carry):
-                spot = pl.ds(pl.multiple_of(tile * height, height), height)
-                left = held["both_expand"]
-                value = dot(left[first_rows, spot], grad_expanded[:, mine], TN)
-                value = value + dot(left[last_rows, spot], their_expanded[:, theirs], TN)
-                emit_owners(emit, tile, value)
-                return carry
-
-            lax.fori_loop(0, width // height, step, 0)
-
-        return make
-
     pieces = {}
-    seen = {}
-    for index, (name, order_of, tall, broad) in enumerate(plan.pieces):
-        cut = seen.get(name, 0)
-        seen[name] = cut + 1
-        out_ref = outputs["grad_" + name]
-        if name == "contract":
-            make = contract_maker(cut)
-            out_ref = out_ref.at[pl.ds(cut * tall, tall), :]
-        elif name == "expand":
-            make = expand_maker(cut)
-            out_ref = out_ref.at[:, pl.ds(cut * broad, broad)]
-        else:
-            make = square_maker(name, order_of[0])
-        landings = [
-            held["landing_" + str(index) + "_" + str(stage)] for stage in range(len(order_of))
+    for piece in plan.pieces:
+        name, short_name, height, row_cut, breadth, column_cut = piece
+        order_of = plan.orders[short_name]
+        out_ref = outputs["grad_" + name].at[
+            pl.ds(row_cut, height), pl.ds(column_cut, breadth)
         ]
-        pieces[name + str(cut)] = Piece(
-            make, order_of, sizes, place, copies, held["held_" + str(index)], landings, out_ref
+        landings = [held["landing_" + short_name + str(stage)] for stage in range(len(order_of))]
+        pieces[short_name] = Piece(
+            maker(piece),
+            order_of,
+            sizes,
+            place,
+            copies,
+            held["held_" + short_name],
+            landings,
+            out_ref,
         )
-    contract_names = ["contract" + str(cut) for cut in range(plan.contract_cuts)]
-    expand_names = ["expand" + str(cut) for cut in range(plan.expand_cuts)]
+
+    def start_pieces(prefix):
+        for short_name, piece in pieces.items():
+            if short_name.startswith(prefix):
+                piece.start()
+
+    def pump(point):
+        for short_name in PUMPS[point]:
+            piece = pieces.get(short_name)
+            if piece is not None and piece.copies:
+                piece.advance()
 
     hand_over("contract", grad_contracted)
     hand_over("gate", grad_logit)
     settle("hidden", "back_contract")
-    for name in contract_names:
-        pieces[name].start()
+    start_pieces("c")
 
     for index in range(panel_count):
 
@@ -829,6 +841,9 @@
         )
         panels.release()
 
+    settle("expand", "expanded")
+    start_pieces("e")
+
     def store_gate(columns, product):
         wide["middle"][:, columns] = product
 
@@ -841,11 +856,9 @@
         edge = edge + wide["middle"][spot, :] * (1.0 - blends[1][...])
         edges_out[2, slot : slot + 1, :] = edge[:1, :]
     edge_copy = copies.start(edges_out.at[2], edges_in.at[2], before)
-    settle("expand", "expanded")
-    for name in expand_names:
-        pieces[name].start()
     settle("gate", "back_gate")
-    pieces["gate0"].start()
+    start_pieces("g")
+    pump(0)
     edge_copy.wait()
 
     grad_branch = held["rows_2"]
@@ -881,6 +894,7 @@
         )
 
     hand_over("output", grad_branch)
+    pump(1)
     grad_recept = held["rows_3"]
 
     def gated_back(columns, product):
@@ -917,7 +931,8 @@
         lax.fori_loop(0, width // WIDE, adjoint_step, 0)
     sum_copies = share(1)
     settle("output", "back_output")
-    pieces["output0"].start()
+    start_pieces("o")
+    pump(2)
     for copy in sum_copies:
         copy.wait()
     later = held["later"]
@@ -965,6 +980,7 @@
     hand_over("key", grad_key)
     hand_over("value", grad_value)
     hand_over("recept", grad_recept)
+    pump(3)
 
     def keeper(name):
         def keep(columns, product):
@@ -985,7 +1001,8 @@
     edge_copy = copies.start(edges_out.at[3], edges_in.at[3], before)
     for name in ("key", "value", "recept"):
         settle(name, "back_" + name)
-        pieces[name + "0"].start()
+        start_pieces(name[0])
+    pump(4)
 
     for slot in range(slots):
 
@@ -1045,17 +1062,34 @@
         for at in range(vector_slot - len(found), vector_slot):
             vectors[...] += vector_in[at]
 
-    squares = ["gate0", "output0", "key0", "value0", "recept0"]
-    rounds = contract_names[:1] + expand_names[:1] + ["gate0"]
-    rounds += contract_names[1:] + expand_names[1:]
-    rounds += ["output0", "key0", "value0", "recept0"]
-    for turn in range(3):
-        axis = "kxy"[turn]
-        found = start_vectors(axis)
-        for name in rounds:
-            pieces[name].advance()
+    found = start_vectors("k")
+    pump(5)
+    finish_vectors(found)
+    found = start_vectors("x")
+    later_axes = ["y", "l", "h"]
+    while any(piece.copies for piece in pieces.values()):
+        for stage in range(len(AXES)):
+            waiting = [p for p in pieces.values() if p.copies and p.stage == stage]
+            if waiting:
+                break
+        for piece in waiting:
+            piece.advance()
         finish_vectors(found)
-    finish_vectors(start_vectors("z"))
+        found = start_vectors(later_axes.pop(0)) if later_axes else []
+    finish_vectors(found)
+    for axis in later_axes:
+        finish_vectors(start_vectors(axis))
+
+
+def place_outputs(plan, *refs):
+    count = len(OUTPUTS)
+    for source, target in zip(refs[: count - 1], refs[count:]):
+        target[...] = source[...]
+    part = plan.width // (plan.seq * plan.ch)
+    at = (lax.axis_index("seq") * plan.ch + lax.axis_index("ch")) * part
+    turned = pltpu.roll(refs[count - 1][...], lax.rem(plan.width - at, plan.width), 1)
+    for index, target in enumerate(refs[2 * count - 1 :]):
+        target[...] = turned[index : index + 1, :part]
 
 
 def body(*arguments):
@@ -1099,11 +1133,17 @@
             collective_id=0, has_side_effects=True, vmem_limit_bytes=62 * 2**20
         ),
     )(*operands)
-    got = dict(zip(OUTPUTS, results))
+    part = width // (plan.seq * plan.ch)
+    shapes = [outs[name] for name in OUTPUTS[:-1]] + [((1, part), F32)] * len(VECTORS)
+    results = pl.pallas_call(
+        functools.partial(place_outputs, plan),
+        out_shape=[jax.ShapeDtypeStruct(*shape) for shape in shapes],
+        in_specs=[pl.BlockSpec(memory_space=pltpu.VMEM)] * len(OUTPUTS),
+        out_specs=[pl.BlockSpec(memory_space=pltpu.VMEM)] * len(shapes),
+    )(*results)
+    got = dict(zip(OUTPUTS[:-1], results))
+    vectors = results[len(OUTPUTS) - 1 :]
     shape = values["tokens"].shape
-    part = width // (plan.seq * plan.ch)
-    at = (lax.axis_index("seq") * plan.ch + lax.axis_index("ch")) * part
-    vectors = lax.dynamic_slice_in_dim(got["vectors"], at, part, 1)
     slots = plan.slots
     return (
         got["mixed_out"].reshape(shape),
@@ -1117,7 +1157,7 @@
         got["grad_expand"],
         got["grad_contract"],
         got["grad_gate"],
-    ) + tuple(vectors[index] for index in range(len(VECTORS)))
+    ) + tuple(vector.reshape(part) for vector in vectors)
 
 
 def solution(mesh):

time: 234 us -> 177 us (0.76)
  Pallas kernels: 221 us -> 175 us
  local copies, waits for them, and re-layouts: 11.7 us -> 1.36 us
    pallas_call x1, Pallas kernels: 221 us -> 171 us  [body(): pl.pallas_call(functools.partial(layer_kernel, plan), out_shape=[jax.Shap...]
    unnamed x23 -> x0, local copies, waits for them, and re-layouts: 8.72 us -> none
    pallas_call x0 -> x1, Pallas kernels: none -> 3.4 us  [body(): pl.pallas_call(functools.partial(place_outputs, plan), out_shape=[jax.Sha...]
where the time goes in v3:
time: 177 us
  Pallas kernels  175 us (99%)
    pallas_call x1, Pallas kernels, body(): pl.pallas_call(functools.partial(layer_kernel, plan), out_shape=[jax.Shap...  171 us

profile of v3, /device:TPU:0, one launch (start us, length us, event | category | flops | bytes accessed | tf_op | source)
XLA Modules:
  0.0 176.6 jit_solution(9332463678946823614)
XLA Ops:
  0.7 171.2 %shard_map.390 = (bf16[256,1024]{1,0:T(8,128)(2,1)}, bf16[256,1024]{1,0:T(8,128)(2,1)}, f32[8,256]{1,0:T(8,128)}, f32[128,256]{1,0:T(8,128)}, f32[128,256]{1,0:T...) custom-call(bf16[256,1024]{1,0:T(8,128)(2,1)} %bitcast.26, ...), custom_call_target="tpu_custom_call" | custom-call | tf_op jit(solution)/shard_map/pallas_call | solution.py:1126
  171.8 3.4 %shard_map.391 = (bf16[256,1024]{1,0:T(8,128)(2,1)}, bf16[256,1024]{1,0:T(8,128)(2,1)}, f32[8,256]{1,0:T(8,128)}, f32[128,256]{1,0:T(8,128)}, f32[128,256]{1,0:T...) custom-call(bf16[256,1024]{1,0:T(8,128)(2,1)} %get-tuple-element.54., ...), custom_call_target="tpu_custom_call" | custom-call | tf_op jit(solution)/shard_map/pallas_call | solution.py:1138
  175.2 1.4 fusion

commit v4 on v3

--- a/solution.py
+++ b/solution.py
@@ -15,30 +15,47 @@
 BF16 = jnp.bfloat16
 TILE = 64
 WIDE = 256
+MATMUL_WIDE = 512
 SLOTS_OF_WEIGHTS = 3
 
 ORDERS = {
-    "c0": "xylh",
-    "c1": "yxlh",
+    "c0": "xlyh",
+    "c1": "ylhx",
     "c2": "lxyh",
-    "c3": "yxlh",
-    "e0": "xylh",
-    "e1": "yxlh",
-    "e2": "lyxh",
-    "e3": "lxyh",
-    "g": "lyxh",
+    "c3": "xylh",
+    "e0": "lxyh",
+    "e1": "ylxh",
+    "e2": "xylh",
+    "e3": "ylxh",
+    "g": "ylxh",
     "o": "xylh",
-    "k": "yxlh",
+    "k": "xylh",
     "v": "xylh",
-    "r": "yxlh",
+    "r": "xylh",
 }
 PUMPS = (
     (),
-    ("c0", "c1", "c2"),
-    ("c3", "e0", "e2"),
-    ("g", "c0", "c1", "c2"),
+    (
+        "c0", "c1",
+    ),
+    (
+        "e1",
+    ),
+    (
+        "c3",
+    ),
+    (
+        "c0",
+    ),
+    (
+        "e2", "c1", "e3",
+    ),
     (),
-    ("e1", "e3", "o", "c3", "c0", "c1", "c2"),
+    (
+        "c2", "e0", "e1", "o", "c1", "g", "e3", "c3", "c0", "r", "!", "g", "*", "c3", "e2", "c0",
+        "c3", "o", "k", "e2", "o", "r", "e2", "o", "k", "v", "r", "k", "c2", "r", "v", "k", "c2",
+        "e0", "v", "e1", "c2", "c1", "e0", "v", "e3", "e1", "g", "*", "e0", "e3", "g", "*",
+    ),
 )
 
 NN = (((1,), (0,)), ((), ()))
@@ -188,6 +205,7 @@
         self.broad = hidden // self.ch
         self.short = width // self.seq
         self.tall = hidden // self.seq
+        self.vector_span = self.short if self.short % 128 == 0 else width
         half = sizes["x"] * self.narrow
         self.pieces = []
         cuts = 4 if (self.tall // 4) % 128 == 0 else 1
@@ -219,7 +237,9 @@
             "finals": vmem((8, width), F32),
             "later": vmem((8, width), F32),
             "factor_ffn": vmem((rows, 128), F32),
+            "vectors": vmem((16, width), F32),
             "vector_in": vmem((self.count_vector_slots(), 16, width), F32),
+            "vector_parts": vmem((self.seq - 1, 16, self.vector_span), F32),
         }
         for name in ("expand", "gate", "output", "key", "value", "recept"):
             shapes["both_" + name] = vmem((2 * rows, width), BF16)
@@ -243,14 +263,15 @@
                 shape = (sizes[axis] - 1,) + tuple(sizes[a] for a in axes) + (height, breadth)
                 shapes["landing_" + short_name + str(stage)] = vmem(shape, BF16)
                 copies += sizes[axis] - 1
-        copies += self.count_vector_slots()
+        copies += self.count_vector_slots() + self.seq
         shapes["sends"] = pltpu.SemaphoreType.DMA((copies,))
         shapes["receives"] = pltpu.SemaphoreType.DMA((copies,))
         shapes["panel_sems"] = pltpu.SemaphoreType.DMA((SLOTS_OF_WEIGHTS,))
         self.shapes = shapes
 
     def count_vector_slots(self):
-        return sum(size - 1 for size in self.sizes.values())
+        axes = "kx" if self.vector_span < self.width else "kxylh"
+        return sum(self.sizes[axis] - 1 for axis in axes)
 
 
 INPUTS = (
@@ -371,11 +392,14 @@
             device_id_type=MESH,
         )
         greeted += 1
-    for axis in "ylh":
-        for step in range(1, sizes[axis]):
-            there = device_at(moved(place, sizes, axis, step))
-            pl.semaphore_signal(barrier, inc=1, device_id=there, device_id_type=MESH)
-            greeted += 1
+    for step in range(1, plan.seq):
+        pl.semaphore_signal(
+            barrier,
+            inc=1,
+            device_id=(lax.rem(seq_at + step, plan.seq), ch_at),
+            device_id_type=MESH,
+        )
+        greeted += 1
     copies = Copies(held["sends"], held["receives"])
     partner = device_at({**place, "k": 1 - place["k"]})
     after = (seq_at, lax.rem(ch_at + 1, ch_size))
@@ -384,7 +408,7 @@
     filled_here = [
         jnp.clip(lengths[slot] - ch_at * length, 0, length) for slot in range(slots)
     ]
-    vectors = outputs["vectors"]
+    vectors = held["vectors"]
     vectors[...] = jnp.zeros_like(vectors)
 
     def add_vector(name, value):
@@ -414,13 +438,13 @@
 
     def matmul(left, panel, how, use, left_columns=None):
         def step(index, carry):
-            columns = pl.ds(pl.multiple_of(index * WIDE, WIDE), WIDE)
+            columns = pl.ds(pl.multiple_of(index * MATMUL_WIDE, MATMUL_WIDE), MATMUL_WIDE)
             right = panel[:, columns] if how is NN else panel[columns, :]
             source = left[...] if left_columns is None else left[:, left_columns]
             use(columns, dot(source, right, how))
             return carry
 
-        lax.fori_loop(0, width // WIDE, step, 0)
+        lax.fori_loop(0, width // MATMUL_WIDE, step, 0)
 
     def counts(slot, shape, offset):
         at = lax.broadcasted_iota(jnp.int32, shape, 0) + offset
@@ -439,8 +463,8 @@
     edges_out, edges_in = held["edges_out"], held["edges_in"]
     edges_out[...] = jnp.zeros_like(edges_out)
     for slot in range(slots):
-        last = tokens[slot * length + length - TILE : slot * length + length, :].astype(F32)
-        edges_out[0, slot : slot + 1, :] = last[TILE - 1 :, :]
+        last = tokens[slot * length + length - 16 : slot * length + length, :].astype(F32)
+        edges_out[0, slot : slot + 1, :] = last[15:, :]
     pl.semaphore_wait(barrier, greeted)
     edge_copy = copies.start(edges_out.at[0], edges_in.at[0], after)
 
@@ -448,23 +472,36 @@
     keep_edge = jnp.where(ch_at > 0, 1.0, 0.0)
     keep_next = jnp.where(ch_at < ch_size - 1, 1.0, 0.0)
 
+    mixes = [inputs["mix_key"], inputs["mix_value"], inputs["mix_recept"]]
+    both_mix = [held["both_key"], held["both_value"], held["both_recept"]]
+
+    def last_row_before(slot, index):
+        return pl.ds(pl.multiple_of(slot * length + index * TILE - 16, 16), 16)
+
+    def mix_tile(slot, index, carry):
+        spot = tiles_of(slot, index)
+        unit, _ = normalize(tokens[spot, :].astype(F32))
+        normed = unit * gain_mix[...] + bias_mix[...]
+        earlier = shift_down(normed, carry)
+        for weights, target in zip(mixes, both_mix):
+            target[spot, :] = blend(normed, earlier, weights[...]).astype(BF16)
+
+    def mix_carry(slot, index):
+        unit, _ = normalize(tokens[last_row_before(slot, index), :].astype(F32))
+        return (unit * gain_mix[...] + bias_mix[...])[15:, :]
+
+    for slot in range(slots):
+
+        def mix_step(index, carry, slot=slot):
+            mix_tile(slot, index, mix_carry(slot, index))
+            return carry
+
+        lax.fori_loop(1, steps_in_slot, mix_step, 0)
     edge_copy.wait()
     edge_unit, _ = normalize(edges_in[0])
     edges_in[0] = (edge_unit * gain_mix[...] + bias_mix[...]) * keep_edge
-    mixes = [inputs["mix_key"], inputs["mix_value"], inputs["mix_recept"]]
-    both_mix = [held["both_key"], held["both_value"], held["both_recept"]]
-    for slot in range(slots):
-
-        def mix_step(index, carry, slot=slot):
-            spot = tiles_of(slot, index)
-            unit, _ = normalize(tokens[spot, :].astype(F32))
-            normed = unit * gain_mix[...] + bias_mix[...]
-            earlier = shift_down(normed, carry)
-            for weights, target in zip(mixes, both_mix):
-                target[spot, :] = blend(normed, earlier, weights[...]).astype(BF16)
-            return normed[TILE - 1 :, :]
-
-        lax.fori_loop(0, steps_in_slot, mix_step, edges_in[0, slot : slot + 1, :])
+    for slot in range(slots):
+        mix_tile(slot, 0, edges_in[0, slot : slot + 1, :])
     exchanges = {}
     for name in ("key", "value", "recept"):
         ref = held["both_" + name]
@@ -611,9 +648,9 @@
     gain_ffn, bias_ffn = inputs["gain_ffn"], inputs["bias_ffn"]
     factor_ffn = held["factor_ffn"]
     for slot in range(slots):
-        last = wide["middle"][slot * length + length - TILE : slot * length + length, :]
+        last = wide["middle"][slot * length + length - 8 : slot * length + length, :]
         unit, _ = normalize(last)
-        edges_out[1, slot : slot + 1, :] = (unit * gain_ffn[...] + bias_ffn[...])[TILE - 1 :, :]
+        edges_out[1, slot : slot + 1, :] = (unit * gain_ffn[...] + bias_ffn[...])[7:, :]
     edge_copy = copies.start(edges_out.at[1], edges_in.at[1], after)
 
     def unit_step(index, carry):
@@ -624,23 +661,28 @@
         return carry
 
     lax.fori_loop(0, rows // TILE, unit_step, 0)
-    edge_copy.wait()
     blends = [inputs["blend_key"], inputs["blend_gate"]]
     both_blend = [held["both_expand"], held["both_gate"]]
+
+    def blend_tile(slot, index, carry):
+        spot = tiles_of(slot, index)
+        normed = wide["unit"][spot, :] * gain_ffn[...] + bias_ffn[...]
+        earlier = shift_down(normed, carry)
+        wide["gap"][spot, :] = normed - earlier
+        for weights, target in zip(blends, both_blend):
+            target[spot, :] = blend(normed, earlier, weights[...]).astype(BF16)
+
     for slot in range(slots):
 
         def blend_step(index, carry, slot=slot):
-            spot = tiles_of(slot, index)
-            normed = wide["unit"][spot, :] * gain_ffn[...] + bias_ffn[...]
-            earlier = shift_down(normed, carry)
-            wide["gap"][spot, :] = normed - earlier
-            for weights, target in zip(blends, both_blend):
-                target[spot, :] = blend(normed, earlier, weights[...]).astype(BF16)
-            return normed[TILE - 1 :, :]
-
-        lax.fori_loop(
-            0, steps_in_slot, blend_step, edges_in[1, slot : slot + 1, :] * keep_edge
-        )
+            last = wide["unit"][last_row_before(slot, index), :][15:, :]
+            blend_tile(slot, index, last * gain_ffn[...] + bias_ffn[...])
+            return carry
+
+        lax.fori_loop(1, steps_in_slot, blend_step, 0)
+    edge_copy.wait()
+    for slot in range(slots):
+        blend_tile(slot, 0, edges_in[1, slot : slot + 1, :] * keep_edge)
     for name in ("expand", "gate"):
         ref = held["both_" + name]
         exchanges[name] = [
@@ -653,8 +695,8 @@
 
         def store_hidden(columns, product, index=index):
             positive = jnp.maximum(product, 0.0)
-            start = pl.multiple_of(columns.start + index * width, WIDE)
-            both_hidden[first_rows, pl.ds(start, WIDE)] = (positive * positive).astype(BF16)
+            start = pl.multiple_of(columns.start + index * width, MATMUL_WIDE)
+            both_hidden[first_rows, pl.ds(start, MATMUL_WIDE)] = (positive * positive).astype(BF16)
 
         matmul(own("expand"), panels.take(), NN, store_hidden)
         panels.release()
@@ -680,7 +722,7 @@
     def finish_forward(columns, product):
         gate = jax.nn.sigmoid(product)
         contracted = wide["total"][:, columns]
-        inside = tall_mask(WIDE)
+        inside = tall_mask(MATMUL_WIDE)
         mixed = wide["middle"][:, columns] + gate * contracted
         outputs["mixed_out"][:, columns] = jnp.where(inside, mixed, 0.0).astype(BF16)
         grad = jnp.where(inside, grad_out[:, columns].astype(F32), 0.0)
@@ -794,8 +836,53 @@
             if short_name.startswith(prefix):
                 piece.start()
 
-    def pump(point):
+    vector_in = held["vector_in"]
+    vector_parts = held["vector_parts"]
+    span = plan.vector_span
+    scattered = span < width
+    vector_queue = {"left": list("kxs" if scattered else "kxylh"), "open": [], "slot": 0}
+
+    def part_of(index):
+        return vectors.at[:, pl.ds(pl.multiple_of(index * span, span), span)]
+
+    def start_vectors():
+        axis = vector_queue["left"].pop(0)
+        if axis == "s":
+            for step in range(1, plan.seq):
+                there = lax.rem(seq_at + step, plan.seq)
+                target = vector_parts.at[step - 1]
+                copy = copies.start(part_of(there), target, (there, ch_at))
+                vector_queue["open"].append((copy, None))
+            return
+        for step in range(1, sizes[axis]):
+            there = device_at(moved(place, sizes, axis, step))
+            copy = copies.start(vectors, vector_in.at[vector_queue["slot"]], there)
+            vector_queue["open"].append((copy, vector_queue["slot"]))
+            vector_queue["slot"] += 1
+
+    def pump_vectors():
+        found, vector_queue["open"] = vector_queue["open"], []
+        for copy, _ in found:
+            copy.wait()
+        for _, slot in found:
+            if slot is not None:
+                vectors[...] += vector_in[slot]
+        if vector_queue["left"]:
+            start_vectors()
+        elif found:
+            total = part_of(seq_at)[...] if scattered else vectors[...]
+            for step in range(plan.seq - 1 if scattered else 0):
+                total = total + vector_parts[step]
+            outputs["vectors"][...] = total
+
+    def pump(point, finish_mix=None):
         for short_name in PUMPS[point]:
+            if short_name == "!":
+                finish_mix()
+                continue
+            if short_name == "*":
+                pump_vectors()
+                continue
             piece = pieces.get(short_name)
             if piece is not None and piece.copies:
                 piece.advance()
@@ -808,13 +895,14 @@
     for index in range(panel_count):
 
         def store_expanded(columns, product, index=index):
-            start = pl.multiple_of(columns.start + index * width, WIDE)
-            spot = pl.ds(start, WIDE)
+            start = pl.multiple_of(columns.start + index * width, MATMUL_WIDE)
+            spot = pl.ds(start, MATMUL_WIDE)
             positive = jnp.sqrt(both_hidden[first_rows, spot].astype(F32))
             grad_expanded[:, spot] = (product * 2.0 * positive).astype(BF16)
 
         matmul(grad_contracted, panels.take(), NT, store_expanded)
         panels.release()
+    pump(0)
     exchanges["expanded"] = []
     for x_at in range(sizes["x"]):
         theirs = pl.multiple_of((x_at * 2 + 1 - place["k"]) * plan.broad, plan.broad)
@@ -841,9 +929,6 @@
         )
         panels.release()
 
-    settle("expand", "expanded")
-    start_pieces("e")
-
     def store_gate(columns, product):
         wide["middle"][:, columns] = product
 
@@ -851,50 +936,59 @@
     panels.release()
 
     for slot in range(slots):
-        spot = slice(slot * length, slot * length + TILE)
+        spot = slice(slot * length, slot * length + 8)
         edge = wide["total"][spot, :] * (1.0 - blends[0][...])
         edge = edge + wide["middle"][spot, :] * (1.0 - blends[1][...])
         edges_out[2, slot : slot + 1, :] = edge[:1, :]
     edge_copy = copies.start(edges_out.at[2], edges_in.at[2], before)
+    settle("expand", "expanded")
+    start_pieces("e")
     settle("gate", "back_gate")
     start_pieces("g")
-    pump(0)
+    pump(1)
+    grad_branch = held["rows_2"]
+
+    def first_row_after(slot, index):
+        return pl.ds(pl.multiple_of(slot * length + (index + 1) * TILE, 8), 8)
+
+    def ffn_back_earlier(spot):
+        earlier = wide["total"][spot, :] * (1.0 - blends[0][...])
+        return earlier + wide["middle"][spot, :] * (1.0 - blends[1][...])
+
+    def ffn_back_tile(slot, index, carry):
+        spot = tiles_of(slot, index)
+        in_expand, in_gate = wide["total"][spot, :], wide["middle"][spot, :]
+        gap = wide["gap"][spot, :]
+        unit = wide["unit"][spot, :]
+        add_vector("blend_key", in_expand * gap)
+        add_vector("blend_gate", in_gate * gap)
+        earlier = ffn_back_earlier(spot)
+        grad_normed = in_expand * blends[0][...] + in_gate * blends[1][...]
+        grad_normed = grad_normed + shift_up(earlier, carry)
+        add_vector("gain_ffn", grad_normed * unit)
+        add_vector("bias_ffn", grad_normed)
+        scaled = grad_normed * gain_ffn[...]
+        centered = scaled - jnp.mean(scaled, axis=-1, keepdims=True)
+        centered = centered - unit * jnp.mean(scaled * unit, axis=-1, keepdims=True)
+        _, _, filled = counts(slot, (TILE, width), index * TILE)
+        grad = jnp.where(filled, grad_out[spot, :].astype(F32), 0.0)
+        grad = grad + factor_ffn[spot, :1] * centered
+        wide["total"][spot, :] = grad
+        grad_branch[spot, :] = grad.astype(BF16)
+
+    for slot in range(slots):
+
+        def ffn_back_step(index, carry, slot=slot):
+            ffn_back_tile(slot, index, ffn_back_earlier(first_row_after(slot, index))[:1, :])
+            return carry
+
+        lax.fori_loop(0, steps_in_slot - 1, ffn_back_step, 0)
     edge_copy.wait()
-
-    grad_branch = held["rows_2"]
-    for slot in range(slots):
-
-        def ffn_back_step(index, carry, slot=slot):
-            spot = tiles_of(slot, steps_in_slot - 1 - index)
-            at = (steps_in_slot - 1 - index) * TILE
-            in_expand, in_gate = wide["total"][spot, :], wide["middle"][spot, :]
-            gap = wide["gap"][spot, :]
-            unit = wide["unit"][spot, :]
-            add_vector("blend_key", in_expand * gap)
-            add_vector("blend_gate", in_gate * gap)
-            weight_key, weight_gate = blends[0][...], blends[1][...]
-            earlier = in_expand * (1.0 - weight_key) + in_gate * (1.0 - weight_gate)
-            grad_normed = (
-                in_expand * weight_key + in_gate * weight_gate + shift_up(earlier, carry)
-            )
-            add_vector("gain_ffn", grad_normed * unit)
-            add_vector("bias_ffn", grad_normed)
-            scaled = grad_normed * gain_ffn[...]
-            centered = scaled - jnp.mean(scaled, axis=-1, keepdims=True)
-            centered = centered - unit * jnp.mean(scaled * unit, axis=-1, keepdims=True)
-            _, _, filled = counts(slot, (TILE, width), at)
-            grad = jnp.where(filled, grad_out[spot, :].astype(F32), 0.0)
-            grad = grad + factor_ffn[spot, :1] * centered
-            wide["total"][spot, :] = grad
-            grad_branch[spot, :] = grad.astype(BF16)
-            return earlier[:1, :]
-
-        lax.fori_loop(
-            0, steps_in_slot, ffn_back_step, edges_in[2, slot : slot + 1, :] * keep_next
-        )
+    for slot in range(slots):
+        ffn_back_tile(slot, steps_in_slot - 1, edges_in[2, slot : slot + 1, :] * keep_next)
 
     hand_over("output", grad_branch)
-    pump(1)
+    pump(2)
     grad_recept = held["rows_3"]
 
     def gated_back(columns, product):
@@ -911,6 +1005,8 @@
 
     matmul(grad_branch, panels.take(), NT, gated_back)
     panels.release()
+    hand_over("recept", grad_recept)
+    pump(3)
 
     for slot in range(slots):
 
@@ -932,7 +1028,9 @@
     sum_copies = share(1)
     settle("output", "back_output")
     start_pieces("o")
-    pump(2)
+    settle("recept", "back_recept")
+    start_pieces("r")
+    pump(4)
     for copy in sum_copies:
         copy.wait()
     later = held["later"]
@@ -979,8 +1077,7 @@
 
     hand_over("key", grad_key)
     hand_over("value", grad_value)
-    hand_over("recept", grad_recept)
-    pump(3)
+    pump(5)
 
     def keeper(name):
         def keep(columns, product):
@@ -993,92 +1090,72 @@
         panels.release()
     in_names = ("sigmoid", "unit", "gap")
     for slot in range(slots):
-        spot = slice(slot * length, slot * length + TILE)
-        edge = jnp.zeros((TILE, width), F32)
+        spot = slice(slot * length, slot * length + 8)
+        edge = jnp.zeros((8, width), F32)
         for name, weights in zip(in_names, mixes):
             edge = edge + wide[name][spot, :] * (1.0 - weights[...])
         edges_out[3, slot : slot + 1, :] = edge[:1, :]
     edge_copy = copies.start(edges_out.at[3], edges_in.at[3], before)
-    for name in ("key", "value", "recept"):
+    for name in ("key", "value"):
         settle(name, "back_" + name)
         start_pieces(name[0])
-    pump(4)
-
-    for slot in range(slots):
-
-        def again_step(index, carry, slot=slot):
-            spot = tiles_of(slot, index)
-            unit, _ = normalize(tokens[spot, :].astype(F32))
-            normed = unit * gain_mix[...] + bias_mix[...]
-            wide["num"][spot, :] = unit
-            wide["den"][spot, :] = normed - shift_down(normed, carry)
-            return normed[TILE - 1 :, :]
-
-        lax.fori_loop(0, steps_in_slot, again_step, edges_in[0, slot : slot + 1, :])
-    edge_copy.wait()
+    pump(6)
+
+    in_carry = [edges_in[0, slot : slot + 1, :] for slot in range(slots)]
     vector_names = ("mix_key", "mix_value", "mix_recept")
+
+    def mix_back_earlier(spot):
+        earlier = wide[in_names[0]][spot, :] * (1.0 - mixes[0][...])
+        for name, weights in zip(in_names[1:], mixes[1:]):
+            earlier = earlier + wide[name][spot, :] * (1.0 - weights[...])
+        return earlier
+
+    def mix_back_tile(slot, index, before_row, after_row):
+        spot = tiles_of(slot, index)
+        unit, factor = normalize(tokens[spot, :].astype(F32))
+        normed = unit * gain_mix[...] + bias_mix[...]
+        gap = normed - shift_down(normed, before_row)
+        grad_normed = shift_up(mix_back_earlier(spot), after_row)
+        for name, weights, vector in zip(in_names, mixes, vector_names):
+            grad = wide[name][spot, :]
+            add_vector(vector, grad * gap)
+            grad_normed = grad_normed + grad * weights[...]
+        add_vector("gain_mix", grad_normed * unit)
+        add_vector("bias_mix", grad_normed)
+        scaled = grad_normed * gain_mix[...]
+        centered = scaled - jnp.mean(scaled, axis=-1, keepdims=True)
+        centered = centered - unit * jnp.mean(scaled * unit, axis=-1, keepdims=True)
+        grad = wide["total"][spot, :] + factor * centered
+        outputs["grad_tokens"][spot, :] = grad.astype(BF16)
+
+    def next_row(slot, index):
+        return mix_back_earlier(first_row_after(slot, index))[:1, :]
+
+    last_tile = steps_in_slot - 1
     for slot in range(slots):
 
         def mix_back_step(index, carry, slot=slot):
-            spot = tiles_of(slot, steps_in_slot - 1 - index)
-            _, factor = normalize(tokens[spot, :].astype(F32))
-            unit, gap = wide["num"][spot, :], wide["den"][spot, :]
-            earlier = jnp.zeros((TILE, width), F32)
-            grad_normed = jnp.zeros((TILE, width), F32)
-            for name, weights, vector in zip(in_names, mixes, vector_names):
-                grad = wide[name][spot, :]
-                add_vector(vector, grad * gap)
-                earlier = earlier + grad * (1.0 - weights[...])
-                grad_normed = grad_normed + grad * weights[...]
-            grad_normed = grad_normed + shift_up(earlier, carry)
-            add_vector("gain_mix", grad_normed * unit)
-            add_vector("bias_mix", grad_normed)
-            scaled = grad_normed * gain_mix[...]
-            centered = scaled - jnp.mean(scaled, axis=-1, keepdims=True)
-            centered = centered - unit * jnp.mean(scaled * unit, axis=-1, keepdims=True)
-            grad = wide["total"][spot, :] + factor * centered
-            outputs["grad_tokens"][spot, :] = grad.astype(BF16)
-            return earlier[:1, :]
-
-        lax.fori_loop(
-            0, steps_in_slot, mix_back_step, edges_in[3, slot : slot + 1, :] * keep_next
-        )
-
-    vector_in = held["vector_in"]
-    vector_slot = 0
-
-    def start_vectors(axis):
-        nonlocal vector_slot
-        found = []
-        for step in range(1, sizes[axis]):
-            there = device_at(moved(place, sizes, axis, step))
-            found.append(copies.start(vectors, vector_in.at[vector_slot], there))
-            vector_slot += 1
-        return found
-
-    def finish_vectors(found):
-        for copy in found:
-            copy.wait()
-        for at in range(vector_slot - len(found), vector_slot):
-            vectors[...] += vector_in[at]
-
-    found = start_vectors("k")
-    pump(5)
-    finish_vectors(found)
-    found = start_vectors("x")
-    later_axes = ["y", "l", "h"]
+            mix_back_tile(slot, index, mix_carry(slot, index), next_row(slot, index))
+            return carry
+
+        lax.fori_loop(1, last_tile, mix_back_step, 0)
+        if last_tile:
+            mix_back_tile(slot, 0, in_carry[slot], next_row(slot, 0))
+    def finish_mix():
+        edge_copy.wait()
+        for slot in range(slots):
+            after_row = edges_in[3, slot : slot + 1, :] * keep_next
+            before_row = mix_carry(slot, last_tile) if last_tile else in_carry[slot]
+            mix_back_tile(slot, last_tile, before_row, after_row)
+        start_vectors()
+
+    pump(7, finish_mix)
     while any(piece.copies for piece in pieces.values()):
-        for stage in range(len(AXES)):
-            waiting = [p for p in pieces.values() if p.copies and p.stage == stage]
-            if waiting:
-                break
-        for piece in waiting:
-            piece.advance()
-        finish_vectors(found)
-        found = start_vectors(later_axes.pop(0)) if later_axes else []
-    finish_vectors(found)
-    for axis in later_axes:
-        finish_vectors(start_vectors(axis))
+        for piece in pieces.values():
+            if piece.copies:
+                piece.advance()
+    while vector_queue["open"]:
+        pump_vectors()
 
 
 def place_outputs(plan, *refs):
@@ -1086,8 +1163,11 @@
     for source, target in zip(refs[: count - 1], refs[count:]):
         target[...] = source[...]
     part = plan.width // (plan.seq * plan.ch)
-    at = (lax.axis_index("seq") * plan.ch + lax.axis_index("ch")) * part
-    turned = pltpu.roll(refs[count - 1][...], lax.rem(plan.width - at, plan.width), 1)
+    at = lax.axis_index("ch") * part
+    span = plan.vector_span
+    if span == plan.width:
+        at = at + lax.axis_index("seq") * plan.short
+    turned = pltpu.roll(refs[count - 1][...], lax.rem(span - at, span), 1)
     for index, target in enumerate(refs[2 * count - 1 :]):
         target[...] = turned[index : index + 1, :part]
 
@@ -1121,7 +1201,7 @@
         "grad_expand": ((plan.short, plan.broad), F32),
         "grad_contract": ((plan.tall, plan.narrow), F32),
         "grad_gate": ((plan.short, plan.narrow), F32),
-        "vectors": ((16, width), F32),
+        "vectors": ((16, plan.vector_span), F32),
     }
     results = pl.pallas_call(
         functools.partial(layer_kernel, plan),
@@ -1130,7 +1210,7 @@
         out_specs=[pl.BlockSpec(memory_space=pltpu.VMEM)] * len(OUTPUTS),
         scratch_shapes=list(plan.shapes.values()),
         compiler_params=pltpu.CompilerParams(
-            collective_id=0, has_side_effects=True, vmem_limit_bytes=62 * 2**20
+            collective_id=0, has_side_effects=True, vmem_limit_bytes=63 * 2**20
         ),
     )(*operands)
     part = width // (plan.seq * plan.ch)

time: 177 us -> 154 us (0.87)
  Pallas kernels: 175 us -> 152 us
    pallas_call x1, Pallas kernels: 171 us -> 148 us  [body(): pl.pallas_call(functools.partial(layer_kernel, plan), out_shape=[jax.Shap...]
where the time goes in v4:
time: 154 us
  Pallas kernels  152 us (99%)
    pallas_call x1, Pallas kernels, body(): pl.pallas_call(functools.partial(layer_kernel, plan), out_shape=[jax.Shap...  148 us
    pallas_call x1, Pallas kernels, body(): pl.pallas_call(functools.partial(place_outputs, plan), out_shape=[jax.Sha...  3.4 us

profile of v4, /device:TPU:0, one launch (start us, length us, event | category | flops | bytes accessed | tf_op | source)
XLA Modules:
  0.0 153.7 jit_solution(1879642161649157015)
XLA Ops:
  0.7 148.3 %shard_map.390 = (bf16[256,1024]{1,0:T(8,128)(2,1)}, bf16[256,1024]{1,0:T(8,128)(2,1)}, f32[8,256]{1,0:T(8,128)}, f32[128,256]{1,0:T(8,128)}, f32[128,256]{1,0:T...) custom-call(bf16[256,1024]{1,0:T(8,128)(2,1)} %bitcast.26, ...), custom_call_target="tpu_custom_call" | custom-call | tf_op jit(solution)/shard_map/pallas_call | solution.py:1206
  149.0 3.4 %shard_map.391 = (bf16[256,1024]{1,0:T(8,128)(2,1)}, bf16[256,1024]{1,0:T(8,128)(2,1)}, f32[8,256]{1,0:T(8,128)}, f32[128,256]{1,0:T(8,128)}, f32[128,256]{1,0:T...) custom-call(bf16[256,1024]{1,0:T(8,128)(2,1)} %get-tuple-element.54., ...), custom_call_target="tpu_custom_call" | custom-call | tf_op jit(solution)/shard_map/pallas_call | solution.py:1218
  152.4 1.4 fusion

commit v5 on v4

--- a/solution.py
+++ b/solution.py
@@ -19,19 +19,19 @@
 SLOTS_OF_WEIGHTS = 3
 
 ORDERS = {
-    "c0": "xlyh",
-    "c1": "ylhx",
-    "c2": "lxyh",
+    "c0": "ylhx",
+    "c1": "lyxh",
+    "c2": "yxlh",
     "c3": "xylh",
-    "e0": "lxyh",
-    "e1": "ylxh",
-    "e2": "xylh",
-    "e3": "ylxh",
-    "g": "ylxh",
+    "e0": "lyh",
+    "e1": "lyh",
+    "e2": "ylh",
+    "e3": "ylh",
+    "g": "lyxh",
     "o": "xylh",
     "k": "xylh",
     "v": "xylh",
-    "r": "xylh",
+    "r": "yxlh",
 }
 PUMPS = (
     (),
@@ -39,22 +39,22 @@
         "c0", "c1",
     ),
     (
-        "e1",
-    ),
-    (
-        "c3",
-    ),
-    (
-        "c0",
-    ),
-    (
-        "e2", "c1", "e3",
+        "c3", "E0", "c2", "g",
     ),
     (),
     (
-        "c2", "e0", "e1", "o", "c1", "g", "e3", "c3", "c0", "r", "!", "g", "*", "c3", "e2", "c0",
-        "c3", "o", "k", "e2", "o", "r", "e2", "o", "k", "v", "r", "k", "c2", "r", "v", "k", "c2",
-        "e0", "v", "e1", "c2", "c1", "e0", "v", "e3", "e1", "g", "*", "e0", "e3", "g", "*",
+        "E1", "c1",
+    ),
+    (
+        "c0", "c2", "c3",
+    ),
+    (
+        "e0", "E2", "g", "e1",
+    ),
+    (
+        "E3", "c0", "c2", "r", "c3", "e0", "c2", "o", "c3", "c1", "!", "e2", "e0", "*", "e1", "c1",
+        "e2", "e3", "e1", "k", "e2", "o", "e3", "o", "k", "e3", "v", "o", "g", "c0", "k", "v", "g",
+        "r", "k", "*", "v", "r", "*", "v", "r",
     ),
 )
 
@@ -114,7 +114,7 @@
     def __init__(self, make, order, sizes, place, copies, held, landings, out_ref):
         self.make, self.order, self.sizes, self.place = make, order, sizes, place
         self.remote, self.held, self.landings, self.out_ref = copies, held, landings, out_ref
-        self.axes = list(AXES)
+        self.axes = [axis for axis in AXES if axis in order]
         self.stage = 0
         self.copies = []
 
@@ -213,20 +213,25 @@
         for cut in range(cuts):
             self.pieces.append(("contract", "c" + str(cut), part, cut * part, self.narrow, 0))
         cuts = 4 if (self.broad // 4) % 128 == 0 else 1
+        self.expand_cuts = cuts
         part = self.broad // cuts
         for cut in range(cuts):
             self.pieces.append(("expand", "e" + str(cut), self.short, 0, part, cut * part))
         for name in ("gate", "output", "key", "value", "recept"):
             self.pieces.append((name, name[0], self.short, 0, self.narrow, 0))
-        self.orders = {
-            piece[1]: ORDERS[piece[1]] if piece[2] % 128 == 0 else "xylh" for piece in self.pieces
-        }
+        self.orders = {}
+        for name, short_name, height, _, _, _ in self.pieces:
+            if height % 128 == 0:
+                self.orders[short_name] = ORDERS[short_name]
+            else:
+                self.orders[short_name] = "hly" if name == "expand" else "xylh"
         vmem = pltpu.VMEM
         shapes = {
             "panels": vmem((SLOTS_OF_WEIGHTS, width, width), BF16),
             "both_hidden": vmem((2 * rows, hidden), BF16),
             "grad_expanded": vmem((rows, hidden), BF16),
-            "their_expanded": vmem((rows, hidden // 2), BF16),
+            "their_expanded": vmem(((self.ch - 1) * rows, self.broad), BF16),
+            "both_expand": vmem((self.ch * rows, width), BF16),
             "key": vmem((rows, width), BF16),
             "value": vmem((rows, width), BF16),
             "edges_out": vmem((4, 8, width), F32),
@@ -241,7 +246,7 @@
             "vector_in": vmem((self.count_vector_slots(), 16, width), F32),
             "vector_parts": vmem((self.seq - 1, 16, self.vector_span), F32),
         }
-        for name in ("expand", "gate", "output", "key", "value", "recept"):
+        for name in ("gate", "output", "key", "value", "recept"):
             shapes["both_" + name] = vmem((2 * rows, width), BF16)
         for name in ("contract", "gate", "output", "key", "value", "recept"):
             shapes["back_" + name] = vmem((2 * rows, half), BF16)
@@ -249,15 +254,15 @@
             shapes["rows_" + str(index)] = vmem((rows, width), BF16)
         for name in ("middle", "total", "sigmoid", "num", "den", "unit", "gap"):
             shapes["wide_" + name] = vmem((rows, width), F32)
-        copies = 64 + 4 * self.ch
+        copies = 64 + 16 * self.ch
         for name, short_name, height, _, breadth, _ in self.pieces:
             order = self.orders[short_name]
-            axes = [axis for axis in AXES if axis != order[0]]
+            axes = [axis for axis in AXES if axis in order[1:]]
             lead = tuple(sizes[a] for a in axes)
             shapes["held_" + short_name] = vmem(
                 (sizes[order[0]] - 1,) + lead + (height, breadth), BF16
             )
-            axes = list(AXES)
+            axes = [axis for axis in AXES if axis in order]
             for stage, axis in enumerate(order):
                 axes.remove(axis)
                 shape = (sizes[axis] - 1,) + tuple(sizes[a] for a in axes) + (height, breadth)
@@ -683,11 +688,21 @@
     edge_copy.wait()
     for slot in range(slots):
         blend_tile(slot, 0, edges_in[1, slot : slot + 1, :] * keep_edge)
-    for name in ("expand", "gate"):
-        ref = held["both_" + name]
-        exchanges[name] = [
-            copies.start(ref.at[pl.ds(0, rows), :], ref.at[pl.ds(rows, rows), :], partner)
-        ]
+    both_expand, both_gate = held["both_expand"], held["both_gate"]
+
+    def block_of(ref, index):
+        return ref.at[pl.ds(index * rows, rows), :]
+
+    exchanges["expand"] = [
+        copies.start(block_of(both_expand, 0), block_of(both_expand, 1), partner)
+    ]
+    across = []
+    for step in range(1, sizes["x"]):
+        there = device_at(moved(place, sizes, "x", step))
+        across.append(
+            copies.start(block_of(both_expand, 0), block_of(both_expand, 2 * step), there)
+        )
+    exchanges["gate"] = [copies.start(block_of(both_gate, 0), block_of(both_gate, 1), partner)]
 
     both_hidden = held["both_hidden"]
     exchanges["hidden"] = []
@@ -763,27 +778,24 @@
         row_step = plan.tall if name == "contract" else plan.short
         if name == "expand":
             rights = (
-                (
-                    first_rows,
-                    grad_expanded,
-                    lambda at: (at * 2 + place["k"]) * plan.broad + column_cut,
-                ),
-                (last_rows, their_expanded, lambda at: at * plan.broad + column_cut),
+                (first_rows, grad_expanded, lambda at: ch_at * plan.broad + column_cut),
+                (slice(rows, ch_size * rows), their_expanded, lambda at: column_cut),
             )
         else:
             rights = ((slice(None), held["back_" + name], lambda at: at * plan.narrow),)
+        kept = [a for a in AXES if a in plan.orders[short_name] and a != first]
 
         def along(axis, coordinate):
             return [coordinate] if axis == first else range(sizes[axis])
 
         def make(coordinate, emit):
             places = [(l, y) for l in along("l", coordinate) for y in along("y", coordinate)]
-            columns = along("x", coordinate)
+            columns = [0] if name == "expand" else along("x", coordinate)
 
             def step(h, carry):
                 starts = [((h * 2 + l) * 2 + y) * row_step + row_cut for l, y in places]
                 spans = [(start, height) for start in starts]
-                if row_step == height and first in "xl":
+                if row_step == height and first in "xlh":
                     spans = [(starts[0], len(starts) * height)]
                 value = None
                 for part, right, column_of in rights:
@@ -805,10 +817,13 @@
                         at = 0 if first == "x" else x
                         block = rows_of[:, at * breadth : (at + 1) * breadth]
                         where = {"h": h, "l": l, "y": y, "x": x}
-                        emit(tuple(where[a] for a in AXES if a != first), block)
+                        emit(tuple(where[a] for a in kept), block)
                 return carry
 
-            lax.fori_loop(0, sizes["h"], step, 0)
+            if first == "h":
+                step(coordinate, 0)
+            else:
+                lax.fori_loop(0, sizes["h"], step, 0)
 
         return make
 
@@ -880,6 +895,10 @@
             if short_name == "!":
                 finish_mix()
                 continue
+            if short_name[0] == "E":
+                if short_name in exchanges:
+                    start_expand(int(short_name[1:]))
+                continue
             if short_name == "*":
                 pump_vectors()
                 continue
@@ -902,17 +921,42 @@
 
         matmul(grad_contracted, panels.take(), NT, store_expanded)
         panels.release()
-    pump(0)
-    exchanges["expanded"] = []
-    for x_at in range(sizes["x"]):
-        theirs = pl.multiple_of((x_at * 2 + 1 - place["k"]) * plan.broad, plan.broad)
-        exchanges["expanded"].append(
+    for step, copy in enumerate(across, 1):
+        copy.wait()
+        exchanges["expand"].append(
             copies.start(
-                grad_expanded.at[:, pl.ds(theirs, plan.broad)],
-                their_expanded.at[:, pl.ds(x_at * plan.broad, plan.broad)],
-                partner,
+                block_of(both_expand, 2 * step), block_of(both_expand, 2 * step + 1), partner
             )
         )
+
+    def send_expanded(cut):
+        if cut >= plan.expand_cuts:
+            return
+        part = plan.broad // plan.expand_cuts
+        found = exchanges["E" + str(cut)] = []
+        targets = [({**place, "k": 1 - place["k"]}, 0)]
+        for step in range(1, sizes["x"]):
+            there = moved(place, sizes, "x", step)
+            targets.append((there, 2 * step - 1))
+            targets.append(({**there, "k": 1 - place["k"]}, 2 * step))
+        for there, slot in targets:
+            start = (there["x"] * 2 + there["k"]) * plan.broad + cut * part
+            found.append(
+                copies.start(
+                    grad_expanded.at[:, pl.ds(pl.multiple_of(start, part), part)],
+                    their_expanded.at[pl.ds(slot * rows, rows), pl.ds(cut * part, part)],
+                    device_at(there),
+                )
+            )
+
+    def start_expand(cut):
+        if "expand" in exchanges:
+            settle("expand")
+        settle("E" + str(cut))
+        pieces["e" + str(cut)].start()
+
+    send_expanded(0)
+    pump(0)
     for index in range(panel_count):
 
         def add_expand(columns, product, index=index):
@@ -941,8 +985,7 @@
         edge = edge + wide["middle"][spot, :] * (1.0 - blends[1][...])
         edges_out[2, slot : slot + 1, :] = edge[:1, :]
     edge_copy = copies.start(edges_out.at[2], edges_in.at[2], before)
-    settle("expand", "expanded")
-    start_pieces("e")
+    send_expanded(1)
     settle("gate", "back_gate")
     start_pieces("g")
     pump(1)
@@ -1026,6 +1069,8 @@
 
         lax.fori_loop(0, width // WIDE, adjoint_step, 0)
     sum_copies = share(1)
+    send_expanded(2)
+    send_expanded(3)
     settle("output", "back_output")
     start_pieces("o")
     settle("recept", "back_recept")
@@ -1150,6 +1195,9 @@
         start_vectors()
 
     pump(7, finish_mix)
+    for cut in range(plan.expand_cuts):
+        if "E" + str(cut) in exchanges:
+            start_expand(cut)
     while any(piece.copies for piece in pieces.values()):
         for piece in pieces.values():
             if piece.copies:
@@ -1158,18 +1206,40 @@
         pump_vectors()
 
 
+LARGE = tuple(name for name in OUTPUTS if name not in ("final", "vectors"))
+
+
 def place_outputs(plan, *refs):
-    count = len(OUTPUTS)
-    for source, target in zip(refs[: count - 1], refs[count:]):
-        target[...] = source[...]
+    count = len(LARGE)
+    refs = list(refs)
+
+    def take(number):
+        return [refs.pop(0) for _ in range(number)]
+
+    sources, (final, vectors) = take(count), take(2)
+    targets, finals, parts = take(count), take(2), take(len(VECTORS))
+    buffers, (sems,) = take(count), take(1)
+    loads, stores = [], []
+    for index in range(count):
+        loads.append(pltpu.make_async_copy(sources[index], buffers[index], sems.at[0, index]))
+        stores.append(pltpu.make_async_copy(buffers[index], targets[index], sems.at[1, index]))
+        loads[-1].start()
+    slots = plan.slots
+    for index, target in enumerate(finals):
+        target[...] = final[index * slots : (index + 1) * slots, :]
     part = plan.width // (plan.seq * plan.ch)
     at = lax.axis_index("ch") * part
     span = plan.vector_span
     if span == plan.width:
         at = at + lax.axis_index("seq") * plan.short
-    turned = pltpu.roll(refs[count - 1][...], lax.rem(span - at, span), 1)
-    for index, target in enumerate(refs[2 * count - 1 :]):
-        target[...] = turned[index : index + 1, :part]
+    turned = pltpu.roll(vectors[...], lax.rem(span - at, span), 1)
+    for index, target in enumerate(parts):
+        target[...] = turned[index, :part]
+    for load, store in zip(loads, stores):
+        load.wait()
+        store.start()
+    for store in stores:
+        store.wait()
 
 
 def body(*arguments):
@@ -1214,30 +1284,29 @@
         ),
     )(*operands)
     part = width // (plan.seq * plan.ch)
-    shapes = [outs[name] for name in OUTPUTS[:-1]] + [((1, part), F32)] * len(VECTORS)
+    slots = plan.slots
+    got = dict(zip(OUTPUTS, results))
+    vmem, hbm = pl.BlockSpec(memory_space=pltpu.VMEM), pl.BlockSpec(memory_space=pl.ANY)
+    shapes = [outs[name] for name in LARGE] + [((slots, plan.narrow), F32)] * 2
+    shapes += [((part,), F32)] * len(VECTORS)
     results = pl.pallas_call(
         functools.partial(place_outputs, plan),
         out_shape=[jax.ShapeDtypeStruct(*shape) for shape in shapes],
-        in_specs=[pl.BlockSpec(memory_space=pltpu.VMEM)] * len(OUTPUTS),
-        out_specs=[pl.BlockSpec(memory_space=pltpu.VMEM)] * len(shapes),
-    )(*results)
-    got = dict(zip(OUTPUTS[:-1], results))
-    vectors = results[len(OUTPUTS) - 1 :]
+        in_specs=[hbm] * len(LARGE) + [vmem] * 2,
+        out_specs=[hbm] * len(LARGE) + [vmem] * (2 + len(VECTORS)),
+        scratch_shapes=[pltpu.VMEM(*outs[name]) for name in LARGE]
+        + [pltpu.SemaphoreType.DMA((2, len(LARGE)))],
+        compiler_params=pltpu.CompilerParams(vmem_limit_bytes=60 * 2**20),
+    )(*[got[name] for name in LARGE], got["final"], got["vectors"])
+    mixed_out, grad_tokens, *weights = results[: len(LARGE)]
     shape = values["tokens"].shape
-    slots = plan.slots
     return (
-        got["mixed_out"].reshape(shape),
-        got["grad_tokens"].reshape(shape),
-        got["final"][:slots],
-        got["final"][slots : 2 * slots],
-        got["grad_key"],
-        got["grad_value"],
-        got["grad_recept"],
-        got["grad_output"],
-        got["grad_expand"],
-        got["grad_contract"],
-        got["grad_gate"],
-    ) + tuple(vector.reshape(part) for vector in vectors)
+        mixed_out.reshape(shape),
+        grad_tokens.reshape(shape),
+        *results[len(LARGE) : len(LARGE) + 2],
+        *weights,
+        *results[len(LARGE) + 2 :],
+    )
 
 
 def solution(mesh):

time: 154 us -> 144 us (0.935)
  Pallas kernels: 152 us -> 143 us
    pallas_call x1, Pallas kernels: 148 us -> 139 us  [body(): pl.pallas_call(functools.partial(layer_kernel, plan), out_shape=[jax.Shap...]
where the time goes in v5:
time: 144 us
  Pallas kernels  143 us (99%)
    pallas_call x1, Pallas kernels, body(): pl.pallas_call(functools.partial(layer_kernel, plan), out_shape=[jax.Shap...  139 us
    pallas_call x1, Pallas kernels, body(): pl.pallas_call(functools.partial(place_outputs, plan), out_shape=[jax.Sha...  4.1 us

profile of v5, /device:TPU:0, one launch (start us, length us, event | category | flops | bytes accessed | tf_op | source)
XLA Modules:
  0.0 144.1 jit_solution(703781726261792931)
XLA Ops:
  0.7 139.2 %shard_map.390 = (bf16[256,1024]{1,0:T(8,128)(2,1)}, bf16[256,1024]{1,0:T(8,128)(2,1)}, f32[8,256]{1,0:T(8,128)}, f32[128,256]{1,0:T(8,128)}, f32[128,256]{1,0:T...) custom-call(bf16[256,1024]{1,0:T(8,128)(2,1)} %bitcast.15, ...), custom_call_target="tpu_custom_call" | custom-call | tf_op jit(solution)/shard_map/pallas_call | solution.py:1276
  139.8 4.1 %shard_map.391 = (bf16[256,1024]{1,0:T(8,128)(2,1)}, bf16[256,1024]{1,0:T(8,128)(2,1)}, f32[128,256]{1,0:T(8,128)}, f32[128,256]{1,0:T(8,128)}, f32[128,256]{1,0...) custom-call(bf16[256,1024]{1,0:T(8,128)(2,1)} %get-tuple-element.55., ...), custom_call_target="tpu_custom_call" | custom-call | tf_op jit(solution)/shard_map/pallas_call | solution.py:1292

commit v6 on v5

--- a/solution.py
+++ b/solution.py
@@ -14,47 +14,45 @@
 F32 = jnp.float32
 BF16 = jnp.bfloat16
 TILE = 64
-WIDE = 256
-MATMUL_WIDE = 512
+WIDE = 512
+MATMUL_WIDE = 1024
 SLOTS_OF_WEIGHTS = 3
 
 ORDERS = {
-    "c0": "ylhx",
-    "c1": "lyxh",
+    "c0": "lyhx",
+    "c1": "lxyh",
     "c2": "yxlh",
-    "c3": "xylh",
-    "e0": "lyh",
-    "e1": "lyh",
+    "c3": "ylhx",
+    "e0": "ylh",
+    "e1": "ylh",
     "e2": "ylh",
     "e3": "ylh",
-    "g": "lyxh",
+    "g": "lxyh",
     "o": "xylh",
     "k": "xylh",
     "v": "xylh",
-    "r": "yxlh",
+    "r": "ylhx",
 }
 PUMPS = (
     (),
+    (),
     (
-        "c0", "c1",
+        "c2", "E0",
     ),
     (
-        "c3", "E0", "c2", "g",
+        "c0", "E1",
     ),
     (),
     (
-        "E1", "c1",
+        "c3", "c2",
     ),
     (
-        "c0", "c2", "c3",
+        "e0", "E2",
     ),
     (
-        "e0", "E2", "g", "e1",
-    ),
-    (
-        "E3", "c0", "c2", "r", "c3", "e0", "c2", "o", "c3", "c1", "!", "e2", "e0", "*", "e1", "c1",
-        "e2", "e3", "e1", "k", "e2", "o", "e3", "o", "k", "e3", "v", "o", "g", "c0", "k", "v", "g",
-        "r", "k", "*", "v", "r", "*", "v", "r",
+        "c1", "g", "c0", "E3", "c3", "e1", "c2", "e0", "o", "!", "c0", "*", "r", "c3", "e1", "c2",
+        "e2", "e0", "k", "r", "e3", "e1", "e2", "o", "r", "v", "e3", "e2", "k", "c1", "o", "e3",
+        "v", "k", "g", "c1", "c0", "o", "*", "v", "c3", "g", "r", "*", "k", "c1", "v", "g",
     ),
 )
 

time: 144 us -> 137 us (0.951)
  Pallas kernels: 143 us -> 136 us
    pallas_call x1, Pallas kernels: 139 us -> 132 us  [body(): pl.pallas_call(functools.partial(layer_kernel, plan), out_shape=[jax.Shap...]
where the time goes in v6:
time: 137 us
  Pallas kernels  136 us (99%)
    pallas_call x1, Pallas kernels, body(): pl.pallas_call(functools.partial(layer_kernel, plan), out_shape=[jax.Shap...  132 us
    pallas_call x1, Pallas kernels, body(): pl.pallas_call(functools.partial(place_outputs, plan), out_shape=[jax.Sha...  4.1 us

profile of v6, /device:TPU:0, one launch (start us, length us, event | category | flops | bytes accessed | tf_op | source)
XLA Modules:
  0.0 136.5 jit_solution(8868176514902165519)
XLA Ops:
  0.7 131.6 %shard_map.390 = (bf16[256,1024]{1,0:T(8,128)(2,1)}, bf16[256,1024]{1,0:T(8,128)(2,1)}, f32[8,256]{1,0:T(8,128)}, f32[128,256]{1,0:T(8,128)}, f32[128,256]{1,0:T...) custom-call(bf16[256,1024]{1,0:T(8,128)(2,1)} %bitcast.15, ...), custom_call_target="tpu_custom_call" | custom-call | tf_op jit(solution)/shard_map/pallas_call | solution.py:1274
  132.3 4.1 %shard_map.391 = (bf16[256,1024]{1,0:T(8,128)(2,1)}, bf16[256,1024]{1,0:T(8,128)(2,1)}, f32[128,256]{1,0:T(8,128)}, f32[128,256]{1,0:T(8,128)}, f32[128,256]{1,0...) custom-call(bf16[256,1024]{1,0:T(8,128)(2,1)} %get-tuple-element.55., ...), custom_call_target="tpu_custom_call" | custom-call | tf_op jit(solution)/shard_map/pallas_call | solution.py:1290

commit v7 on v6

--- a/solution.py
+++ b/solution.py
@@ -19,40 +19,38 @@
 SLOTS_OF_WEIGHTS = 3
 
 ORDERS = {
-    "c0": "lyhx",
-    "c1": "lxyh",
-    "c2": "yxlh",
-    "c3": "ylhx",
+    "c0": "yxlh",
+    "c1": "lyhx",
+    "c2": "ylhx",
+    "c3": "lxyh",
     "e0": "ylh",
     "e1": "ylh",
     "e2": "ylh",
     "e3": "ylh",
     "g": "lxyh",
-    "o": "xylh",
+    "o": "ylhx",
     "k": "xylh",
     "v": "xylh",
-    "r": "ylhx",
+    "r": "xylh",
 }
 PUMPS = (
     (),
     (),
     (
-        "c2", "E0",
+        "c0", "c1", "E0",
+    ),
+    (),
+    (),
+    (
+        "E1", "c2", "c0",
     ),
     (
-        "c0", "E1",
-    ),
-    (),
-    (
-        "c3", "c2",
+        "c3", "c1", "E2",
     ),
     (
-        "e0", "E2",
-    ),
-    (
-        "c1", "g", "c0", "E3", "c3", "e1", "c2", "e0", "o", "!", "c0", "*", "r", "c3", "e1", "c2",
-        "e2", "e0", "k", "r", "e3", "e1", "e2", "o", "r", "v", "e3", "e2", "k", "c1", "o", "e3",
-        "v", "k", "g", "c1", "c0", "o", "*", "v", "c3", "g", "r", "*", "k", "c1", "v", "g",
+        "e0", "g", "E3", "c2", "c0", "o", "c1", "r", "!", "e0", "e1", "*", "c2", "c0", "e2", "o",
+        "k", "e0", "e3", "e1", "e2", "r", "o", "v", "e3", "e1", "k", "c3", "e2", "r", "e3", "v",
+        "k", "c3", "g", "c1", "r", "*", "v", "c2", "g", "o", "*", "k", "c3", "v", "g",
     ),
 )
 
@@ -906,9 +904,6 @@
 
     hand_over("contract", grad_contracted)
     hand_over("gate", grad_logit)
-    settle("hidden", "back_contract")
-    start_pieces("c")
-
     for index in range(panel_count):
 
         def store_expanded(columns, product, index=index):
@@ -919,6 +914,9 @@
 
         matmul(grad_contracted, panels.take(), NT, store_expanded)
         panels.release()
+        if index == 0:
+            settle("hidden", "back_contract")
+            start_pieces("c")
     for step, copy in enumerate(across, 1):
         copy.wait()
         exchanges["expand"].append(

time: 137 us -> 137 us (level)
  no operation moved by 1% of the time
where the time goes in v7:
time: 137 us; the launch traced here: 136 us
  Pallas kernels  135 us (99%)
    pallas_call x1, Pallas kernels, body(): pl.pallas_call(functools.partial(layer_kernel, plan), out_shape=[jax.Shap...  131 us
    pallas_call x1, Pallas kernels, body(): pl.pallas_call(functools.partial(place_outputs, plan), out_shape=[jax.Sha...  4.1 us

profile of v7, /device:TPU:0, one launch (start us, length us, event | category | flops | bytes accessed | tf_op | source)
XLA Modules:
  0.0 136.3 jit_solution(6006410424711497610)
XLA Ops:
  0.7 131.3 %shard_map.390 = (bf16[256,1024]{1,0:T(8,128)(2,1)}, bf16[256,1024]{1,0:T(8,128)(2,1)}, f32[8,256]{1,0:T(8,128)}, f32[128,256]{1,0:T(8,128)}, f32[128,256]{1,0:T...) custom-call(bf16[256,1024]{1,0:T(8,128)(2,1)} %bitcast.15, ...), custom_call_target="tpu_custom_call" | custom-call | tf_op jit(solution)/shard_map/pallas_call | solution.py:1272
  132.0 4.1 %shard_map.391 = (bf16[256,1024]{1,0:T(8,128)(2,1)}, bf16[256,1024]{1,0:T(8,128)(2,1)}, f32[128,256]{1,0:T(8,128)}, f32[128,256]{1,0:T(8,128)}, f32[128,256]{1,0...) custom-call(bf16[256,1024]{1,0:T(8,128)(2,1)} %get-tuple-element.55., ...), custom_call_target="tpu_custom_call" | custom-call | tf_op jit(solution)/shard_map/pallas_call | solution.py:1288

commit v8 on v7

--- a/solution.py
+++ b/solution.py
@@ -1214,12 +1214,6 @@
 
     sources, (final, vectors) = take(count), take(2)
     targets, finals, parts = take(count), take(2), take(len(VECTORS))
-    buffers, (sems,) = take(count), take(1)
-    loads, stores = [], []
-    for index in range(count):
-        loads.append(pltpu.make_async_copy(sources[index], buffers[index], sems.at[0, index]))
-        stores.append(pltpu.make_async_copy(buffers[index], targets[index], sems.at[1, index]))
-        loads[-1].start()
     slots = plan.slots
     for index, target in enumerate(finals):
         target[...] = final[index * slots : (index + 1) * slots, :]
@@ -1231,11 +1225,8 @@
     turned = pltpu.roll(vectors[...], lax.rem(span - at, span), 1)
     for index, target in enumerate(parts):
         target[...] = turned[index, :part]
-    for load, store in zip(loads, stores):
-        load.wait()
-        store.start()
-    for store in stores:
-        store.wait()
+    for source, target in zip(sources, targets):
+        target[...] = source[...]
 
 
 def body(*arguments):
@@ -1282,16 +1273,14 @@
     part = width // (plan.seq * plan.ch)
     slots = plan.slots
     got = dict(zip(OUTPUTS, results))
-    vmem, hbm = pl.BlockSpec(memory_space=pltpu.VMEM), pl.BlockSpec(memory_space=pl.ANY)
+    vmem = pl.BlockSpec(memory_space=pltpu.VMEM)
     shapes = [outs[name] for name in LARGE] + [((slots, plan.narrow), F32)] * 2
     shapes += [((part,), F32)] * len(VECTORS)
     results = pl.pallas_call(
         functools.partial(place_outputs, plan),
         out_shape=[jax.ShapeDtypeStruct(*shape) for shape in shapes],
-        in_specs=[hbm] * len(LARGE) + [vmem] * 2,
-        out_specs=[hbm] * len(LARGE) + [vmem] * (2 + len(VECTORS)),
-        scratch_shapes=[pltpu.VMEM(*outs[name]) for name in LARGE]
-        + [pltpu.SemaphoreType.DMA((2, len(LARGE)))],
+        in_specs=[vmem] * (len(LARGE) + 2),
+        out_specs=[vmem] * len(shapes),
         compiler_params=pltpu.CompilerParams(vmem_limit_bytes=60 * 2**20),
     )(*[got[name] for name in LARGE], got["final"], got["vectors"])
     mixed_out, grad_tokens, *weights = results[: len(LARGE)]

time: 137 us -> 136 us (level)
  no operation moved by 1% of the time
where the time goes in v8:
time: 136 us
  Pallas kernels  135 us (99%)
    pallas_call x1, Pallas kernels, body(): pl.pallas_call(functools.partial(layer_kernel, plan), out_shape=[jax.Shap...  131 us
    pallas_call x1, Pallas kernels, body(): pl.pallas_call(functools.partial(place_outputs, plan), out_shape=[jax.Sha...  3.37 us

profile of v8, /device:TPU:0, one launch (start us, length us, event | category | flops | bytes accessed | tf_op | source)
XLA Modules:
  0.0 135.5 jit_solution(12906757828099056554)
XLA Ops:
  0.7 131.3 %shard_map.390 = (bf16[256,1024]{1,0:T(8,128)(2,1)}, bf16[256,1024]{1,0:T(8,128)(2,1)}, f32[8,256]{1,0:T(8,128)}, f32[128,256]{1,0:T(8,128)}, f32[128,256]{1,0:T...) custom-call(bf16[256,1024]{1,0:T(8,128)(2,1)} %bitcast.15, ...), custom_call_target="tpu_custom_call" | custom-call | tf_op jit(solution)/shard_map/pallas_call | solution.py:1263
  132.0 3.4 %shard_map.391 = (bf16[256,1024]{1,0:T(8,128)(2,1)}, bf16[256,1024]{1,0:T(8,128)(2,1)}, f32[128,256]{1,0:T(8,128)}, f32[128,256]{1,0:T(8,128)}, f32[128,256]{1,0...) custom-call(bf16[256,1024]{1,0:T(8,128)(2,1)} %get-tuple-element.55., ...), custom_call_target="tpu_custom_call" | custom-call | tf_op jit(solution)/shard_map/pallas_call | solution.py:1279
